TPU v7x, 32 devices: a whole 2x2x4 slice. The times are simulated.
32 devices in a mesh: groups: 2 (over x), frames: 16 (over z, y, core).
Axes of the slice: x: 2, y: 2, z: 4, core: 2. Of those that a mesh axis runs over, the one named last changes fastest.
Arguments:
- latents: bfloat16 [4, 64, 128, 320], P('groups', 'frames'), parts along dimension 0, may hold values from -6 to 6
- in_weight: bfloat16 [3, 3, 320, 320], replicated, may hold values from -0.109375 to 0.109375
- time_weight: bfloat16 [3, 320, 320], replicated, may hold values from -0.1875 to 0.1875
- mid_weight: bfloat16 [3, 3, 320, 640], replicated, may hold values from -0.109375 to 0.109375
- up_weight: bfloat16 [3, 3, 960, 320], replicated, may hold values from -0.0625 to 0.0625
Outputs:
- mixed: bfloat16 [4, 64, 128, 320], P('groups', 'frames'), parts along dimension 0
There are 2 independent parts, one for each index of `groups`. A program takes and returns all parts, laid end to end along the dimension named above; an argument that names none is the same for every part. Nothing has to cross between parts.
All inputs are finite; a program needn't handle non-finite values.
Results may differ from a plain program's by a relative error of at most 0.0045.
Values may be sent and summed in bfloat16 or wider, within the bound.
No kernel may reach another device: no remote copies, remote signals or barrier semaphores. Data moves between devices by JAX's collectives and lax.ppermute only.
A program may use at most 64 MiB of HBM per device.

v0:
```python
import jax
import jax.numpy as jnp
from jax import lax
from jax.sharding import PartitionSpec as P

FRAMES = 4


def with_halo(block, sides, width):
    for axis, dim in sides:
        count = lax.axis_size(axis)
        forward = [(i, i + 1) for i in range(count - 1)]
        forward.append((count - 1, 0))
        backward = [(target, source) for source, target in forward]
        low = lax.ppermute(
            lax.slice_in_dim(block, block.shape[dim] - width, None, axis=dim), axis, forward
        )
        high = lax.ppermute(lax.slice_in_dim(block, 0, width, axis=dim), axis, backward)
        block = jnp.concatenate([low, block, high], axis=dim)
    return block


def from_behind(value, axis, steps):
    count = lax.axis_size(axis)
    pairs = [(source, (source + steps) % count) for source in range(count)]
    return lax.ppermute(value, axis, pairs)


def spatial(padded, weight):
    return lax.conv_general_dilated(
        padded,
        weight,
        (1, 1),
        ((0, 0), (1, 1)),
        dimension_numbers=("NHWC", "HWIO", "NHWC"),
        preferred_element_type=jnp.float32,
    )


def clip_rims(padded, margin, band_index, band_count):
    length = padded.shape[1]
    row_index = lax.broadcasted_iota(jnp.int32, (1, length, 1, 1), 1)
    upper = jnp.logical_and(row_index < margin, band_index == 0)
    lower = jnp.logical_and(row_index >= length - margin, band_index == band_count - 1)
    keep = jnp.logical_not(jnp.logical_or(upper, lower))
    return jnp.where(keep, padded, jnp.zeros((), padded.dtype))


def time_product(before, centre, after, merged_time):
    stacked = jnp.concatenate([before, centre, after], axis=-1)
    product = jnp.dot(
        stacked.reshape(-1, stacked.shape[-1]), merged_time, preferred_element_type=jnp.float32
    )
    return (centre.astype(jnp.float32) + product.reshape(centre.shape)).astype(jnp.bfloat16)


def body(latents, in_weight, time_weight, mid_weight, up_weight):
    device_count = lax.axis_size("frames")
    band_count = device_count // FRAMES
    half_bands = band_count // 2
    placed = lax.axis_index("frames") + half_bands
    band_index = placed % band_count
    frame_index = placed // band_count % FRAMES
    clip_count, row_count, columns, channels = latents.shape
    merged_time = time_weight.reshape(3 * channels, channels)
    padded = with_halo(latents, (("frames", 1),), 1)
    first = jax.nn.silu(spatial(clip_rims(padded, 1, band_index, band_count), in_weight)).astype(
        jnp.bfloat16
    )
    before = from_behind(first, "frames", band_count)
    after = from_behind(first, "frames", -band_count)
    before = jnp.where(frame_index == 0, jnp.zeros((), before.dtype), before)
    after = jnp.where(frame_index == FRAMES - 1, jnp.zeros((), after.dtype), after)
    skip = time_product(before, first, after, merged_time)
    pooled = (
        skip.astype(jnp.float32)
        .reshape(clip_count, row_count // 2, 2, columns // 2, 2, channels)
        .mean(axis=(2, 4))
        .astype(jnp.bfloat16)
    )
    pooled_pad = with_halo(pooled, (("frames", 1),), 1)
    middle = jax.nn.silu(
        spatial(clip_rims(pooled_pad, 1, band_index, band_count), mid_weight)
    ).astype(jnp.bfloat16)
    upsampled = jnp.repeat(jnp.repeat(middle, 2, axis=1), 2, axis=2)
    joined = jnp.concatenate([skip, upsampled], axis=-1)
    joined_pad = clip_rims(with_halo(joined, (("frames", 1),), 1), 1, band_index, band_count)
    return (latents.astype(jnp.float32) + spatial(joined_pad, up_weight)).astype(jnp.bfloat16)


def solution(mesh):
    in_specs = (P("groups", "frames", None, None), P(), P(), P(), P())
    out_specs = P("groups", "frames", None, None)
    return jax.shard_map(body, mesh=mesh, in_specs=in_specs, out_specs=out_specs, check_vma=False)
```

profile of v0, /device:TPU:1, one launch (start us, length us, event | category | flops | bytes accessed | tf_op | source)
XLA Modules:
  0.0 133.2 jit_solution(16330944914423519638)
XLA Ops:
  0.0 1.2 fusion.30
  1.2 2.7 %collective-permute-start = (bf16[2,1,128,320]{2,3,1,0:T(8,128)(2,1)S(1)}, bf16[2,1,128,320]{2,3,1,0:T(8,128)(2,1)S(1)}, u32[]{:S(2)}, u32[]{:S(2)}) collective-permute-start(bf16[2,1,128,320]{2,3,1,0:T(8,128)(2,1)S(1)} %get-tuple-element.7), channel_id=1, source_target_pairs={{0,1},{1,2},{2,3},{3,4},{4,5},{5,6},{6,7},{7,8},{8,9},{9,10},{10,1... | collective-permute-start | bytes 491528 | tf_op jit(solution)/shard_map/ppermute | solution.py:15
  3.9 0.0 collective-permute-start.1
  3.9 2.3 %collective-permute-done = bf16[2,1,128,320]{2,3,1,0:T(8,128)(2,1)S(1)} collective-permute-done((bf16[2,1,128,320]{2,3,1,0:T(8,128)(2,1)S(1)}, bf16[2,1,128,320]{2,3,1,0:T(8,128)(2,1)S(1)}, u32[]{:S(2)}, u32[]{:S(2)}) %collective-permute-start) | collective-permute-done | bytes 163872 | tf_op jit(solution)/shard_map/ppermute | solution.py:15
  6.1 4.2 %collective-permute-done.1 = bf16[2,1,128,320]{2,3,1,0:T(8,128)(2,1)S(1)} collective-permute-done((bf16[2,1,128,320]{2,3,1,0:T(8,128)(2,1)S(1)}, bf16[2,1,128,320]{2,3,1,0:T(8,128)(2,1)S(1)}, u32[]{:S(2)}, u32[]{:S(2)}) %collective-permute-start.1) | collective-permute-done | bytes 163872 | tf_op jit(solution)/shard_map/ppermute | solution.py:18
  10.4 2.2 %fusion.24 = bf16[6,2,128,320]{2,3,0,1:T(8,128)(2,1)} fusion(bf16[2,1,128,320]{2,3,1,0:T(8,128)(2,1)S(1)} %collective-permute-done.1, bf16[2,4,128,320]{2,3,1,0:T(8,128)(2,1)} %param.5, bf16[2,1,128,320]{2,3,1,0:T(8,128)(2,1)S(1)} %collective-permute-done, pred[6]{0:T(512)(128)(4,1)S(1)} %or_not_fusion.1), kind=kLoop, calls=%fused_computation.26 | loop fusion | flops 1474560 | bytes 1966086 | tf_op jit(solution)/shard_map/jit(_where)/select_n | solution.py:46
  12.6 3.6 %copy.46 = bf16[6,2,128,320]{3,1,2,0:T(2,128)(2,1)S(1)} copy(bf16[6,2,128,320]{2,3,0,1:T(8,128)(2,1)} %fusion.24) | data formatting | bytes 1966080
  16.2 0.0 copy-start.5
  16.2 1.0 pad.clone
  17.2 0.1 slice.31
  17.3 1.4 %fusion.14 = bf16[6,2,8,19,320]{4,1,3,2,0:T(2,128)(2,1)S(1)} fusion(bf16[6,2,7,2,320]{4,1,3,2,0:T(2,128)(2,1)S(1)} %slice.31, bf16[6,2,8,17,320]{4,1,3,2,0:T(2,128)(2,1)S(1)} %bitcast.51), kind=kLoop, calls=%fused_computation.17 | loop fusion | flops 3502080 | bytes 2319360 | tf_op jit(solution)/shard_map/conv_general_dilated | solution.py:30
  18.7 0.0 copy-done
  18.7 0.0 copy-done.5
  18.7 3.7 %multiply_convert_fusion = bf16[4,16,17,320]{3,1,2,0:T(8,128)(2,1)S(1)} fusion(bf16[3,3,320,320]{3,2,1,0:T(8,128)(2,1)S(1)} %copy-done, bf16[6,2,8,19,320]{4,1,3,2,0:T(2,128)(2,1)S(1)} %fusion.14, pred[16,17]{0,1:T(8,128)(4,1)S(1)} %copy-done.5), kind=kOutput, calls=%fused_computation.15 | convolution fusion | flops 2007490560 | bytes 3707152 | tf_op jit(solution)/shard_map/conv_general_dilated | solution.py:30
  22.5 0.3 copy.30
  22.8 1.2 slice.33
  24.0 2.1 %copy.44 = bf16[4,2,128,320]{2,3,0,1:T(8,128)(2,1)} copy(bf16[4,2,128,320]{3,0,2,1:T(4,128)(2,1)} %slice.33) | data formatting | bytes 1310720
  26.1 2.4 %collective-permute-start.3 = (bf16[2,4,128,320]{2,3,1,0:T(8,128)(2,1)}, bf16[2,4,128,320]{2,3,1,0:T(8,128)(2,1)}, u32[]{:S(2)}, u32[]{:S(2)}) collective-permute-start(bf16[2,4,128,320]{2,3,1,0:T(8,128)(2,1)} %bitcast.57), channel_id=1, source_target_pairs={{0,12},{1,13},{2,14},{3,15},{4,0},{5,1},{6,2},{7,3},{8,4},{9,5},{1... | collective-permute-start | bytes 1966088 | tf_op jit(solution)/shard_map/ppermute | solution.py:26
  28.5 0.0 collective-permute-start.2
  28.5 0.3 copy.28
  28.9 1.4 %slice.32 = f32[4,2,128,320]{3,0,2,1:T(4,128)} slice(f32[4,2,136,320]{3,0,2,1:T(4,128)S(1)} %bitcast.47), slice={[0:4], [0:2], [0:128], [0:320]} | slice | bytes 2621440 | tf_op jit(solution)/shard_map/convert_element_type | solution.py:54
  30.3 2.6 %copy.43 = f32[4,2,128,320]{2,3,0,1:T(8,128)} copy(f32[4,2,128,320]{3,0,2,1:T(4,128)} %slice.32) | data formatting | bytes 2621440
  32.9 10.5 %collective-permute-done.3 = bf16[2,4,128,320]{2,3,1,0:T(8,128)(2,1)} collective-permute-done((bf16[2,4,128,320]{2,3,1,0:T(8,128)(2,1)}, bf16[2,4,128,320]{2,3,1,0:T(8,128)(2,1)}, u32[]{:S(2)}, u32[]{:S(2)}) %collective-permute-start.3) | collective-permute-done | bytes 655392 | tf_op jit(solution)/shard_map/ppermute | solution.py:26
  43.4 1.1 broadcast_select_fusion.2
  44.5 13.0 %collective-permute-done.2 = bf16[2,4,128,320]{2,3,1,0:T(8,128)(2,1)} collective-permute-done((bf16[2,4,128,320]{2,3,1,0:T(8,128)(2,1)}, bf16[2,4,128,320]{2,3,1,0:T(8,128)(2,1)}, u32[]{:S(2)}, u32[]{:S(2)}) %collective-permute-start.2) | collective-permute-done | bytes 655392 | tf_op jit(solution)/shard_map/ppermute | solution.py:26
  57.6 0.0 copy-done.3
  57.6 0.0 copy-done.2
  57.6 0.9 fusion.20
  58.5 0.0 copy-start.1
  58.5 2.1 %copy.33 = f32[2,4,128,320]{3,0,2,1:T(2,128)} copy(bf16[2,4,128,320]{2,3,1,0:T(8,128)(2,1)S(1)} %fusion.20) | data formatting | bytes 1966080 | tf_op jit(solution)/shard_map/reshape | solution.py:77
  60.6 3.0 %reduce_sum.9 = f32[2,2,64,320]{3,0,2,1:T(2,128)} reduce(f32[2,2,2,64,2,320]{5,0,4,3,2,1:T(2,128)} %bitcast.49, f32[]{:T(128)} %constant.52.clone.1), dimensions={2,4}, to_apply=%region_0.1 | reduce | flops 245760 | bytes 1638404 | tf_op jit(solution)/shard_map/reduce_sum | solution.py:78
  63.7 1.2 multiply_convert_fusion.2
  64.9 0.1 fusion.31
  65.0 0.0 copy-start.6
  65.0 1.8 %collective-permute-start.4 = (bf16[2,1,64,320]{3,0,2,1:T(2,128)(2,1)S(1)}, bf16[2,1,64,320]{3,0,2,1:T(2,128)(2,1)S(1)}, u32[]{:S(2)}, u32[]{:S(2)}) collective-permute-start(bf16[2,1,64,320]{3,0,2,1:T(2,128)(2,1)S(1)} %get-tuple-element.9), channel_id=1, source_target_pairs={{0,1},{1,2},{2,3},{3,4},{4,5},{5,6},{6,7},{7,8},{8,9},{9,10},{10,1... | collective-permute-start | bytes 245768 | tf_op jit(solution)/shard_map/ppermute | solution.py:15
  66.8 0.0 collective-permute-start.5
  66.8 2.6 %copy.37 = bf16[2,4,128,320]{3,0,2,1:T(2,128)(2,1)S(1)} copy(bf16[2,4,128,320]{2,3,1,0:T(8,128)(2,1)} %copy-done.1) | data formatting | bytes 1310720 | tf_op jit(solution)/shard_map/convert_element_type | solution.py:54
  69.4 0.0 collective-permute-done.4
  69.4 2.6 %collective-permute-done.5 = bf16[2,1,64,320]{3,0,2,1:T(2,128)(2,1)} collective-permute-done((bf16[2,1,64,320]{3,0,2,1:T(2,128)(2,1)S(1)}, bf16[2,1,64,320]{3,0,2,1:T(2,128)(2,1)}, u32[]{:S(2)}, u32[]{:S(2)}) %collective-permute-start.5) | collective-permute-done | bytes 81952 | tf_op jit(solution)/shard_map/ppermute | solution.py:18
  72.0 1.6 %fusion.28 = bf16[4,2,64,320]{3,1,2,0:T(2,128)(2,1)S(1)} fusion(bf16[2,1,64,320]{3,0,2,1:T(2,128)(2,1)} %collective-permute-done.5, bf16[2,2,64,320]{3,0,2,1:T(2,128)(2,1)S(1)} %multiply_convert_fusion.2, bf16[2,1,64,320]{3,0,2,1:T(2,128)(2,1)S(1)} %collective-permute-done.4, pred[4]{0:T(512)(128)(4,1)S(1)} %or_not_fusion), kind=kLoop, calls=%fused_computation.37 | loop fusion | flops 491520 | bytes 655364 | tf_op jit(solution)/shard_map/jit(_where)/select_n | solution.py:46
  73.6 0.4 pad.2
  73.9 0.1 slice.36
  74.0 0.5 fusion.25
  74.5 3.6 %multiply_convert_fusion.1 = bf16[2,16,9,640]{3,1,2,0:T(8,128)(2,1)S(1)} fusion(bf16[3,3,320,640]{3,2,1,0:T(8,128)(2,1)} %param.8, bf16[4,2,8,11,320]{4,1,3,2,0:T(2,128)(2,1)S(1)} %fusion.25, pred[16,9]{0,1:T(8,128)(4,1)S(1)} %copy-done.6), kind=kOutput, calls=%fused_computation.28 | convolution fusion | flops 1062789120 | bytes 4505744 | tf_op jit(solution)/shard_map/conv_general_dilated | solution.py:30
  78.1 0.3 copy.35
  78.4 0.2 slice_bitcast_fusion
  78.7 0.3 copy.36
  79.0 0.3 broadcast_in_dim.53
  79.4 0.7 broadcast_in_dim.54
  80.0 1.6 %pad_maximum_fusion.1 = (bf16[2,1,128,960]{3,0,2,1:T(2,128)(2,1)S(1)}, bf16[2,1,128,960]{3,0,2,1:T(2,128)(2,1)S(1)}) fusion(bf16[2,4,128,640]{3,0,2,1:T(2,128)(2,1)S(1)} %bitcast.45, bf16[2,4,128,320]{3,0,2,1:T(2,128)(2,1)S(1)} %copy.37), kind=kLoop, calls=%fused_computation.35 | loop fusion | flops 1966080 | bytes 2949120 | tf_op jit(solution)/shard_map/slice | solution.py:16
  81.7 0.1 collective-permute-start.6
  81.7 0.5 collective-permute-start.7
  82.2 11.2 %collective-permute-done.6 = bf16[2,1,128,960]{3,0,2,1:T(2,128)(2,1)S(1)} collective-permute-done((bf16[2,1,128,960]{3,0,2,1:T(2,128)(2,1)S(1)}, bf16[2,1,128,960]{3,0,2,1:T(2,128)(2,1)S(1)}, u32[]{:S(2)}, u32[]{:S(2)}) %collective-permute-start.6) | collective-permute-done | bytes 491552 | tf_op jit(solution)/shard_map/ppermute | solution.py:15
  93.5 3.0 %collective-permute-done.7 = bf16[2,1,128,960]{3,0,2,1:T(2,128)(2,1)S(1)} collective-permute-done((bf16[2,1,128,960]{3,0,2,1:T(2,128)(2,1)S(1)}, bf16[2,1,128,960]{3,0,2,1:T(2,128)(2,1)S(1)}, u32[]{:S(2)}, u32[]{:S(2)}) %collective-permute-start.7) | collective-permute-done | bytes 491552 | tf_op jit(solution)/shard_map/ppermute | solution.py:18
  96.5 13.0 %fusion.4 = bf16[6,2,128,960]{3,1,2,0:T(2,128)(2,1)S(1)} fusion(bf16[2,1,128,960]{3,0,2,1:T(2,128)(2,1)S(1)} %collective-permute-done.7, bf16[2,4,128,640]{3,0,2,1:T(2,128)(2,1)S(1)} %bitcast.46, bf16[2,4,128,320]{3,0,2,1:T(2,128)(2,1)S(1)} %copy.37, bf16[2,1,128,960]{3,0,2,1:T(2,128)(2,1)S(1)} %collective-permute-done.6, pred[6]{0:T(512)(128)(4,1)S(1)} %or_not_fusion.1), kind=kLoop, calls=%fused_computation.7 | loop fusion | flops 13271040 | bytes 5898246 | tf_op jit(solution)/shard_map/jit(_where)/select_n | solution.py:46
  109.5 0.0 slice-start.1
  109.5 2.6 %pad.4 = bf16[6,2,136,960]{3,1,2,0:T(2,128)(2,1)S(1)} pad(bf16[6,2,128,960]{3,1,2,0:T(2,128)(2,1)S(1)} %fusion.4, bf16[]{:T(256)} %constant.49.clone.1), padding=0_0x0_0x1_7x0_0 | pad | bytes 6082562 | tf_op jit(solution)/shard_map/jit(_where)/select_n | solution.py:46
  112.1 0.2 slice.38
  112.4 4.3 %fusion = bf16[6,2,8,19,960]{4,1,3,2,0:T(2,128)(2,1)S(1)} fusion(bf16[6,2,7,2,960]{4,1,3,2,0:T(2,128)(2,1)S(1)} %slice.38, bf16[6,2,8,17,960]{4,1,3,2,0:T(2,128)(2,1)S(1)} %bitcast.44), kind=kLoop, calls=%fused_computation.3 | loop fusion | flops 10506240 | bytes 6958080 | tf_op jit(solution)/shard_map/conv_general_dilated | solution.py:30
  116.7 10.7 %fusion.11 = f32[4,16,17,320]{3,1,2,0:T(8,128)S(1)} fusion(bf16[3,3,960,320]{2,3,1,0:T(8,128)(2,1)S(1)} %bitcast.61, bf16[6,2,8,19,960]{4,1,3,2,0:T(2,128)(2,1)S(1)} %fusion, pred[16,17]{0,1:T(8,128)(4,1)S(1)} %copy-done.5), kind=kOutput, calls=%fused_computation.16 | convolution fusion | flops 6016552960 | bytes 10424592 | tf_op jit(solution)/shard_map/conv_general_dilated | solution.py:30
  127.4 0.6 copy.39
  128.0 1.4 %slice.39 = f32[4,2,128,320]{3,0,2,1:T(4,128)} slice(f32[4,2,136,320]{3,0,2,1:T(4,128)S(1)} %bitcast.48), slice={[0:4], [0:2], [0:128], [0:320]} | slice | bytes 2621440 | tf_op jit(solution)/shard_map/conv_general_dilated | solution.py:30
  129.5 1.7 %copy.45 = f32[4,2,128,320]{2,3,0,1:T(8,128)S(1)} copy(f32[4,2,128,320]{3,0,2,1:T(4,128)} %slice.39) | data formatting | bytes 2621440
  131.2 2.1 %fusion.23 = bf16[2,4,128,320]{2,3,1,0:T(8,128)(2,1)} fusion(f32[4,2,128,320]{2,3,0,1:T(8,128)S(1)} %copy.45, bf16[2,4,128,320]{2,3,1,0:T(8,128)(2,1)} %param.5), kind=kLoop, calls=%fused_computation.23 | loop fusion | flops 983040 | bytes 2621440 | tf_op jit(solution)/shard_map/convert_element_type | solution.py:88
  (14 shorter events, 0.1 us)
Async XLA Ops:
  0.0 18.7 %copy-start = (bf16[3,3,320,320]{3,2,1,0:T(8,128)(2,1)S(1)}, bf16[3,3,320,320]{3,2,1,0:T(8,128)(2,1)}, u32[]{:S(2)}) copy-start(bf16[3,3,320,320]{3,2,1,0:T(8,128)(2,1)} %param.6) | copy-start | bytes 5529604
  1.2 4.9 %collective-permute-start = (bf16[2,1,128,320]{2,3,1,0:T(8,128)(2,1)S(1)}, bf16[2,1,128,320]{2,3,1,0:T(8,128)(2,1)S(1)}, u32[]{:S(2)}, u32[]{:S(2)}) collective-permute-start(bf16[2,1,128,320]{2,3,1,0:T(8,128)(2,1)S(1)} %get-tuple-element.7), channel_id=1, source_target_pairs={{0,1},{1,2},{2,3},{3,4},{4,5},{5,6},{6,7},{7,8},{8,9},{9,10},{10,1... | collective-permute-start | bytes 491528 | tf_op jit(solution)/shard_map/ppermute | solution.py:15
  3.9 6.5 %collective-permute-start.1 = (bf16[2,1,128,320]{2,3,1,0:T(8,128)(2,1)S(1)}, bf16[2,1,128,320]{2,3,1,0:T(8,128)(2,1)S(1)}, u32[]{:S(2)}, u32[]{:S(2)}) collective-permute-start(bf16[2,1,128,320]{2,3,1,0:T(8,128)(2,1)S(1)} %get-tuple-element.8), channel_id=1, source_target_pairs={{1,0},{2,1},{3,2},{4,3},{5,4},{6,5},{7,6},{8,7},{9,8},{10,9},{11,1... | collective-permute-start | bytes 491528 | tf_op jit(solution)/shard_map/ppermute | solution.py:18
  16.2 2.6 %copy-start.5 = (pred[16,17]{0,1:T(8,128)(4,1)S(1)}, pred[16,17]{0,1:T(8,128)(4,1)}, u32[]{:S(2)}) copy-start(pred[16,17]{0,1:T(8,128)(4,1)} %constant.67) | copy-start | bytes 820
  26.1 17.2 %collective-permute-start.3 = (bf16[2,4,128,320]{2,3,1,0:T(8,128)(2,1)}, bf16[2,4,128,320]{2,3,1,0:T(8,128)(2,1)}, u32[]{:S(2)}, u32[]{:S(2)}) collective-permute-start(bf16[2,4,128,320]{2,3,1,0:T(8,128)(2,1)} %bitcast.57), channel_id=1, source_target_pairs={{0,12},{1,13},{2,14},{3,15},{4,0},{5,1},{6,2},{7,3},{8,4},{9,5},{1... | collective-permute-start | bytes 1966088 | tf_op jit(solution)/shard_map/ppermute | solution.py:26
  28.5 29.0 %collective-permute-start.2 = (bf16[2,4,128,320]{2,3,1,0:T(8,128)(2,1)}, bf16[2,4,128,320]{2,3,1,0:T(8,128)(2,1)}, u32[]{:S(2)}, u32[]{:S(2)}) collective-permute-start(bf16[2,4,128,320]{2,3,1,0:T(8,128)(2,1)} %bitcast.58), channel_id=1, source_target_pairs={{0,4},{1,5},{2,6},{3,7},{4,8},{5,9},{6,10},{7,11},{8,12},{9,13},{1... | collective-permute-start | bytes 1966088 | tf_op jit(solution)/shard_map/ppermute | solution.py:26
  30.3 27.3 %copy-start.3 = (bf16[4,2,128,320]{2,3,0,1:T(8,128)(2,1)S(1)}, bf16[4,2,128,320]{2,3,0,1:T(8,128)(2,1)}, u32[]{:S(2)}) copy-start(bf16[4,2,128,320]{2,3,0,1:T(8,128)(2,1)} %copy.44) | copy-start | bytes 1966084
  32.9 24.7 %copy-start.2 = (f32[4,2,128,320]{2,3,0,1:T(8,128)S(1)}, f32[4,2,128,320]{2,3,0,1:T(8,128)}, u32[]{:S(2)}) copy-start(f32[4,2,128,320]{2,3,0,1:T(8,128)} %copy.43) | copy-start | bytes 3932164
  32.9 24.7 %copy-start.4 = (bf16[3,320,320]{2,1,0:T(8,128)(2,1)S(1)}, bf16[3,320,320]{2,1,0:T(8,128)(2,1)}, u32[]{:S(2)}) copy-start(bf16[3,320,320]{2,1,0:T(8,128)(2,1)} %param.7) | copy-start | bytes 1843204
  58.5 6.3 %copy-start.1 = (bf16[2,4,128,320]{2,3,1,0:T(8,128)(2,1)}, bf16[2,4,128,320]{2,3,1,0:T(8,128)(2,1)S(1)}, u32[]{:S(2)}) copy-start(bf16[2,4,128,320]{2,3,1,0:T(8,128)(2,1)S(1)} %fusion.20) | copy-start | bytes 1966084
  65.0 9.5 %copy-start.6 = (pred[16,9]{0,1:T(8,128)(4,1)S(1)}, pred[16,9]{0,1:T(8,128)(4,1)}, u32[]{:S(2)}) copy-start(pred[16,9]{0,1:T(8,128)(4,1)} %constant.69) | copy-start | bytes 436
  65.0 4.3 %collective-permute-start.4 = (bf16[2,1,64,320]{3,0,2,1:T(2,128)(2,1)S(1)}, bf16[2,1,64,320]{3,0,2,1:T(2,128)(2,1)S(1)}, u32[]{:S(2)}, u32[]{:S(2)}) collective-permute-start(bf16[2,1,64,320]{3,0,2,1:T(2,128)(2,1)S(1)} %get-tuple-element.9), channel_id=1, source_target_pairs={{0,1},{1,2},{2,3},{3,4},{4,5},{5,6},{6,7},{7,8},{8,9},{9,10},{10,1... | collective-permute-start | bytes 245768 | tf_op jit(solution)/shard_map/ppermute | solution.py:15
  66.8 5.2 %collective-permute-start.5 = (bf16[2,1,64,320]{3,0,2,1:T(2,128)(2,1)S(1)}, bf16[2,1,64,320]{3,0,2,1:T(2,128)(2,1)}, u32[]{:S(2)}, u32[]{:S(2)}) collective-permute-start(bf16[2,1,64,320]{3,0,2,1:T(2,128)(2,1)S(1)} %get-tuple-element.10), channel_id=1, source_target_pairs={{1,0},{2,1},{3,2},{4,3},{5,4},{6,5},{7,6},{8,7},{9,8},{10,9},{11,1... | collective-permute-start | bytes 245768 | tf_op jit(solution)/shard_map/ppermute | solution.py:18
  81.7 11.8 %collective-permute-start.6 = (bf16[2,1,128,960]{3,0,2,1:T(2,128)(2,1)S(1)}, bf16[2,1,128,960]{3,0,2,1:T(2,128)(2,1)S(1)}, u32[]{:S(2)}, u32[]{:S(2)}) collective-permute-start(bf16[2,1,128,960]{3,0,2,1:T(2,128)(2,1)S(1)} %get-tuple-element.5), channel_id=1, source_target_pairs={{0,1},{1,2},{2,3},{3,4},{4,5},{5,6},{6,7},{7,8},{8,9},{9,10},{10,1... | collective-permute-start | bytes 1474568 | tf_op jit(solution)/shard_map/ppermute | solution.py:15
  81.7 14.7 %collective-permute-start.7 = (bf16[2,1,128,960]{3,0,2,1:T(2,128)(2,1)S(1)}, bf16[2,1,128,960]{3,0,2,1:T(2,128)(2,1)S(1)}, u32[]{:S(2)}, u32[]{:S(2)}) collective-permute-start(bf16[2,1,128,960]{3,0,2,1:T(2,128)(2,1)S(1)} %get-tuple-element.6), channel_id=1, source_target_pairs={{1,0},{2,1},{3,2},{4,3},{5,4},{6,5},{7,6},{8,7},{9,8},{10,9},{11,1... | collective-permute-start | bytes 1474568 | tf_op jit(solution)/shard_map/ppermute | solution.py:18
  96.5 20.2 %slice-start = ((s8[5898240]{0:T(1024)(128)(4,1)}), s8[1703936]{0:T(1024)(128)(4,1)S(1)}, s32[]{:S(2)}) async-start(s8[5898240]{0:T(1024)(128)(4,1)} %bitcast.60), calls=%async_computation | async-start | bytes 3407872
  109.5 7.2 %slice-start.1 = ((s8[5898240]{0:T(1024)(128)(4,1)}), s8[4194304]{0:T(1024)(128)(4,1)S(1)}, s32[]{:S(2)}) async-start(s8[5898240]{0:T(1024)(128)(4,1)} %bitcast.60), calls=%async_computation.1 | async-start | bytes 8388608
where the time goes:
time: 134 us; the launch traced here: 133 us
  waiting for transfers between devices  46.8 us (35%)
  other arithmetic  32 us (24%)
  local copies, waits for them, and re-layouts  27.7 us (21%)
  matrix products  18.9 us (14%)
  starting transfers between devices  7.41 us (6%)
    ppermute x2, waiting for transfers between devices, from_behind(): return lax.ppermute(value, axis, pairs)  23.5 us
    conv_general_dilated x3, matrix products, spatial(): lax.conv_general_dilated(padded, weight, (1, 1), ((0, 0), (1, 1)), dimens...  18 us
    select_n x3, other arithmetic, clip_rims(): return jnp.where(keep, padded, jnp.zeros((), padded.dtype))  16.8 us
    ppermute x3, waiting for transfers between devices, with_halo(): lax.ppermute(lax.slice_in_dim(block, block.shape[dim] - width, None, axis...  13.5 us
    unnamed x22, local copies, waits for them, and re-layouts  10.1 us
    ppermute x3, waiting for transfers between devices, with_halo(): lax.ppermute(lax.slice_in_dim(block, 0, width, axis=dim), axis, backward)  9.84 us
    conv_general_dilated x3, other arithmetic, spatial(): lax.conv_general_dilated(padded, weight, (1, 1), ((0, 0), (1, 1)), dimens...  6.14 us
    ppermute x3, starting transfers between devices, with_halo(): lax.ppermute(lax.slice_in_dim(block, block.shape[dim] - width, None, axis...  4.5 us
  transfers between devices with their start and end apart: 8, of which 7 were waited for; matrix products, arithmetic and copies ran while one was open for 6% of the time, Pallas kernels for 0%

commit v1 on v0

v1 whole, which is shorter than its diff:
```python
import jax
import jax.numpy as jnp
from jax import lax
from jax.experimental import pallas as pl
from jax.experimental.pallas import tpu as pltpu
from jax.sharding import PartitionSpec as P


FRAMES = 4
BF16 = jnp.bfloat16
F32 = jnp.float32
LIMIT = 32 * 1024 * 1024


def one_hot(source):
    width = source.shape[1]
    rows = lax.broadcasted_iota(jnp.int32, (source_rows(source), width), 0)
    return (rows == source).astype(BF16)


def source_rows(source):
    return source.shape[1] if source.shape[0] == 1 else source.shape[0]


def lanes(width):
    return lax.broadcasted_iota(jnp.int32, (1, width), 1)


def picks(sources):
    return jnp.concatenate([one_hot(source) for source in sources], axis=1)


def sort_picks(width):
    lane = lanes(width)
    column = jnp.where(lane < width // 2, 2 * lane, 2 * lane - width + 1)
    return picks([column - 1, column, column + 1])


def sorted_shift_picks(width):
    half = width // 2
    lane = lanes(width)
    left = jnp.where(lane < half, jnp.where(lane == 0, -1, lane + half - 1), lane - half)
    right = jnp.where(lane < half, lane + half, jnp.where(lane == width - 1, -1, lane - half + 1))
    return picks([left, right])


def pair_shift_picks(width):
    half = width // 2
    lane = lanes(width)
    left = jnp.where(lane % half == 0, -1, lane - 1)
    right = jnp.where(lane % half == half - 1, -1, lane + 1)
    return picks([left, right])


def unsort_pick(width):
    lane = lanes(width)
    return one_hot(jnp.where(lane % 2 == 0, lane // 2, width // 2 + lane // 2))


def dot(left, right):
    return jnp.dot(left, right, preferred_element_type=F32)


def silu(value):
    return value / (1.0 + jnp.exp(-value))


def fill_sorted(field, place, latent, row, pick, clips):
    channels, width = latent(0).shape
    for clip in range(clips):
        moved = dot(latent(clip), pick).astype(BF16)
        for tap in range(3):
            start = (row * 3 + tap) * channels
            field[start : start + channels, clip * width : (clip + 1) * width] = moved[
                :, tap * width : (tap + 1) * width
            ]


def inner_kernel(latent_ref, weight_ref, first_ref, turned_ref, field_ref):
    clips, rows, channels, width = latent_ref.shape
    pick = sort_picks(width)
    for row in range(rows):
        fill_sorted(field_ref, None, lambda clip: latent_ref[clip, row], row, pick, clips)
    turned_ref[...] = weight_ref[...].T
    depth = 3 * channels
    for row in range(rows - 2):
        total = dot(turned_ref[...], field_ref[row * depth : (row + 3) * depth, :])
        first_ref[row] = silu(total).astype(BF16)


def outer_kernel(low_ref, high_ref, turned_ref, field_ref, first_ref, rim_ref):
    clips, _, channels, width = low_ref.shape
    rows = field_ref.shape[0] // (3 * channels)
    depth = 3 * channels
    pick = sort_picks(width)
    fill_sorted(rim_ref, None, lambda clip: low_ref[clip, 0], 0, pick, clips)
    fill_sorted(rim_ref, None, lambda clip: high_ref[clip, 0], 1, pick, clips)
    top = dot(turned_ref[:, :depth], rim_ref[:depth, :])
    top += dot(turned_ref[:, depth:], field_ref[: 2 * depth, :])
    first_ref[0] = silu(top).astype(BF16)
    bottom = dot(turned_ref[:, : 2 * depth], field_ref[(rows - 2) * depth :, :])
    bottom += dot(turned_ref[:, 2 * depth :], rim_ref[depth:, :])
    first_ref[1] = silu(bottom).astype(BF16)


def weights_kernel(time_ref, mid_ref, up_ref, time_out, mid_out, skip_out, phase_out):
    channels = up_ref.shape[2]
    time_out[...] = time_ref[...].T
    mid_out[...] = mid_ref[...].T
    skip_out[...] = jnp.concatenate(
        [up_ref[dr, dc, :, :channels] for dr in range(3) for dc in range(3)], axis=1
    )
    inner = up_ref.shape[3] - channels
    taps = [[up_ref[dr, dc, :, channels:].astype(F32) for dc in range(3)] for dr in range(3)]
    groups = ((lambda t: t[0], lambda t: t[1] + t[2]), (lambda t: t[0] + t[1], lambda t: t[2]))
    for row_phase in range(2):
        for row_tap in range(2):
            merged = [groups[row_phase][row_tap]([taps[dr][dc] for dr in range(3)]) for dc in range(3)]
            for column_phase in range(2):
                for column_tap in range(2):
                    value = groups[column_phase][column_tap](merged)
                    start = (2 * row_tap + column_tap) * inner
                    phase_out[2 * row_phase + column_phase, :, start : start + inner] = value.astype(
                        BF16
                    )


def skip_kernel(
    inner_ref, outer_ref, inner_before, outer_before, inner_after, outer_after, weight_ref,
    skip_ref, previous_ref, next_ref,
):
    rows = skip_ref.shape[0]
    wide = skip_ref.shape[2]
    half = wide // 4
    lane = lax.broadcasted_iota(jnp.int32, (1, wide), 1)
    lower = (lane // half) % 2 == 0
    sums = []
    for row in range(rows):
        edge = row in (0, rows - 1)
        at = (0 if row == 0 else 1) if edge else row - 1
        before, own, after = (
            (outer_before, outer_ref, outer_after) if edge else (inner_before, inner_ref, inner_after)
        )
        centre = own[at]
        stacked = jnp.concatenate([before[at], centre, after[at]], axis=0)
        skip = (centre.astype(F32) + dot(weight_ref[...], stacked)).astype(BF16)
        skip_ref[row] = skip
        sums.append(skip.astype(F32))
        if row == 0:
            previous_ref[0] = skip
        if row == rows - 1:
            next_ref[0] = skip
    parts = []
    for pooled_row in range(rows // 2):
        both = sums[2 * pooled_row] + sums[2 * pooled_row + 1]
        swapped = jnp.where(
            lower, jnp.roll(both, -half, axis=1), jnp.roll(both, half, axis=1)
        )
        parts.append((both + swapped) * 0.25)
    pooled = jnp.where(lower, parts[0], parts[1]).astype(BF16)
    previous_ref[1] = pooled
    next_ref[1] = pooled


def half_swap(value, lower, half):
    return jnp.where(lower, jnp.roll(value, -half, axis=1), jnp.roll(value, half, axis=1))


def joined_pair(left, right, lower, half):
    mixed = jnp.where(lower, right.astype(F32), left.astype(F32))
    return half_swap(mixed, lower, half).astype(BF16)


def last_kernel(
    flag_ref, skip_ref, own_ref, low_ref, high_ref, mid_ref, skip_weight, phase_weight, latent_ref,
    out_ref, field, pooled_field, middle_field,
):
    rows, channels, wide = skip_ref.shape
    clips = latent_ref.shape[0]
    width = wide // clips
    half = width // 2
    inner = mid_ref.shape[0]
    depth = 3 * channels
    lane = lax.broadcasted_iota(jnp.int32, (1, wide), 1)
    lower = (lane // half) % 2 == 0

    pair_pick = pair_shift_picks(width)
    low_pair, own_pair, high_pair = low_ref[1], own_ref[1], high_ref[1]
    pairs = [
        low_pair,
        joined_pair(low_pair, own_pair, lower, half),
        own_pair,
        joined_pair(own_pair, high_pair, lower, half),
        high_pair,
    ]

    def store_shifted(target, base, value, size, pick):
        target[base + size : base + 2 * size, :] = value
        for clip in range(clips):
            span = slice(clip * width, (clip + 1) * width)
            moved = dot(value[:, span], pick).astype(BF16)
            target[base : base + size, span] = moved[:, :width]
            target[base + 2 * size : base + 3 * size, span] = moved[:, width:]

    for at, pair in enumerate(pairs):
        store_shifted(pooled_field, at * depth, pair, channels, pair_pick)
    keep_low = jnp.logical_or(flag_ref[0] == 0, jnp.logical_not(lower))
    keep_high = jnp.logical_or(flag_ref[1] == 0, lower)
    above = silu(dot(mid_ref[...], pooled_field[: 3 * depth, :]))
    above = jnp.where(keep_low, above, 0.0)
    below = silu(dot(mid_ref[...], pooled_field[2 * depth :, :]))
    below = jnp.where(keep_high, below, 0.0)
    centre = half_swap(jnp.where(lower, below, above), lower, half)
    for at, value in enumerate((above, centre, below)):
        store_shifted(middle_field, at * 3 * inner, value.astype(BF16), inner, pair_pick)

    shift_pick = sorted_shift_picks(width)
    for row in range(rows + 2):
        value = low_ref[0] if row == 0 else high_ref[0] if row == rows + 1 else skip_ref[row - 1]
        store_shifted(field, row * depth, value, channels, shift_pick)

    sort_pick = sort_picks(width)[:, width : 2 * width]
    unsort = unsort_pick(width)
    for row_phase in range(2):
        phases = []
        for column_phase in range(2):
            weight = phase_weight[2 * row_phase + column_phase]
            total = None
            for tap in range(2):
                start = (row_phase + tap) * 3 * inner + column_phase * inner
                part = dot(
                    weight[:, tap * 2 * inner : (tap + 1) * 2 * inner],
                    middle_field[start : start + 2 * inner, :],
                )
                total = part if total is None else total + part
            phases.append(total)
        uppers = (
            jnp.where(lower, phases[0], jnp.roll(phases[1], half, axis=1)),
            jnp.where(lower, jnp.roll(phases[0], -half, axis=1), phases[1]),
        )
        for at in range(rows // 2):
            row = 2 * at + row_phase
            total = uppers[at] + dot(skip_weight[...], field[row * depth : (row + 3) * depth, :])
            for clip in range(clips):
                span = slice(clip * width, (clip + 1) * width)
                latent = dot(latent_ref[clip, row], sort_pick)
                mixed = (latent + total[:, span]).astype(BF16)
                out_ref[clip, row] = dot(mixed, unsort).astype(BF16)


def call(kernel, name, outputs, scratch=(), flops=0, kept=True, inputs=None):
    shapes = [
        pltpu.VMEM(shape, dtype) if kept else jax.ShapeDtypeStruct(shape, dtype)
        for shape, dtype in outputs
    ]
    specs = {} if inputs is None else {"in_specs": inputs}
    return pl.pallas_call(
        kernel,
        out_shape=shapes,
        scratch_shapes=list(scratch),
        compiler_params=pltpu.CompilerParams(vmem_limit_bytes=LIMIT),
        cost_estimate=pl.CostEstimate(flops=flops, bytes_accessed=1 << 20, transcendentals=0),
        name=name,
        **specs,
    )


def chain(axis, step, keep):
    count = lax.axis_size(axis)
    return [
        (source, (source + step) % count) for source in range(count) if keep(source)
    ]


def body(latents, in_weight, time_weight, mid_weight, up_weight):
    device_count = lax.axis_size("frames")
    bands = device_count // FRAMES
    offset = bands // 2
    band_of = lambda index: (index + offset) % bands
    frame_of = lambda index: (index + offset) // bands % FRAMES
    band = band_of(lax.axis_index("frames"))
    down = chain("frames", 1, lambda i: band_of(i) != bands - 1)
    up = chain("frames", -1, lambda i: band_of(i) != 0)
    later = chain("frames", bands, lambda i: frame_of(i) != FRAMES - 1)
    earlier = chain("frames", -bands, lambda i: frame_of(i) != 0)

    clips, rows, width, channels = latents.shape
    inner = mid_weight.shape[3]
    wide = clips * width
    depth = 3 * channels
    turned = jnp.swapaxes(latents, 2, 3)
    low = lax.ppermute(turned[:, rows - 1 :], "frames", down)
    high = lax.ppermute(turned[:, :1], "frames", up)

    first_inner, in_turned, field = call(
        inner_kernel,
        "first_inner",
        [
            ((rows - 2, channels, wide), BF16),
            ((channels, 3 * depth), BF16),
            ((rows * depth, wide), BF16),
        ],
        flops=2 * (rows - 2) * wide * channels * 3 * depth,
    )(turned, in_weight.reshape(3 * depth, channels))
    inner_before = lax.ppermute(first_inner, "frames", later)
    inner_after = lax.ppermute(first_inner, "frames", earlier)

    (first_outer,) = call(
        outer_kernel,
        "first_outer",
        [((2, channels, wide), BF16)],
        [pltpu.VMEM((2 * depth, wide), BF16)],
        flops=2 * 2 * wide * channels * 3 * depth,
    )(low, high, in_turned, field)
    outer_before = lax.ppermute(first_outer, "frames", later)
    outer_after = lax.ppermute(first_outer, "frames", earlier)

    time_rows, mid_rows, up_rows, first_outer = lax.optimization_barrier(
        (
            time_weight.reshape(depth, channels),
            mid_weight.reshape(3 * depth, inner),
            jnp.swapaxes(up_weight, 2, 3),
            first_outer,
        )
    )
    time_turned, mid_turned, skip_weight, phase_weight = call(
        weights_kernel,
        "weights",
        [
            ((channels, depth), BF16),
            ((inner, 3 * depth), BF16),
            ((channels, 3 * depth), BF16),
            ((4, channels, 4 * inner), BF16),
        ],
        flops=10**10,
    )(time_rows, mid_rows, up_rows)

    skip, to_previous, to_next = call(
        skip_kernel,
        "skip",
        [
            ((rows, channels, wide), BF16),
            ((2, channels, wide), BF16),
            ((2, channels, wide), BF16),
        ],
        flops=2 * rows * wide * depth * channels,
    )(first_inner, first_outer, inner_before, outer_before, inner_after, outer_after, time_turned)
    from_previous = lax.ppermute(to_next, "frames", down)
    from_next = lax.ppermute(to_previous, "frames", up)

    flags = jnp.stack([band == 0, band == bands - 1]).astype(jnp.int32)
    whole = pl.BlockSpec(memory_space=pltpu.VMEM)
    (mixed,) = call(
        last_kernel,
        "last",
        [(turned.shape, BF16)],
        [
            pltpu.VMEM(((rows + 2) * depth, wide), BF16),
            pltpu.VMEM((5 * depth, wide), BF16),
            pltpu.VMEM((9 * inner, wide), BF16),
        ],
        flops=2 * rows * wide * channels * (3 * depth + 4 * inner),
        kept=False,
        inputs=[pl.BlockSpec(memory_space=pltpu.SMEM)] + [whole] * 8,
    )(
        flags, skip, to_previous, from_previous, from_next, mid_turned, skip_weight, phase_weight,
        turned,
    )
    return jnp.swapaxes(mixed, 2, 3)


def solution(mesh):
    in_specs = (P("groups", "frames", None, None), P(), P(), P(), P())
    out_specs = P("groups", "frames", None, None)
    return jax.shard_map(body, mesh=mesh, in_specs=in_specs, out_specs=out_specs, check_vma=False)
```

time: 134 us -> 75.7 us (0.56)
  the two profiles are of different devices: /device:TPU:1 before, /device:TPU:0 now
where the time goes in v1:
time: 75.7 us; the launch traced here: 75.2 us
  starting transfers between devices  32.8 us (43%)
  Pallas kernels  24.6 us (32%)
  local copies, waits for them, and re-layouts  13.3 us (18%)
  waiting for transfers between devices  4.31 us (6%)
    pallas_call x1, Pallas kernels, body(): call(last_kernel, 'last', [(turned.shape, BF16)], [pltpu.VMEM(((rows + 2)...  12.7 us
    ppermute x1, starting transfers between devices, body(): from_next = lax.ppermute(to_previous, 'frames', up)  12.4 us
    unnamed x18, local copies, waits for them, and re-layouts  12.2 us
    ppermute x1, starting transfers between devices, body(): high = lax.ppermute(turned[:, :1], 'frames', up)  6.91 us
    pallas_call x1, Pallas kernels, body(): call(weights_kernel, 'weights', [((channels, depth), BF16), ((inner, 3 *...  6.76 us
    ppermute x1, starting transfers between devices, body(): outer_before = lax.ppermute(first_outer, 'frames', later)  4.57 us
    ppermute x1, waiting for transfers between devices, body(): from_previous = lax.ppermute(to_next, 'frames', down)  2.86 us
    ppermute x1, starting transfers between devices, body(): low = lax.ppermute(turned[:, rows - 1:], 'frames', down)  2.36 us
  transfers between devices with their start and end apart: 8, of which 2 were waited for; matrix products, arithmetic and copies ran while one was open for 0% of the time, Pallas kernels for 13%

profile of v1, /device:TPU:0, one launch (start us, length us, event | category | flops | bytes accessed | tf_op | source)
XLA Modules:
  0.0 75.2 jit_solution(14359626236249576787)
XLA Ops:
  0.0 1.0 %fusion = (bf16[2,1,320,128]{3,2,1,0:T(8,128)(2,1)S(1)}, bf16[2,1,320,128]{3,2,1,0:T(8,128)(2,1)S(1)}) fusion(bf16[2,4,320,128]{3,2,1,0:T(8,128)(2,1)} %bitcast.8), kind=kLoop, calls=%fused_computation.1 | loop fusion | bytes 655360 | tf_op jit(solution)/shard_map/slice | solution.py:293
  1.0 2.4 %collective-permute-start = (bf16[2,1,320,128]{3,2,1,0:T(8,128)(2,1)S(1)}, bf16[2,1,320,128]{3,2,1,0:T(8,128)(2,1)S(1)}, u32[]{:S(2)}, u32[]{:S(2)}) collective-permute-start(bf16[2,1,320,128]{3,2,1,0:T(8,128)(2,1)S(1)} %get-tuple-element.34), channel_id=1, source_target_pairs={{0,1},{2,3},{3,4},{4,5},{6,7},{7,8},{8,9},{10,11},{11,12},{12,13},... | collective-permute-start | bytes 491528 | tf_op jit(solution)/shard_map/ppermute | solution.py:292
  3.4 6.9 %collective-permute-start.1 = (bf16[2,1,320,128]{3,2,1,0:T(8,128)(2,1)S(1)}, bf16[2,1,320,128]{3,2,1,0:T(8,128)(2,1)S(1)}, u32[]{:S(2)}, u32[]{:S(2)}) collective-permute-start(bf16[2,1,320,128]{3,2,1,0:T(8,128)(2,1)S(1)} %get-tuple-element.33), channel_id=1, source_target_pairs={{0,15},{1,0},{3,2},{4,3},{5,4},{7,6},{8,7},{9,8},{11,10},{12,11},{... | collective-permute-start | bytes 491528 | tf_op jit(solution)/shard_map/ppermute | solution.py:293
  10.3 0.0 copy-start.4
  10.3 1.1 %copy-done.4 = bf16[2,4,128,320]{2,3,1,0:T(8,128)(2,1)S(1)} copy-done((bf16[2,4,128,320]{2,3,1,0:T(8,128)(2,1)S(1)}, bf16[2,4,128,320]{2,3,1,0:T(8,128)(2,1)}, u32[]{:S(2)}) %copy-start.4) | copy-done | bytes 655384
  11.4 0.0 copy-start.7
  11.4 1.6 %copy-done.7 = bf16[3,3,320,320]{3,2,1,0:T(8,128)(2,1)S(1)} copy-done((bf16[3,3,320,320]{3,2,1,0:T(8,128)(2,1)S(1)}, bf16[3,3,320,320]{3,2,1,0:T(8,128)(2,1)}, u32[]{:S(2)}) %copy-start.7) | copy-done | bytes 1843224
  13.0 0.0 copy-start.6
  13.0 0.0 copy-start.8
  13.0 1.8 %first_inner.1 = (bf16[2,320,256]{2,1,0:T(8,128)(2,1)S(1)}, bf16[320,2880]{1,0:T(8,128)(2,1)S(1)}, bf16[3840,256]{1,0:T(8,128)(2,1)S(1)}) custom-call(bf16[2,4,320,128]{3,2,1,0:T(8,128)(2,1)S(1)} %bitcast.9, bf16[2880,320]{1,0:T(8,128)(2,1)S(1)} %bitcast.12), custom_call_target="tpu_custom_call" | custom-call | flops 943718400 | bytes 1048576 | tf_op jit(solution)/shard_map/first_inner/pallas_call | solution.py:295
  14.8 2.1 %collective-permute-start.2 = (bf16[2,320,256]{2,1,0:T(8,128)(2,1)S(1)}, bf16[2,320,256]{2,1,0:T(8,128)(2,1)S(1)}, u32[]{:S(2)}, u32[]{:S(2)}) collective-permute-start(bf16[2,320,256]{2,1,0:T(8,128)(2,1)S(1)} %get-tuple-element.19.inner_ref), channel_id=1, source_target_pairs={{0,4},{1,5},{2,6},{3,7},{4,8},{5,9},{6,10},{7,11},{8,12},{9,13},{1... | collective-permute-start | bytes 983048 | tf_op jit(solution)/shard_map/ppermute | solution.py:305
  17.0 1.3 %collective-permute-start.4 = (bf16[2,320,256]{2,1,0:T(8,128)(2,1)S(1)}, bf16[2,320,256]{2,1,0:T(8,128)(2,1)S(1)}, u32[]{:S(2)}, u32[]{:S(2)}) collective-permute-start(bf16[2,320,256]{2,1,0:T(8,128)(2,1)S(1)} %get-tuple-element.19.inner_ref), channel_id=1, source_target_pairs={{2,14},{3,15},{4,0},{5,1},{6,2},{7,3},{8,4},{9,5},{10,6},{11,7},{1... | collective-permute-start | bytes 983048 | tf_op jit(solution)/shard_map/ppermute | solution.py:306
  18.3 0.0 collective-permute-done.low_ref
  18.3 0.0 collective-permute-done.1.high_ref
  18.3 1.6 %first_outer.1.outer_ref = bf16[2,320,256]{2,1,0:T(8,128)(2,1)S(1)} custom-call(bf16[2,1,320,128]{3,2,1,0:T(8,128)(2,1)S(1)} %collective-permute-done.low_ref, bf16[2,1,320,128]{3,2,1,0:T(8,128)(2,1)S(1)} %collective-permute-done.1.high_ref, bf16[320,2880]{1,0:T(8,128)(2,1)S(1)} %get-tuple-element.20.turned_ref, ...), custom_call_target="tpu_custom_call" | custom-call | flops 943718400 | bytes 1048576 | tf_op jit(solution)/shard_map/first_outer/pallas_call | solution.py:308
  19.9 4.6 %collective-permute-start.3 = (bf16[2,320,256]{2,1,0:T(8,128)(2,1)S(1)}, bf16[2,320,256]{2,1,0:T(8,128)(2,1)S(1)}, u32[]{:S(2)}, u32[]{:S(2)}) collective-permute-start(bf16[2,320,256]{2,1,0:T(8,128)(2,1)S(1)} %first_outer.1.outer_ref), channel_id=1, source_target_pairs={{0,4},{1,5},{2,6},{3,7},{4,8},{5,9},{6,10},{7,11},{8,12},{9,13},{1... | collective-permute-start | bytes 983048 | tf_op jit(solution)/shard_map/ppermute | solution.py:315
  24.4 1.3 %collective-permute-start.5 = (bf16[2,320,256]{2,1,0:T(8,128)(2,1)S(1)}, bf16[2,320,256]{2,1,0:T(8,128)(2,1)S(1)}, u32[]{:S(2)}, u32[]{:S(2)}) collective-permute-start(bf16[2,320,256]{2,1,0:T(8,128)(2,1)S(1)} %first_outer.1.outer_ref), channel_id=1, source_target_pairs={{2,14},{3,15},{4,0},{5,1},{6,2},{7,3},{8,4},{9,5},{10,6},{11,7},{1... | collective-permute-start | bytes 983048 | tf_op jit(solution)/shard_map/ppermute | solution.py:316
  25.7 0.0 copy-done.6
  25.7 0.0 copy-done.8
  25.8 0.0 copy-start.5
  25.8 6.8 %weights.1 = (bf16[320,960]{1,0:T(8,128)(2,1)S(1)}, bf16[640,2880]{1,0:T(8,128)(2,1)S(1)}, bf16[320,2880]{1,0:T(8,128)(2,1)S(1)}, bf16[4,320,2560]{2,1,0:T(8,128)(2,1)S(1)}) custom-call(bf16[960,320]{1,0:T(8,128)(2,1)S(1)} %bitcast.13, bf16[2880,640]{1,0:T(8,128)(2,1)S(1)} %bitcast.11, bf16[3,3,320,960]{3,2,1,0:T(8,128)(2,1)} %bitcast.14), custom_call_target="tpu_custom_call" | custom-call | flops 10000000000 | bytes 1048576 | tf_op jit(solution)/shard_map/weights/pallas_call | solution.py:326
  32.5 0.0 copy-start
  32.6 2.7 %copy-done = bf16[4,320,2560]{2,1,0:T(8,128)(2,1)} copy-done((bf16[4,320,2560]{2,1,0:T(8,128)(2,1)}, bf16[4,320,2560]{2,1,0:T(8,128)(2,1)S(1)}, u32[]{:S(2)}) %copy-start) | copy-done | bytes 6553624
  35.3 0.0 copy-start.2
  35.3 1.9 %copy-done.2 = bf16[640,2880]{1,0:T(8,128)(2,1)} copy-done((bf16[640,2880]{1,0:T(8,128)(2,1)}, bf16[640,2880]{1,0:T(8,128)(2,1)S(1)}, u32[]{:S(2)}) %copy-start.2) | copy-done | bytes 3686424
  37.1 0.0 collective-permute-done.2.inner_before
  37.2 0.0 collective-permute-done.4.inner_after
  37.2 0.0 collective-permute-done.3.outer_before
  37.2 0.0 collective-permute-done.5.outer_after
  37.2 1.7 %skip.1 = (bf16[4,320,256]{2,1,0:T(8,128)(2,1)S(1)}, bf16[2,320,256]{2,1,0:T(8,128)(2,1)S(1)}, bf16[2,320,256]{2,1,0:T(8,128)(2,1)}) custom-call(bf16[2,320,256]{2,1,0:T(8,128)(2,1)S(1)} %get-tuple-element.19.inner_ref, bf16[2,320,256]{2,1,0:T(8,128)(2,1)S(1)} %first_outer.1.outer_ref, bf16[2,320,256]{2,1,0:T(8,128)(2,1)S(1)} %collective-permute-done.2.inner_before, ...), custom_call_target="tpu_custom_call" | custom-call | flops 629145600 | bytes 1048576 | tf_op jit(solution)/shard_map/skip/pallas_call | solution.py:338
  38.9 1.9 %collective-permute-start.6 = (bf16[2,320,256]{2,1,0:T(8,128)(2,1)}, bf16[2,320,256]{2,1,0:T(8,128)(2,1)}, u32[]{:S(2)}, u32[]{:S(2)}) collective-permute-start(bf16[2,320,256]{2,1,0:T(8,128)(2,1)} %get-tuple-element.29), channel_id=1, source_target_pairs={{0,1},{2,3},{3,4},{4,5},{6,7},{7,8},{8,9},{10,11},{11,12},{12,13},... | collective-permute-start | bytes 983048 | tf_op jit(solution)/shard_map/ppermute | solution.py:348
  40.8 12.4 %collective-permute-start.7 = (bf16[2,320,256]{2,1,0:T(8,128)(2,1)S(1)}, bf16[2,320,256]{2,1,0:T(8,128)(2,1)}, u32[]{:S(2)}, u32[]{:S(2)}) collective-permute-start(bf16[2,320,256]{2,1,0:T(8,128)(2,1)S(1)} %get-tuple-element.28.own_ref), channel_id=1, source_target_pairs={{0,15},{1,0},{3,2},{4,3},{5,4},{7,6},{8,7},{9,8},{11,10},{12,11},{... | collective-permute-start | bytes 983048 | tf_op jit(solution)/shard_map/ppermute | solution.py:349
  53.2 0.1 add_convert_fusion.flag_ref
  53.3 2.9 %collective-permute-done.6.low_ref = bf16[2,320,256]{2,1,0:T(8,128)(2,1)} collective-permute-done((bf16[2,320,256]{2,1,0:T(8,128)(2,1)}, bf16[2,320,256]{2,1,0:T(8,128)(2,1)}, u32[]{:S(2)}, u32[]{:S(2)}) %collective-permute-start.6) | collective-permute-done | bytes 327712 | tf_op jit(solution)/shard_map/ppermute | solution.py:348
  56.1 1.4 %collective-permute-done.7.high_ref = bf16[2,320,256]{2,1,0:T(8,128)(2,1)} collective-permute-done((bf16[2,320,256]{2,1,0:T(8,128)(2,1)S(1)}, bf16[2,320,256]{2,1,0:T(8,128)(2,1)}, u32[]{:S(2)}, u32[]{:S(2)}) %collective-permute-start.7) | collective-permute-done | bytes 327712 | tf_op jit(solution)/shard_map/ppermute | solution.py:349
  57.6 0.0 copy-done.5
  57.6 0.0 copy-start.1
  57.6 2.9 %copy-done.1 = bf16[4,320,2560]{2,1,0:T(8,128)(2,1)S(1)} copy-done((bf16[4,320,2560]{2,1,0:T(8,128)(2,1)S(1)}, bf16[4,320,2560]{2,1,0:T(8,128)(2,1)}, u32[]{:S(2)}) %copy-start.1) | copy-done | bytes 6553624
  60.4 0.0 copy-start.3
  60.4 2.1 %copy-done.3 = bf16[640,2880]{1,0:T(8,128)(2,1)S(1)} copy-done((bf16[640,2880]{1,0:T(8,128)(2,1)S(1)}, bf16[640,2880]{1,0:T(8,128)(2,1)}, u32[]{:S(2)}) %copy-start.3) | copy-done | bytes 3686424
  62.5 12.7 %last.1 = bf16[2,4,320,128]{3,2,1,0:T(8,128)(2,1)} custom-call(s32[2]{0:T(128)S(1)} %add_convert_fusion.flag_ref, bf16[4,320,256]{2,1,0:T(8,128)(2,1)S(1)} %get-tuple-element.27.skip_ref, bf16[2,320,256]{2,1,0:T(8,128)(2,1)S(1)} %get-tuple-element.28.own_ref, bf16[2,320,256]{2,1,0:T(8,128)(2,1)} %collective-permute-done.6.low_ref, ...), custom_call_target="tpu_custom_call" | custom-call | flops 3565158400 | bytes 1048576 | tf_op jit(solution)/shard_map/last/pallas_call | solution.py:353
Async XLA Ops:
  1.0 17.3 %collective-permute-start = (bf16[2,1,320,128]{3,2,1,0:T(8,128)(2,1)S(1)}, bf16[2,1,320,128]{3,2,1,0:T(8,128)(2,1)S(1)}, u32[]{:S(2)}, u32[]{:S(2)}) collective-permute-start(bf16[2,1,320,128]{3,2,1,0:T(8,128)(2,1)S(1)} %get-tuple-element.34), channel_id=1, source_target_pairs={{0,1},{2,3},{3,4},{4,5},{6,7},{7,8},{8,9},{10,11},{11,12},{12,13},... | collective-permute-start | bytes 491528 | tf_op jit(solution)/shard_map/ppermute | solution.py:292
  3.4 14.9 %collective-permute-start.1 = (bf16[2,1,320,128]{3,2,1,0:T(8,128)(2,1)S(1)}, bf16[2,1,320,128]{3,2,1,0:T(8,128)(2,1)S(1)}, u32[]{:S(2)}, u32[]{:S(2)}) collective-permute-start(bf16[2,1,320,128]{3,2,1,0:T(8,128)(2,1)S(1)} %get-tuple-element.33), channel_id=1, source_target_pairs={{0,15},{1,0},{3,2},{4,3},{5,4},{7,6},{8,7},{9,8},{11,10},{12,11},{... | collective-permute-start | bytes 491528 | tf_op jit(solution)/shard_map/ppermute | solution.py:293
  10.3 1.1 %copy-start.4 = (bf16[2,4,128,320]{2,3,1,0:T(8,128)(2,1)S(1)}, bf16[2,4,128,320]{2,3,1,0:T(8,128)(2,1)}, u32[]{:S(2)}) copy-start(bf16[2,4,128,320]{2,3,1,0:T(8,128)(2,1)} %param.5) | copy-start | bytes 1966084
  11.4 1.6 %copy-start.7 = (bf16[3,3,320,320]{3,2,1,0:T(8,128)(2,1)S(1)}, bf16[3,3,320,320]{3,2,1,0:T(8,128)(2,1)}, u32[]{:S(2)}) copy-start(bf16[3,3,320,320]{3,2,1,0:T(8,128)(2,1)} %param.6) | copy-start | bytes 5529604
  13.0 12.7 %copy-start.6 = (bf16[3,3,320,640]{3,2,1,0:T(8,128)(2,1)S(1)}, bf16[3,3,320,640]{3,2,1,0:T(8,128)(2,1)}, u32[]{:S(2)}) copy-start(bf16[3,3,320,640]{3,2,1,0:T(8,128)(2,1)} %param.8) | copy-start | bytes 11059204
  13.0 12.7 %copy-start.8 = (bf16[3,320,320]{2,1,0:T(8,128)(2,1)S(1)}, bf16[3,320,320]{2,1,0:T(8,128)(2,1)}, u32[]{:S(2)}) copy-start(bf16[3,320,320]{2,1,0:T(8,128)(2,1)} %param.7) | copy-start | bytes 1843204
  14.8 22.3 %collective-permute-start.2 = (bf16[2,320,256]{2,1,0:T(8,128)(2,1)S(1)}, bf16[2,320,256]{2,1,0:T(8,128)(2,1)S(1)}, u32[]{:S(2)}, u32[]{:S(2)}) collective-permute-start(bf16[2,320,256]{2,1,0:T(8,128)(2,1)S(1)} %get-tuple-element.19.inner_ref), channel_id=1, source_target_pairs={{0,4},{1,5},{2,6},{3,7},{4,8},{5,9},{6,10},{7,11},{8,12},{9,13},{1... | collective-permute-start | bytes 983048 | tf_op jit(solution)/shard_map/ppermute | solution.py:305
  17.0 20.2 %collective-permute-start.4 = (bf16[2,320,256]{2,1,0:T(8,128)(2,1)S(1)}, bf16[2,320,256]{2,1,0:T(8,128)(2,1)S(1)}, u32[]{:S(2)}, u32[]{:S(2)}) collective-permute-start(bf16[2,320,256]{2,1,0:T(8,128)(2,1)S(1)} %get-tuple-element.19.inner_ref), channel_id=1, source_target_pairs={{2,14},{3,15},{4,0},{5,1},{6,2},{7,3},{8,4},{9,5},{10,6},{11,7},{1... | collective-permute-start | bytes 983048 | tf_op jit(solution)/shard_map/ppermute | solution.py:306
  19.9 17.3 %collective-permute-start.3 = (bf16[2,320,256]{2,1,0:T(8,128)(2,1)S(1)}, bf16[2,320,256]{2,1,0:T(8,128)(2,1)S(1)}, u32[]{:S(2)}, u32[]{:S(2)}) collective-permute-start(bf16[2,320,256]{2,1,0:T(8,128)(2,1)S(1)} %first_outer.1.outer_ref), channel_id=1, source_target_pairs={{0,4},{1,5},{2,6},{3,7},{4,8},{5,9},{6,10},{7,11},{8,12},{9,13},{1... | collective-permute-start | bytes 983048 | tf_op jit(solution)/shard_map/ppermute | solution.py:315
  24.4 12.7 %collective-permute-start.5 = (bf16[2,320,256]{2,1,0:T(8,128)(2,1)S(1)}, bf16[2,320,256]{2,1,0:T(8,128)(2,1)S(1)}, u32[]{:S(2)}, u32[]{:S(2)}) collective-permute-start(bf16[2,320,256]{2,1,0:T(8,128)(2,1)S(1)} %first_outer.1.outer_ref), channel_id=1, source_target_pairs={{2,14},{3,15},{4,0},{5,1},{6,2},{7,3},{8,4},{9,5},{10,6},{11,7},{1... | collective-permute-start | bytes 983048 | tf_op jit(solution)/shard_map/ppermute | solution.py:316
  25.8 31.8 %copy-start.5 = (bf16[2,4,128,320]{2,3,1,0:T(8,128)(2,1)S(1)}, bf16[2,4,128,320]{2,3,1,0:T(8,128)(2,1)}, u32[]{:S(2)}) copy-start(bf16[2,4,128,320]{2,3,1,0:T(8,128)(2,1)} %param.5) | copy-start | bytes 1966084
  32.5 2.7 %copy-start = (bf16[4,320,2560]{2,1,0:T(8,128)(2,1)}, bf16[4,320,2560]{2,1,0:T(8,128)(2,1)S(1)}, u32[]{:S(2)}) copy-start(bf16[4,320,2560]{2,1,0:T(8,128)(2,1)S(1)} %get-tuple-element.32.phase_weight) | copy-start | bytes 19660804
  35.3 1.9 %copy-start.2 = (bf16[640,2880]{1,0:T(8,128)(2,1)}, bf16[640,2880]{1,0:T(8,128)(2,1)S(1)}, u32[]{:S(2)}) copy-start(bf16[640,2880]{1,0:T(8,128)(2,1)S(1)} %get-tuple-element.30.mid_ref) | copy-start | bytes 11059204
  38.9 17.2 %collective-permute-start.6 = (bf16[2,320,256]{2,1,0:T(8,128)(2,1)}, bf16[2,320,256]{2,1,0:T(8,128)(2,1)}, u32[]{:S(2)}, u32[]{:S(2)}) collective-permute-start(bf16[2,320,256]{2,1,0:T(8,128)(2,1)} %get-tuple-element.29), channel_id=1, source_target_pairs={{0,1},{2,3},{3,4},{4,5},{6,7},{7,8},{8,9},{10,11},{11,12},{12,13},... | collective-permute-start | bytes 983048 | tf_op jit(solution)/shard_map/ppermute | solution.py:348
  40.8 16.8 %collective-permute-start.7 = (bf16[2,320,256]{2,1,0:T(8,128)(2,1)S(1)}, bf16[2,320,256]{2,1,0:T(8,128)(2,1)}, u32[]{:S(2)}, u32[]{:S(2)}) collective-permute-start(bf16[2,320,256]{2,1,0:T(8,128)(2,1)S(1)} %get-tuple-element.28.own_ref), channel_id=1, source_target_pairs={{0,15},{1,0},{3,2},{4,3},{5,4},{7,6},{8,7},{9,8},{11,10},{12,11},{... | collective-permute-start | bytes 983048 | tf_op jit(solution)/shard_map/ppermute | solution.py:349
  57.6 2.9 %copy-start.1 = (bf16[4,320,2560]{2,1,0:T(8,128)(2,1)S(1)}, bf16[4,320,2560]{2,1,0:T(8,128)(2,1)}, u32[]{:S(2)}) copy-start(bf16[4,320,2560]{2,1,0:T(8,128)(2,1)} %copy-done) | copy-start | bytes 19660804
  60.4 2.1 %copy-start.3 = (bf16[640,2880]{1,0:T(8,128)(2,1)S(1)}, bf16[640,2880]{1,0:T(8,128)(2,1)}, u32[]{:S(2)}) copy-start(bf16[640,2880]{1,0:T(8,128)(2,1)} %copy-done.2) | copy-start | bytes 11059204

commit v2 on v0

v2 whole, which is shorter than its diff:
```python
import jax
import jax.numpy as jnp
from jax import lax
from jax.experimental import pallas as pl
from jax.experimental.pallas import tpu as pltpu
from jax.sharding import PartitionSpec as P


FRAMES = 4
BF16 = jnp.bfloat16
F32 = jnp.float32
MIB = 1024 * 1024


def dot(left, right):
    return jnp.dot(left, right, preferred_element_type=F32)


def silu(value):
    return value / (1.0 + jnp.exp(-value))


def sort_pick(width, clips):
    wide, half = width * clips, width // 2
    source = lax.broadcasted_iota(jnp.int32, (wide, wide), 0)
    lane = lax.broadcasted_iota(jnp.int32, (wide, wide), 1)
    parity, clip, j = lane // (wide // 2), lane // half % clips, lane % half
    return (source == clip * width + 2 * j + parity).astype(BF16)


def unsort_pick(width, clips):
    wide, half = width * clips, width // 2
    source = lax.broadcasted_iota(jnp.int32, (wide, wide), 0)
    lane = lax.broadcasted_iota(jnp.int32, (wide, wide), 1)
    clip, column = lane // width, lane % width
    return (source == column % 2 * (wide // 2) + clip * half + column // 2).astype(BF16)


def from_left(value, half):
    lane = lax.broadcasted_iota(jnp.int32, (1, value.shape[1]), 1)
    return jnp.where(lane % half == 0, 0.0, pltpu.roll(value, 1, 1))


def from_right(value, half):
    width = value.shape[1]
    lane = lax.broadcasted_iota(jnp.int32, (1, width), 1)
    return jnp.where(lane % half == half - 1, 0.0, pltpu.roll(value, width - 1, 1))


def store_taps(field, base, even, odd, half):
    channels, lanes = even.shape
    e, o = even.astype(BF16), odd.astype(BF16)
    blocks = ((from_left(odd, half).astype(BF16), e), (e, o), (o, from_right(even, half).astype(BF16)))
    for tap, pair in enumerate(blocks):
        rows = slice(base + tap * channels, base + (tap + 1) * channels)
        field[rows, :lanes] = pair[0]
        field[rows, lanes:] = pair[1]


def store_row_taps(field, base, lane_base, value, half):
    channels, lanes = value.shape
    blocks = (from_left(value, half).astype(BF16), value.astype(BF16), from_right(value, half).astype(BF16))
    for tap, block in enumerate(blocks):
        field[base + tap * channels : base + (tap + 1) * channels, lane_base : lane_base + lanes] = block


def first_inner_kernel(
    latent_hbm, weight_hbm, first_ref, turned_ref, field_ref, low_ref, high_ref,
    latent, weight, latent_sem, weight_sem,
):
    clips, rows, channels, width = latent.shape
    taps = weight.shape[0]
    wide = clips * width
    get_latent = pltpu.make_async_copy(latent_hbm, latent, latent_sem)
    get_latent.start()
    cuts = list(range(0, taps, 1024)) + [taps]
    gets = [
        pltpu.make_async_copy(weight_hbm.at[a:b], weight.at[a:b], weight_sem.at[n])
        for n, (a, b) in enumerate(zip(cuts, cuts[1:]))
    ]
    for get in gets:
        get.start()
    pick = sort_pick(width, clips)
    get_latent.wait()
    low_ref[...] = latent[:, rows - 1]
    high_ref[...] = latent[:, 0]
    depth = 3 * channels
    for row in range(rows):
        natural = jnp.concatenate([latent[clip, row] for clip in range(clips)], axis=1)
        value = dot(natural, pick)
        store_taps(field_ref, row * depth, value[:, : wide // 2], value[:, wide // 2 :], width // 2)
    for get, a, b in zip(gets, cuts, cuts[1:]):
        get.wait()
        turned_ref[:, a:b] = weight[a:b, :].T
    for row in range(rows - 2):
        total = dot(turned_ref[...], field_ref[row * depth : (row + 3) * depth, :])
        first_ref[row] = silu(total).astype(BF16)


def first_outer_kernel(low_ref, high_ref, turned_ref, field_ref, first_ref, rim):
    clips, channels, width = low_ref.shape
    depth = 3 * channels
    rows = field_ref.shape[0] // depth
    wide = clips * width
    pick = sort_pick(width, clips)
    for at, ref in enumerate((low_ref, high_ref)):
        natural = jnp.concatenate([ref[clip] for clip in range(clips)], axis=1)
        value = dot(natural, pick)
        store_taps(rim, at * depth, value[:, : wide // 2], value[:, wide // 2 :], width // 2)
    top = dot(turned_ref[:, depth:], field_ref[: 2 * depth, :])
    top += dot(turned_ref[:, :depth], rim[:depth, :])
    first_ref[0] = silu(top).astype(BF16)
    bottom = dot(turned_ref[:, : 2 * depth], field_ref[(rows - 2) * depth :, :])
    bottom += dot(turned_ref[:, 2 * depth :], rim[depth:, :])
    first_ref[1] = silu(bottom).astype(BF16)


def weights_kernel(
    time_hbm, mid_hbm, up_hbm, time_out, mid_out, skip_out, phase_out,
    time_rows, mid_rows, up_rows, sems,
):
    taps, inner = mid_rows.shape
    channels = up_rows.shape[2]
    cuts = list(range(0, taps, 1024)) + [taps]
    pieces = [(time_hbm, time_rows)]
    pieces += [(mid_hbm.at[a:b], mid_rows.at[a:b]) for a, b in zip(cuts, cuts[1:])]
    pieces += [(up_hbm, up_rows)]
    gets = [
        pltpu.make_async_copy(source, target, sems.at[n])
        for n, (source, target) in enumerate(pieces)
    ]
    for get in gets:
        get.start()
    gets[0].wait()
    time_out[...] = time_rows[...].T
    for get, a, b in zip(gets[1:-1], cuts, cuts[1:]):
        get.wait()
        mid_out[:, a:b] = mid_rows[a:b, :].T
    gets[-1].wait()
    skip_out[...] = jnp.concatenate(
        [up_rows[dr, dc, :, :channels] for dr in range(3) for dc in range(3)], axis=1
    )
    taps = [[up_rows[dr, dc, :, channels:].astype(F32) for dc in range(3)] for dr in range(3)]
    groups = ((lambda t: t[0], lambda t: t[1] + t[2]), (lambda t: t[0] + t[1], lambda t: t[2]))
    for row_phase in range(2):
        for row_tap in range(2):
            merged = [groups[row_phase][row_tap]([taps[dr][dc] for dr in range(3)]) for dc in range(3)]
            for column_phase in range(2):
                for column_tap in range(2):
                    value = groups[column_phase][column_tap](merged)
                    start = (2 * row_tap + column_tap) * inner
                    phase_out[2 * row_phase + column_phase, :, start : start + inner] = value.astype(
                        BF16
                    )


def skip_kernel(
    flag_ref, inner_ref, outer_ref, inner_before, outer_before, inner_after, outer_after, relayed,
    weight_ref, skip_ref, previous_ref, next_ref,
):
    rows, _, wide = skip_ref.shape
    lanes = wide // 2
    for pooled_row in range(rows // 2):
        sums = None
        for row in (2 * pooled_row, 2 * pooled_row + 1):
            edge = row in (0, rows - 1)
            at = (0 if row == 0 else 1) if edge else row - 1
            before, own, after = (
                (outer_before, outer_ref, outer_after)
                if edge
                else (inner_before, inner_ref, inner_after)
            )
            centre, early, late = own[at], before[at], after[at]
            if not edge:
                early = jnp.where(flag_ref[2] != 0, relayed[at], early)
                late = jnp.where(flag_ref[3] != 0, relayed[at], late)
            stacked = jnp.concatenate([early, centre, late], axis=0)
            skip = (centre.astype(F32) + dot(weight_ref[...], stacked)).astype(BF16)
            skip_ref[row] = skip
            if row == 0:
                previous_ref[0] = skip
            if row == rows - 1:
                next_ref[0] = skip
            skip = skip.astype(F32)
            sums = skip if sums is None else sums + skip
        pooled = ((sums[:, :lanes] + sums[:, lanes:]) * 0.25).astype(BF16)
        span = slice(pooled_row * lanes, (pooled_row + 1) * lanes)
        previous_ref[1, :, span] = pooled
        next_ref[1, :, span] = pooled


def own_kernel(skip_ref, pair_ref, mid_ref, skip_weight, mixed_ref, middle_ref, field, pooled, *, half):
    rows, channels, wide = skip_ref.shape
    lanes = wide // 2
    depth = 3 * channels
    for at in range(2):
        row = pair_ref[1, :, at * lanes : (at + 1) * lanes].astype(F32)
        store_row_taps(pooled, 0, at * lanes, row, half)
    for row in range(rows):
        value = skip_ref[row].astype(F32)
        store_taps(field, row * depth, value[:, :lanes], value[:, lanes:], half)
    parts = [dot(mid_ref[:, dr * depth : (dr + 1) * depth], pooled[...]) for dr in range(3)]
    middle_ref[:, :lanes] = parts[2][:, :lanes]
    middle_ref[:, lanes : 2 * lanes] = parts[2][:, lanes:] + parts[1][:, :lanes]
    middle_ref[:, 2 * lanes : 3 * lanes] = parts[1][:, lanes:] + parts[0][:, :lanes]
    middle_ref[:, 3 * lanes :] = parts[0][:, lanes:]
    for row in range(rows):
        first, last = max(row - 1, 0), min(row + 2, rows)
        mixed_ref[row] = dot(
            skip_weight[:, (first - row + 1) * depth : (last - row + 1) * depth],
            field[first * depth : last * depth, :],
        )


def last_kernel(
    flag_ref, mixed_ref, middle_ref, low_ref, high_ref, mid_ref, skip_weight, phase_weight, field_ref,
    out_ref, low_field, high_field, cross_field, rims, middle_field,
):
    rows, channels, wide = mixed_ref.shape
    clips, _, _, width = out_ref.shape
    half, lanes = width // 2, wide // 2
    inner = mid_ref.shape[0]
    depth = 3 * channels

    for target, ref, inward in ((low_field, low_ref, 1), (high_field, high_ref, 0)):
        for at in range(2):
            row = ref[1, :, at * lanes : (at + 1) * lanes].astype(F32)
            store_row_taps(target, 0, at * lanes, row, half)
        cross_field[:, (1 - inward) * lanes : (2 - inward) * lanes] = target[
            :, inward * lanes : (inward + 1) * lanes
        ]
    above = dot(mid_ref[:, :depth], low_field[...])
    cross = dot(mid_ref[:, depth : 2 * depth], cross_field[...])
    below = dot(mid_ref[:, 2 * depth :], high_field[...])
    middles = [
        middle_ref[:, :lanes] + above[:, :lanes] + cross[:, :lanes],
        middle_ref[:, lanes : 2 * lanes] + above[:, lanes:],
        middle_ref[:, 2 * lanes : 3 * lanes] + below[:, :lanes],
        middle_ref[:, 3 * lanes :] + below[:, lanes:] + cross[:, lanes:],
    ]
    kept = (flag_ref[0] == 0, None, None, flag_ref[1] == 0)
    for at, (value, keep) in enumerate(zip(middles, kept)):
        value = silu(value)
        if keep is not None:
            value = jnp.where(keep, value, 0.0)
        store_row_taps(middle_field, at * 3 * inner, 0, value.astype(BF16).astype(F32), half)

    for at, ref in enumerate((low_ref, high_ref)):
        value = ref[0].astype(F32)
        store_taps(rims, at * depth, value[:, :lanes], value[:, lanes:], half)
    from_rim = {
        0: dot(skip_weight[:, :depth], rims[:depth, :]),
        rows - 1: dot(skip_weight[:, 2 * depth :], rims[depth:, :]),
    }
    unsort = unsort_pick(width, clips)
    block = 3 * inner
    for row_phase in range(2):
        phases = []
        for column_phase in range(2):
            total = None
            for tap in range(2):
                sides = [
                    middle_field[
                        (row_phase + tap + at) * block
                        + column_phase * inner : (row_phase + tap + at) * block
                        + (column_phase + 2) * inner,
                        :,
                    ]
                    for at in range(rows // 2)
                ]
                part = dot(
                    phase_weight[
                        2 * row_phase + column_phase, :, tap * 2 * inner : (tap + 1) * 2 * inner
                    ],
                    jnp.concatenate(sides, axis=1),
                )
                total = part if total is None else total + part
            phases.append(total)
        for at in range(rows // 2):
            row = 2 * at + row_phase
            latent = field_ref[row * depth + channels : row * depth + 2 * channels, :].astype(F32)
            upper = jnp.concatenate([phase[:, at * lanes : (at + 1) * lanes] for phase in phases], axis=1)
            total = latent + mixed_ref[row] + upper
            if row in from_rim:
                total += from_rim[row]
            natural = dot(total.astype(BF16), unsort).astype(BF16)
            for clip in range(clips):
                out_ref[clip, row] = natural[:, clip * width : (clip + 1) * width]


def call(kernel, name, outputs, limit, scratch=(), flops=0, kept=True, inputs=None):
    shapes = [
        pltpu.VMEM(shape, dtype) if kept else jax.ShapeDtypeStruct(shape, dtype)
        for shape, dtype in outputs
    ]
    specs = {} if inputs is None else {"in_specs": inputs}
    return pl.pallas_call(
        kernel,
        out_shape=shapes,
        scratch_shapes=list(scratch),
        compiler_params=pltpu.CompilerParams(vmem_limit_bytes=limit * MIB),
        cost_estimate=pl.CostEstimate(flops=flops, bytes_accessed=1 << 20, transcendentals=0),
        name=name,
        **specs,
    )


def in_hbm(value):
    return pltpu.with_memory_space_constraint(value, pltpu.HBM)


def in_vmem(*values):
    return [pltpu.with_memory_space_constraint(value, pltpu.VMEM) for value in values]


def body(latents, in_weight, time_weight, mid_weight, up_weight):
    device_count = lax.axis_size("frames")
    bands = device_count // FRAMES
    offset = bands // 2
    band_of = lambda index: (index + offset) % bands
    frame_of = lambda index: (index + offset) // bands % FRAMES
    chain = lambda step, keep: [
        (i, (i + step) % device_count) for i in range(device_count) if keep(i)
    ]
    band = band_of(lax.axis_index("frames"))
    down = chain(1, lambda i: band_of(i) != bands - 1)
    up = chain(-1, lambda i: band_of(i) != 0)
    later = chain(bands, lambda i: frame_of(i) != FRAMES - 1)
    earlier = chain(-bands, lambda i: frame_of(i) != 0)
    near = lambda pairs: [(i, j) for i, j in pairs if abs(i - j) == bands]
    far = [(i, j) for i, j in later + earlier if abs(i - j) != bands]
    hops = [(i, i - offset) for i, _ in far]
    relays = [(i - offset, j) for i, j in far]
    index = lax.axis_index("frames")
    flags = jnp.stack(
        [
            band == 0,
            band == bands - 1,
            jnp.logical_and(index >= offset, index < bands),
            index >= device_count - offset,
        ]
    ).astype(jnp.int32)

    clips, rows, width, channels = latents.shape
    inner = mid_weight.shape[3]
    wide = clips * width
    depth = 3 * channels
    anywhere = pl.BlockSpec(memory_space=pl.ANY)
    whole = pl.BlockSpec(memory_space=pltpu.VMEM)
    scalars = pl.BlockSpec(memory_space=pltpu.SMEM)
    turned = jnp.swapaxes(latents, 2, 3)

    first_inner, in_turned, field, low_rim, high_rim = call(
        first_inner_kernel,
        "first_inner",
        [
            ((rows - 2, channels, wide), BF16),
            ((channels, 3 * depth), BF16),
            ((rows * depth, wide), BF16),
            ((clips, channels, width), BF16),
            ((clips, channels, width), BF16),
        ],
        12,
        [
            pltpu.VMEM(turned.shape, BF16),
            pltpu.VMEM((3 * depth, channels), BF16),
            pltpu.SemaphoreType.DMA(()),
            pltpu.SemaphoreType.DMA((-(-3 * depth // 1024),)),
        ],
        flops=2 * (rows - 2) * wide * channels * 3 * depth,
        inputs=[anywhere, anywhere],
    )(in_hbm(turned), in_hbm(in_weight.reshape(3 * depth, channels)))
    hopped = lax.ppermute(first_inner, "frames", hops)
    inner_before = lax.ppermute(first_inner, "frames", near(later))
    inner_after = lax.ppermute(first_inner, "frames", near(earlier))
    relayed = lax.ppermute(hopped, "frames", relays)
    low = lax.ppermute(low_rim, "frames", down)
    high = lax.ppermute(high_rim, "frames", up)

    (first_outer,) = call(
        first_outer_kernel,
        "first_outer",
        [((2, channels, wide), BF16)],
        8,
        [pltpu.VMEM((2 * depth, wide), BF16)],
        flops=2 * 2 * wide * channels * 3 * depth,
        inputs=[whole] * 4,
    )(*in_vmem(low, high, in_turned, field))
    outer_before = lax.ppermute(first_outer, "frames", later)
    outer_after = lax.ppermute(first_outer, "frames", earlier)

    time_rows, mid_rows, up_rows, first_outer, _ = lax.optimization_barrier(
        (
            time_weight.reshape(depth, channels),
            mid_weight.reshape(3 * depth, inner),
            jnp.swapaxes(up_weight, 2, 3),
            first_outer,
            hopped,
        )
    )
    time_turned, mid_turned, skip_weight, phase_weight = call(
        weights_kernel,
        "weights",
        [
            ((channels, depth), BF16),
            ((inner, 3 * depth), BF16),
            ((channels, 3 * depth), BF16),
            ((4, channels, 4 * inner), BF16),
        ],
        20,
        [
            pltpu.VMEM(time_rows.shape, BF16),
            pltpu.VMEM(mid_rows.shape, BF16),
            pltpu.VMEM(up_rows.shape, BF16),
            pltpu.SemaphoreType.DMA((2 + -(-3 * depth // 1024),)),
        ],
        flops=2 * 10**9,
        inputs=[anywhere] * 3,
    )(in_hbm(time_rows), in_hbm(mid_rows), in_hbm(up_rows))

    skip, to_previous, to_next = call(
        skip_kernel,
        "skip",
        [
            ((rows, channels, wide), BF16),
            ((2, channels, wide), BF16),
            ((2, channels, wide), BF16),
        ],
        8,
        flops=2 * rows * wide * depth * channels,
        inputs=[scalars] + [whole] * 8,
    )(
        flags,
        *in_vmem(
            first_inner,
            first_outer,
            inner_before,
            outer_before,
            inner_after,
            outer_after,
            relayed,
            time_turned,
        ),
    )
    from_previous = lax.ppermute(to_next, "frames", down)
    from_next = lax.ppermute(to_previous, "frames", up)

    mixed, middle = call(
        lambda *refs: own_kernel(*refs, half=width // 2),
        "own_rows",
        [((rows, channels, wide), F32), ((inner, 2 * wide), F32)],
        16,
        [pltpu.VMEM((rows * depth, wide), BF16), pltpu.VMEM((depth, wide), BF16)],
        flops=2 * wide * depth * (3 * inner + (3 * rows - 2) * channels),
        inputs=[whole] * 4,
    )(*in_vmem(skip, to_previous, mid_turned, skip_weight))

    (out,) = call(
        last_kernel,
        "last",
        [(turned.shape, BF16)],
        20,
        [
            pltpu.VMEM((depth, wide), BF16),
            pltpu.VMEM((depth, wide), BF16),
            pltpu.VMEM((depth, wide), BF16),
            pltpu.VMEM((2 * depth, wide), BF16),
            pltpu.VMEM((4 * 3 * inner, wide // 2), BF16),
        ],
        flops=2 * wide * (3 * depth * inner + 2 * depth * channels + rows * 4 * inner * channels),
        kept=False,
        inputs=[scalars] + [whole] * 8,
    )(
        flags,
        *in_vmem(
            mixed, middle, from_previous, from_next, mid_turned, skip_weight, phase_weight, field
        ),
    )
    return jnp.swapaxes(out, 2, 3)


def solution(mesh):
    in_specs = (P("groups", "frames", None, None), P(), P(), P(), P())
    out_specs = P("groups", "frames", None, None)
    return jax.shard_map(body, mesh=mesh, in_specs=in_specs, out_specs=out_specs, check_vma=False)
```

time: 134 us -> 61.9 us (0.46)
  the two profiles are of different devices: /device:TPU:1 before, /device:TPU:0 now
where the time goes in v2:
time: 61.9 us; the launch traced here: 61.5 us
  starting transfers between devices  37.1 us (60%)
  Pallas kernels  22.9 us (37%)
  waiting for transfers between devices  1.31 us (2%)
    ppermute x1, starting transfers between devices, body(): high = lax.ppermute(high_rim, 'frames', up)  8.45 us
    ppermute x1, starting transfers between devices, body(): from_previous = lax.ppermute(to_next, 'frames', down)  7.08 us
    pallas_call x1, Pallas kernels, body(): call(weights_kernel, 'weights', [((channels, depth), BF16), ((inner, 3 *...  6.9 us
    pallas_call x1, Pallas kernels, body(): call(last_kernel, 'last', [(turned.shape, BF16)], 20, [pltpu.VMEM((depth,...  5.35 us
    ppermute x1, starting transfers between devices, body(): outer_before = lax.ppermute(first_outer, 'frames', later)  5.27 us
    ppermute x1, starting transfers between devices, body(): inner_before = lax.ppermute(first_inner, 'frames', near(later))  4.57 us
    pallas_call x1, Pallas kernels, body(): call(first_inner_kernel, 'first_inner', [((rows - 2, channels, wide), BF1...  3.87 us
    ppermute x1, starting transfers between devices, body(): from_next = lax.ppermute(to_previous, 'frames', up)  3.43 us
  transfers between devices with their start and end apart: 10, of which 1 were waited for; matrix products, arithmetic and copies ran while one was open for 0% of the time, Pallas kernels for 19%

profile of v2, /device:TPU:0, one launch (start us, length us, event | category | flops | bytes accessed | tf_op | source)
XLA Modules:
  0.0 61.5 jit_solution(6286835042285858422)
XLA Ops:
  0.0 3.9 %first_inner.1 = (bf16[2,320,256]{2,1,0:T(8,128)(2,1)S(1)}, bf16[320,2880]{1,0:T(8,128)(2,1)S(1)}, bf16[3840,256]{1,0:T(8,128)(2,1)S(1)}, bf16[2,320,128]{2,1,0:T(8,128)(2,1)S(1)}, bf16[2,320,128]{2,1,0:T(8,128)(2,1)S(1)}) custom-call(bf16[2,4,320,128]{3,2,1,0:T(8,128)(2,1)} %bitcast.14, bf16[2880,320]{1,0:T(8,128)(2,1)} %bitcast.13), custom_call_target="tpu_custom_call" | custom-call | flops 943718400 | bytes 1048576 | tf_op jit(solution)/shard_map/first_inner/pallas_call | solution.py:353
  3.9 1.3 %collective-permute-start.2 = (bf16[2,320,256]{2,1,0:T(8,128)(2,1)S(1)}, bf16[2,320,256]{2,1,0:T(8,128)(2,1)}, u32[]{:S(2)}, u32[]{:S(2)}) collective-permute-start(bf16[2,320,256]{2,1,0:T(8,128)(2,1)S(1)} %get-tuple-element.23.inner_ref), channel_id=1, source_target_pairs={{14,12},{15,13},{2,0},{3,1},{30,28},{31,29},{18,16},{19,17}} | collective-permute-start | bytes 983048 | tf_op jit(solution)/shard_map/ppermute | solution.py:373
  5.2 2.4 %collective-permute-start = (bf16[2,320,128]{2,1,0:T(8,128)(2,1)S(1)}, bf16[2,320,128]{2,1,0:T(8,128)(2,1)S(1)}, u32[]{:S(2)}, u32[]{:S(2)}) collective-permute-start(bf16[2,320,128]{2,1,0:T(8,128)(2,1)S(1)} %get-tuple-element.24), channel_id=1, source_target_pairs={{0,1},{2,3},{3,4},{4,5},{6,7},{7,8},{8,9},{10,11},{11,12},{12,13},... | collective-permute-start | bytes 491528 | tf_op jit(solution)/shard_map/ppermute | solution.py:377
  7.5 8.5 %collective-permute-start.1 = (bf16[2,320,128]{2,1,0:T(8,128)(2,1)S(1)}, bf16[2,320,128]{2,1,0:T(8,128)(2,1)S(1)}, u32[]{:S(2)}, u32[]{:S(2)}) collective-permute-start(bf16[2,320,128]{2,1,0:T(8,128)(2,1)S(1)} %get-tuple-element.25), channel_id=1, source_target_pairs={{0,15},{1,0},{3,2},{4,3},{5,4},{7,6},{8,7},{9,8},{11,10},{12,11},{... | collective-permute-start | bytes 491528 | tf_op jit(solution)/shard_map/ppermute | solution.py:378
  16.0 1.3 %collective-permute-start.5 = (bf16[2,320,256]{2,1,0:T(8,128)(2,1)S(1)}, bf16[2,320,256]{2,1,0:T(8,128)(2,1)S(1)}, u32[]{:S(2)}, u32[]{:S(2)}) collective-permute-start(bf16[2,320,256]{2,1,0:T(8,128)(2,1)S(1)} %get-tuple-element.23.inner_ref), channel_id=1, source_target_pairs={{4,0},{5,1},{6,2},{7,3},{8,4},{9,5},{10,6},{11,7},{12,8},{13,9},{2... | collective-permute-start | bytes 983048 | tf_op jit(solution)/shard_map/ppermute | solution.py:375
  17.3 4.6 %collective-permute-start.3 = (bf16[2,320,256]{2,1,0:T(8,128)(2,1)S(1)}, bf16[2,320,256]{2,1,0:T(8,128)(2,1)S(1)}, u32[]{:S(2)}, u32[]{:S(2)}) collective-permute-start(bf16[2,320,256]{2,1,0:T(8,128)(2,1)S(1)} %get-tuple-element.23.inner_ref), channel_id=1, source_target_pairs={{0,4},{1,5},{2,6},{3,7},{4,8},{5,9},{6,10},{7,11},{8,12},{9,13},{1... | collective-permute-start | bytes 983048 | tf_op jit(solution)/shard_map/ppermute | solution.py:374
  21.9 0.0 collective-permute-done.low_ref
  21.9 0.0 collective-permute-done.1.high_ref
  21.9 1.6 %first_outer.1.outer_ref = bf16[2,320,256]{2,1,0:T(8,128)(2,1)S(1)} custom-call(bf16[2,320,128]{2,1,0:T(8,128)(2,1)S(1)} %collective-permute-done.low_ref, bf16[2,320,128]{2,1,0:T(8,128)(2,1)S(1)} %collective-permute-done.1.high_ref, bf16[320,2880]{1,0:T(8,128)(2,1)S(1)} %get-tuple-element.26.turned_ref, bf16[3840,256]{1,0:T(8,128)(2,1)S(1)} %get-tuple-element.27.field_ref), custom_call_target="tpu_custom_call" | custom-call | flops 943718400 | bytes 1048576 | tf_op jit(solution)/shard_map/first_outer/pallas_call | solution.py:380
  23.5 1.3 %collective-permute-start.6 = (bf16[2,320,256]{2,1,0:T(8,128)(2,1)S(1)}, bf16[2,320,256]{2,1,0:T(8,128)(2,1)}, u32[]{:S(2)}, u32[]{:S(2)}) collective-permute-start(bf16[2,320,256]{2,1,0:T(8,128)(2,1)S(1)} %first_outer.1.outer_ref), channel_id=1, source_target_pairs={{2,14},{3,15},{4,0},{5,1},{6,2},{7,3},{8,4},{9,5},{10,6},{11,7},{1... | collective-permute-start | bytes 983048 | tf_op jit(solution)/shard_map/ppermute | solution.py:390
  24.8 5.3 %collective-permute-start.4 = (bf16[2,320,256]{2,1,0:T(8,128)(2,1)S(1)}, bf16[2,320,256]{2,1,0:T(8,128)(2,1)}, u32[]{:S(2)}, u32[]{:S(2)}) collective-permute-start(bf16[2,320,256]{2,1,0:T(8,128)(2,1)S(1)} %first_outer.1.outer_ref), channel_id=1, source_target_pairs={{0,4},{1,5},{2,6},{3,7},{4,8},{5,9},{6,10},{7,11},{8,12},{9,13},{1... | collective-permute-start | bytes 983048 | tf_op jit(solution)/shard_map/ppermute | solution.py:389
  30.1 0.0 collective-permute-done.2
  30.1 2.0 %collective-permute-start.7 = (bf16[2,320,256]{2,1,0:T(8,128)(2,1)}, bf16[2,320,256]{2,1,0:T(8,128)(2,1)}, u32[]{:S(2)}, u32[]{:S(2)}) collective-permute-start(bf16[2,320,256]{2,1,0:T(8,128)(2,1)} %collective-permute-done.2), channel_id=1, source_target_pairs={{12,2},{13,3},{0,14},{1,15},{28,18},{29,19},{16,30},{17,31}} | collective-permute-start | bytes 983048 | tf_op jit(solution)/shard_map/ppermute | solution.py:376
  32.1 0.1 add_convert_fusion.flag_ref
  32.2 6.9 %weights.1 = (bf16[320,960]{1,0:T(8,128)(2,1)S(1)}, bf16[640,2880]{1,0:T(8,128)(2,1)S(1)}, bf16[320,2880]{1,0:T(8,128)(2,1)S(1)}, bf16[4,320,2560]{2,1,0:T(8,128)(2,1)S(1)}) custom-call(bf16[960,320]{1,0:T(8,128)(2,1)} %bitcast.12, bf16[2880,640]{1,0:T(8,128)(2,1)} %bitcast.11, bf16[3,3,320,960]{3,2,1,0:T(8,128)(2,1)} %bitcast.10), custom_call_target="tpu_custom_call" | custom-call | flops 2000000000 | bytes 1048576 | tf_op jit(solution)/shard_map/weights/pallas_call | solution.py:401
  39.1 0.0 collective-permute-done.5.inner_after
  39.1 0.0 collective-permute-done.3.inner_before
  39.1 0.0 collective-permute-done.6.outer_after
  39.1 0.0 collective-permute-done.4.outer_before
  39.1 0.0 collective-permute-done.7.relayed
  39.1 2.1 %skip.1 = (bf16[4,320,256]{2,1,0:T(8,128)(2,1)S(1)}, bf16[2,320,256]{2,1,0:T(8,128)(2,1)S(1)}, bf16[2,320,256]{2,1,0:T(8,128)(2,1)S(1)}) custom-call(s32[4]{0:T(128)S(1)} %add_convert_fusion.flag_ref, bf16[2,320,256]{2,1,0:T(8,128)(2,1)S(1)} %get-tuple-element.23.inner_ref, bf16[2,320,256]{2,1,0:T(8,128)(2,1)S(1)} %first_outer.1.outer_ref, ...), custom_call_target="tpu_custom_call" | custom-call | flops 629145600 | bytes 1048576 | tf_op jit(solution)/shard_map/skip/pallas_call | solution.py:421
  41.3 7.1 %collective-permute-start.8 = (bf16[2,320,256]{2,1,0:T(8,128)(2,1)S(1)}, bf16[2,320,256]{2,1,0:T(8,128)(2,1)S(1)}, u32[]{:S(2)}, u32[]{:S(2)}) collective-permute-start(bf16[2,320,256]{2,1,0:T(8,128)(2,1)S(1)} %get-tuple-element.39), channel_id=1, source_target_pairs={{0,1},{2,3},{3,4},{4,5},{6,7},{7,8},{8,9},{10,11},{11,12},{12,13},... | collective-permute-start | bytes 983048 | tf_op jit(solution)/shard_map/ppermute | solution.py:445
  48.4 3.4 %collective-permute-start.9 = (bf16[2,320,256]{2,1,0:T(8,128)(2,1)S(1)}, bf16[2,320,256]{2,1,0:T(8,128)(2,1)S(1)}, u32[]{:S(2)}, u32[]{:S(2)}) collective-permute-start(bf16[2,320,256]{2,1,0:T(8,128)(2,1)S(1)} %get-tuple-element.34.refs_1_), channel_id=1, source_target_pairs={{0,15},{1,0},{3,2},{4,3},{5,4},{7,6},{8,7},{9,8},{11,10},{12,11},{... | collective-permute-start | bytes 983048 | tf_op jit(solution)/shard_map/ppermute | solution.py:446
  51.8 3.1 %own_rows.1 = (f32[4,320,256]{2,1,0:T(8,128)S(1)}, f32[640,512]{1,0:T(8,128)S(1)}) custom-call(bf16[4,320,256]{2,1,0:T(8,128)(2,1)S(1)} %get-tuple-element.33.refs_0_, bf16[2,320,256]{2,1,0:T(8,128)(2,1)S(1)} %get-tuple-element.34.refs_1_, bf16[640,2880]{1,0:T(8,128)(2,1)S(1)} %get-tuple-element.35.refs_2_.mid_ref, ...), custom_call_target="tpu_custom_call" | custom-call | flops 2516582400 | bytes 1048576 | tf_op jit(solution)/shard_map/own_rows/pallas_call | solution.py:448
  54.9 0.0 collective-permute-done.8.low_ref
  54.9 1.3 %collective-permute-done.9.high_ref = bf16[2,320,256]{2,1,0:T(8,128)(2,1)S(1)} collective-permute-done((bf16[2,320,256]{2,1,0:T(8,128)(2,1)S(1)}, bf16[2,320,256]{2,1,0:T(8,128)(2,1)S(1)}, u32[]{:S(2)}, u32[]{:S(2)}) %collective-permute-start.9) | collective-permute-done | bytes 327712 | tf_op jit(solution)/shard_map/ppermute | solution.py:446
  56.2 5.3 %last.1 = bf16[2,4,320,128]{3,2,1,0:T(8,128)(2,1)} custom-call(s32[4]{0:T(128)S(1)} %add_convert_fusion.flag_ref, f32[4,320,256]{2,1,0:T(8,128)S(1)} %get-tuple-element.37.mixed_ref, f32[640,512]{1,0:T(8,128)S(1)} %get-tuple-element.38.middle_ref, bf16[2,320,256]{2,1,0:T(8,128)(2,1)S(1)} %collective-permute-done.8.low_ref, ...), custom_call_target="tpu_custom_call" | custom-call | flops 2936012800 | bytes 1048576 | tf_op jit(solution)/shard_map/last/pallas_call | solution.py:458
Async XLA Ops:
  3.9 26.2 %collective-permute-start.2 = (bf16[2,320,256]{2,1,0:T(8,128)(2,1)S(1)}, bf16[2,320,256]{2,1,0:T(8,128)(2,1)}, u32[]{:S(2)}, u32[]{:S(2)}) collective-permute-start(bf16[2,320,256]{2,1,0:T(8,128)(2,1)S(1)} %get-tuple-element.23.inner_ref), channel_id=1, source_target_pairs={{14,12},{15,13},{2,0},{3,1},{30,28},{31,29},{18,16},{19,17}} | collective-permute-start | bytes 983048 | tf_op jit(solution)/shard_map/ppermute | solution.py:373
  5.2 16.7 %collective-permute-start = (bf16[2,320,128]{2,1,0:T(8,128)(2,1)S(1)}, bf16[2,320,128]{2,1,0:T(8,128)(2,1)S(1)}, u32[]{:S(2)}, u32[]{:S(2)}) collective-permute-start(bf16[2,320,128]{2,1,0:T(8,128)(2,1)S(1)} %get-tuple-element.24), channel_id=1, source_target_pairs={{0,1},{2,3},{3,4},{4,5},{6,7},{7,8},{8,9},{10,11},{11,12},{12,13},... | collective-permute-start | bytes 491528 | tf_op jit(solution)/shard_map/ppermute | solution.py:377
  7.5 14.3 %collective-permute-start.1 = (bf16[2,320,128]{2,1,0:T(8,128)(2,1)S(1)}, bf16[2,320,128]{2,1,0:T(8,128)(2,1)S(1)}, u32[]{:S(2)}, u32[]{:S(2)}) collective-permute-start(bf16[2,320,128]{2,1,0:T(8,128)(2,1)S(1)} %get-tuple-element.25), channel_id=1, source_target_pairs={{0,15},{1,0},{3,2},{4,3},{5,4},{7,6},{8,7},{9,8},{11,10},{12,11},{... | collective-permute-start | bytes 491528 | tf_op jit(solution)/shard_map/ppermute | solution.py:378
  16.0 23.1 %collective-permute-start.5 = (bf16[2,320,256]{2,1,0:T(8,128)(2,1)S(1)}, bf16[2,320,256]{2,1,0:T(8,128)(2,1)S(1)}, u32[]{:S(2)}, u32[]{:S(2)}) collective-permute-start(bf16[2,320,256]{2,1,0:T(8,128)(2,1)S(1)} %get-tuple-element.23.inner_ref), channel_id=1, source_target_pairs={{4,0},{5,1},{6,2},{7,3},{8,4},{9,5},{10,6},{11,7},{12,8},{13,9},{2... | collective-permute-start | bytes 983048 | tf_op jit(solution)/shard_map/ppermute | solution.py:375
  17.3 21.8 %collective-permute-start.3 = (bf16[2,320,256]{2,1,0:T(8,128)(2,1)S(1)}, bf16[2,320,256]{2,1,0:T(8,128)(2,1)S(1)}, u32[]{:S(2)}, u32[]{:S(2)}) collective-permute-start(bf16[2,320,256]{2,1,0:T(8,128)(2,1)S(1)} %get-tuple-element.23.inner_ref), channel_id=1, source_target_pairs={{0,4},{1,5},{2,6},{3,7},{4,8},{5,9},{6,10},{7,11},{8,12},{9,13},{1... | collective-permute-start | bytes 983048 | tf_op jit(solution)/shard_map/ppermute | solution.py:374
  23.5 15.6 %collective-permute-start.6 = (bf16[2,320,256]{2,1,0:T(8,128)(2,1)S(1)}, bf16[2,320,256]{2,1,0:T(8,128)(2,1)}, u32[]{:S(2)}, u32[]{:S(2)}) collective-permute-start(bf16[2,320,256]{2,1,0:T(8,128)(2,1)S(1)} %first_outer.1.outer_ref), channel_id=1, source_target_pairs={{2,14},{3,15},{4,0},{5,1},{6,2},{7,3},{8,4},{9,5},{10,6},{11,7},{1... | collective-permute-start | bytes 983048 | tf_op jit(solution)/shard_map/ppermute | solution.py:390
  24.8 14.3 %collective-permute-start.4 = (bf16[2,320,256]{2,1,0:T(8,128)(2,1)S(1)}, bf16[2,320,256]{2,1,0:T(8,128)(2,1)}, u32[]{:S(2)}, u32[]{:S(2)}) collective-permute-start(bf16[2,320,256]{2,1,0:T(8,128)(2,1)S(1)} %first_outer.1.outer_ref), channel_id=1, source_target_pairs={{0,4},{1,5},{2,6},{3,7},{4,8},{5,9},{6,10},{7,11},{8,12},{9,13},{1... | collective-permute-start | bytes 983048 | tf_op jit(solution)/shard_map/ppermute | solution.py:389
  30.1 9.1 %collective-permute-start.7 = (bf16[2,320,256]{2,1,0:T(8,128)(2,1)}, bf16[2,320,256]{2,1,0:T(8,128)(2,1)}, u32[]{:S(2)}, u32[]{:S(2)}) collective-permute-start(bf16[2,320,256]{2,1,0:T(8,128)(2,1)} %collective-permute-done.2), channel_id=1, source_target_pairs={{12,2},{13,3},{0,14},{1,15},{28,18},{29,19},{16,30},{17,31}} | collective-permute-start | bytes 983048 | tf_op jit(solution)/shard_map/ppermute | solution.py:376
  41.3 13.6 %collective-permute-start.8 = (bf16[2,320,256]{2,1,0:T(8,128)(2,1)S(1)}, bf16[2,320,256]{2,1,0:T(8,128)(2,1)S(1)}, u32[]{:S(2)}, u32[]{:S(2)}) collective-permute-start(bf16[2,320,256]{2,1,0:T(8,128)(2,1)S(1)} %get-tuple-element.39), channel_id=1, source_target_pairs={{0,1},{2,3},{3,4},{4,5},{6,7},{7,8},{8,9},{10,11},{11,12},{12,13},... | collective-permute-start | bytes 983048 | tf_op jit(solution)/shard_map/ppermute | solution.py:445
  48.4 7.8 %collective-permute-start.9 = (bf16[2,320,256]{2,1,0:T(8,128)(2,1)S(1)}, bf16[2,320,256]{2,1,0:T(8,128)(2,1)S(1)}, u32[]{:S(2)}, u32[]{:S(2)}) collective-permute-start(bf16[2,320,256]{2,1,0:T(8,128)(2,1)S(1)} %get-tuple-element.34.refs_1_), channel_id=1, source_target_pairs={{0,15},{1,0},{3,2},{4,3},{5,4},{7,6},{8,7},{9,8},{11,10},{12,11},{... | collective-permute-start | bytes 983048 | tf_op jit(solution)/shard_map/ppermute | solution.py:446

commit v3 on v2

--- a/solution.py
+++ b/solution.py
@@ -64,13 +64,24 @@
         field[base + tap * channels : base + (tap + 1) * channels, lane_base : lane_base + lanes] = block
 
 
-def first_inner_kernel(
-    latent_hbm, weight_hbm, first_ref, turned_ref, field_ref, low_ref, high_ref,
-    latent, weight, latent_sem, weight_sem,
+def rims_kernel(flag_ref, latent_hbm, inside_ref, across_ref, sems):
+    last = latent_hbm.shape[1] - 1
+    odd = flag_ref[2]
+    gets = [
+        pltpu.make_async_copy(latent_hbm.at[:, row], ref, sems.at[at])
+        for at, (row, ref) in enumerate(((last * (1 - odd), inside_ref), (last * odd, across_ref)))
+    ]
+    for get in gets:
+        get.start()
+    for get in gets:
+        get.wait()
+
+
+def prepare_kernel(
+    latent_hbm, weight_hbm, turned_ref, field_ref, latent, weight, latent_sem, weight_sem
 ):
     clips, rows, channels, width = latent.shape
     taps = weight.shape[0]
-    wide = clips * width
     get_latent = pltpu.make_async_copy(latent_hbm, latent, latent_sem)
     get_latent.start()
     cuts = list(range(0, taps, 1024)) + [taps]
@@ -82,37 +93,50 @@
         get.start()
     pick = sort_pick(width, clips)
     get_latent.wait()
-    low_ref[...] = latent[:, rows - 1]
-    high_ref[...] = latent[:, 0]
-    depth = 3 * channels
     for row in range(rows):
-        natural = jnp.concatenate([latent[clip, row] for clip in range(clips)], axis=1)
-        value = dot(natural, pick)
-        store_taps(field_ref, row * depth, value[:, : wide // 2], value[:, wide // 2 :], width // 2)
+        value = dot(jnp.concatenate([latent[clip, row] for clip in range(clips)], axis=1), pick)
+        lanes = value.shape[1] // 2
+        store_taps(field_ref, row * 3 * channels, value[:, :lanes], value[:, lanes:], width // 2)
     for get, a, b in zip(gets, cuts, cuts[1:]):
         get.wait()
         turned_ref[:, a:b] = weight[a:b, :].T
-    for row in range(rows - 2):
-        total = dot(turned_ref[...], field_ref[row * depth : (row + 3) * depth, :])
-        first_ref[row] = silu(total).astype(BF16)
-
-
-def first_outer_kernel(low_ref, high_ref, turned_ref, field_ref, first_ref, rim):
-    clips, channels, width = low_ref.shape
+
+
+def first_own_kernel(turned_ref, field_ref, first_ref, partial_ref):
+    rows, channels, _ = first_ref.shape
     depth = 3 * channels
-    rows = field_ref.shape[0] // depth
-    wide = clips * width
+    for row in range(rows):
+        start, stop = max(row - 1, 0), min(row + 2, rows)
+        total = dot(
+            turned_ref[:, (start - row + 1) * depth : (stop - row + 1) * depth],
+            field_ref[start * depth : stop * depth, :],
+        )
+        if row == 0:
+            partial_ref[0] = total
+        elif row == rows - 1:
+            partial_ref[1] = total
+        else:
+            first_ref[row] = silu(total).astype(BF16)
+
+
+def first_rest_kernel(
+    flag_ref, inside_ref, across_ref, turned_ref, partial_ref, own_ref, first_ref, rim
+):
+    clips, channels, width = inside_ref.shape
+    depth = 3 * channels
+    rows = first_ref.shape[0]
     pick = sort_pick(width, clips)
-    for at, ref in enumerate((low_ref, high_ref)):
-        natural = jnp.concatenate([ref[clip] for clip in range(clips)], axis=1)
-        value = dot(natural, pick)
-        store_taps(rim, at * depth, value[:, : wide // 2], value[:, wide // 2 :], width // 2)
-    top = dot(turned_ref[:, depth:], field_ref[: 2 * depth, :])
-    top += dot(turned_ref[:, :depth], rim[:depth, :])
+    odd = flag_ref[2] != 0
+    for at in range(2):
+        one, other = (inside_ref, across_ref) if at == 0 else (across_ref, inside_ref)
+        blocks = [jnp.where(odd, one[clip], other[clip]) for clip in range(clips)]
+        value = dot(jnp.concatenate(blocks, axis=1), pick)
+        lanes = value.shape[1] // 2
+        store_taps(rim, at * depth, value[:, :lanes], value[:, lanes:], width // 2)
+    top = partial_ref[0] + dot(turned_ref[:, :depth], rim[:depth, :])
     first_ref[0] = silu(top).astype(BF16)
-    bottom = dot(turned_ref[:, : 2 * depth], field_ref[(rows - 2) * depth :, :])
-    bottom += dot(turned_ref[:, 2 * depth :], rim[depth:, :])
-    first_ref[1] = silu(bottom).astype(BF16)
+    bottom = partial_ref[1] + dot(turned_ref[:, 2 * depth :], rim[depth:, :])
+    first_ref[rows - 1] = silu(bottom).astype(BF16)
 
 
 def weights_kernel(
@@ -155,38 +179,30 @@
 
 
 def skip_kernel(
-    flag_ref, inner_ref, outer_ref, inner_before, outer_before, inner_after, outer_after, relayed,
-    weight_ref, skip_ref, previous_ref, next_ref,
+    flag_ref, first_ref, outer_ref, middle_ref, relayed_ref, weight_ref,
+    skip_ref, inside_ref, across_ref,
 ):
     rows, _, wide = skip_ref.shape
     lanes = wide // 2
+    odd_band, odd_frame = flag_ref[2] != 0, flag_ref[3] != 0
+    skips = []
+    for row in range(rows):
+        centre, middle = first_ref[row], middle_ref[row]
+        outer = jnp.where(flag_ref[4] != 0, relayed_ref[row], outer_ref[row])
+        before = jnp.where(odd_frame, outer, middle)
+        after = jnp.where(odd_frame, middle, outer)
+        stacked = jnp.concatenate([before, centre, after], axis=0)
+        skip = (centre.astype(F32) + dot(weight_ref[...], stacked)).astype(BF16)
+        skip_ref[row] = skip
+        skips.append(skip)
+    inside_ref[0] = jnp.where(odd_band, skips[0], skips[-1])
+    across_ref[0] = jnp.where(odd_band, skips[-1], skips[0])
     for pooled_row in range(rows // 2):
-        sums = None
-        for row in (2 * pooled_row, 2 * pooled_row + 1):
-            edge = row in (0, rows - 1)
-            at = (0 if row == 0 else 1) if edge else row - 1
-            before, own, after = (
-                (outer_before, outer_ref, outer_after)
-                if edge
-                else (inner_before, inner_ref, inner_after)
-            )
-            centre, early, late = own[at], before[at], after[at]
-            if not edge:
-                early = jnp.where(flag_ref[2] != 0, relayed[at], early)
-                late = jnp.where(flag_ref[3] != 0, relayed[at], late)
-            stacked = jnp.concatenate([early, centre, late], axis=0)
-            skip = (centre.astype(F32) + dot(weight_ref[...], stacked)).astype(BF16)
-            skip_ref[row] = skip
-            if row == 0:
-                previous_ref[0] = skip
-            if row == rows - 1:
-                next_ref[0] = skip
-            skip = skip.astype(F32)
-            sums = skip if sums is None else sums + skip
+        sums = skips[2 * pooled_row].astype(F32) + skips[2 * pooled_row + 1].astype(F32)
         pooled = ((sums[:, :lanes] + sums[:, lanes:]) * 0.25).astype(BF16)
         span = slice(pooled_row * lanes, (pooled_row + 1) * lanes)
-        previous_ref[1, :, span] = pooled
-        next_ref[1, :, span] = pooled
+        inside_ref[1, :, span] = pooled
+        across_ref[1, :, span] = pooled
 
 
 def own_kernel(skip_ref, pair_ref, mid_ref, skip_weight, mixed_ref, middle_ref, field, pooled, *, half):
@@ -213,7 +229,7 @@
 
 
 def last_kernel(
-    flag_ref, mixed_ref, middle_ref, low_ref, high_ref, mid_ref, skip_weight, phase_weight, field_ref,
+    flag_ref, mixed_ref, middle_ref, inside_ref, across_ref, mid_ref, skip_weight, phase_weight, field_ref,
     out_ref, low_field, high_field, cross_field, rims, middle_field,
 ):
     rows, channels, wide = mixed_ref.shape
@@ -222,9 +238,12 @@
     inner = mid_ref.shape[0]
     depth = 3 * channels
 
-    for target, ref, inward in ((low_field, low_ref, 1), (high_field, high_ref, 0)):
+    odd = flag_ref[2] != 0
+    lows = [jnp.where(odd, inside_ref[at], across_ref[at]) for at in range(2)]
+    highs = [jnp.where(odd, across_ref[at], inside_ref[at]) for at in range(2)]
+    for target, pair, inward in ((low_field, lows[1], 1), (high_field, highs[1], 0)):
         for at in range(2):
-            row = ref[1, :, at * lanes : (at + 1) * lanes].astype(F32)
+            row = pair[:, at * lanes : (at + 1) * lanes].astype(F32)
             store_row_taps(target, 0, at * lanes, row, half)
         cross_field[:, (1 - inward) * lanes : (2 - inward) * lanes] = target[
             :, inward * lanes : (inward + 1) * lanes
@@ -245,8 +264,8 @@
             value = jnp.where(keep, value, 0.0)
         store_row_taps(middle_field, at * 3 * inner, 0, value.astype(BF16).astype(F32), half)
 
-    for at, ref in enumerate((low_ref, high_ref)):
-        value = ref[0].astype(F32)
+    for at, row in enumerate((lows[0], highs[0])):
+        value = row.astype(F32)
         store_taps(rims, at * depth, value[:, :lanes], value[:, lanes:], half)
     from_rim = {
         0: dot(skip_weight[:, :depth], rims[:depth, :]),
@@ -288,7 +307,7 @@
                 out_ref[clip, row] = natural[:, clip * width : (clip + 1) * width]
 
 
-def call(kernel, name, outputs, limit, scratch=(), flops=0, kept=True, inputs=None):
+def call(kernel, name, outputs, limit, scratch=(), flops=0, kept=True, inputs=None, aliases=None):
     shapes = [
         pltpu.VMEM(shape, dtype) if kept else jax.ShapeDtypeStruct(shape, dtype)
         for shape, dtype in outputs
@@ -301,6 +320,7 @@
         compiler_params=pltpu.CompilerParams(vmem_limit_bytes=limit * MIB),
         cost_estimate=pl.CostEstimate(flops=flops, bytes_accessed=1 << 20, transcendentals=0),
         name=name,
+        input_output_aliases=aliases or {},
         **specs,
     )
 
@@ -319,27 +339,23 @@
     offset = bands // 2
     band_of = lambda index: (index + offset) % bands
     frame_of = lambda index: (index + offset) // bands % FRAMES
-    chain = lambda step, keep: [
-        (i, (i + step) % device_count) for i in range(device_count) if keep(i)
-    ]
-    band = band_of(lax.axis_index("frames"))
-    down = chain(1, lambda i: band_of(i) != bands - 1)
-    up = chain(-1, lambda i: band_of(i) != 0)
-    later = chain(bands, lambda i: frame_of(i) != FRAMES - 1)
-    earlier = chain(-bands, lambda i: frame_of(i) != 0)
-    near = lambda pairs: [(i, j) for i, j in pairs if abs(i - j) == bands]
-    far = [(i, j) for i, j in later + earlier if abs(i - j) != bands]
-    hops = [(i, i - offset) for i, _ in far]
-    relays = [(i - offset, j) for i, j in far]
+    swap = lambda step, group, lowest: [
+        pair
+        for i in range(device_count)
+        if group(i) % 2 == lowest and group(i) + 1 < (FRAMES if step == bands else bands)
+        for j in [(i + step) % device_count]
+        for pair in ((i, j), (j, i))
+    ]
+    inside, across = swap(1, band_of, 0), swap(1, band_of, 1)
+    outer_frames, middle_frames = swap(bands, frame_of, 0), swap(bands, frame_of, 1)
+    relayed_pairs = [(i, j) for i, j in outer_frames if abs(i - j) != bands and band_of(i) % 2 == 0]
+    hops = [(i, i - offset + 1) for i, _ in relayed_pairs]
+    relays = [(i - offset + 1, j) for i, j in relayed_pairs]
+    outer_frames = [pair for pair in outer_frames if pair not in relayed_pairs]
     index = lax.axis_index("frames")
-    flags = jnp.stack(
-        [
-            band == 0,
-            band == bands - 1,
-            jnp.logical_and(index >= offset, index < bands),
-            index >= device_count - offset,
-        ]
-    ).astype(jnp.int32)
+    band, frame = band_of(index), frame_of(index)
+    is_relayed = jnp.logical_and(jnp.logical_and(frame < 2, band < offset), band % 2 == 0)
+    flags = jnp.stack([band == 0, band == bands - 1, band % 2, frame % 2, is_relayed]).astype(jnp.int32)
 
     clips, rows, width, channels = latents.shape
     inner = mid_weight.shape[3]
@@ -350,52 +366,58 @@
     scalars = pl.BlockSpec(memory_space=pltpu.SMEM)
     turned = jnp.swapaxes(latents, 2, 3)
 
-    first_inner, in_turned, field, low_rim, high_rim = call(
-        first_inner_kernel,
-        "first_inner",
-        [
-            ((rows - 2, channels, wide), BF16),
-            ((channels, 3 * depth), BF16),
-            ((rows * depth, wide), BF16),
-            ((clips, channels, width), BF16),
-            ((clips, channels, width), BF16),
-        ],
-        12,
+    inside_rim, across_rim = call(
+        rims_kernel,
+        "rims",
+        [((clips, channels, width), BF16)] * 2,
+        1,
+        [pltpu.SemaphoreType.DMA((2,))],
+        inputs=[scalars, anywhere],
+    )(flags, in_hbm(turned))
+    inside_row = lax.ppermute(inside_rim, "frames", inside)
+    across_row = lax.ppermute(across_rim, "frames", across)
+    in_turned, field = call(
+        prepare_kernel,
+        "prepare",
+        [((channels, 3 * depth), BF16), ((rows * depth, wide), BF16)],
+        8,
         [
             pltpu.VMEM(turned.shape, BF16),
             pltpu.VMEM((3 * depth, channels), BF16),
             pltpu.SemaphoreType.DMA(()),
             pltpu.SemaphoreType.DMA((-(-3 * depth // 1024),)),
         ],
-        flops=2 * (rows - 2) * wide * channels * 3 * depth,
+        flops=2 * rows * wide * channels * wide,
         inputs=[anywhere, anywhere],
     )(in_hbm(turned), in_hbm(in_weight.reshape(3 * depth, channels)))
-    hopped = lax.ppermute(first_inner, "frames", hops)
-    inner_before = lax.ppermute(first_inner, "frames", near(later))
-    inner_after = lax.ppermute(first_inner, "frames", near(earlier))
-    relayed = lax.ppermute(hopped, "frames", relays)
-    low = lax.ppermute(low_rim, "frames", down)
-    high = lax.ppermute(high_rim, "frames", up)
-
-    (first_outer,) = call(
-        first_outer_kernel,
-        "first_outer",
-        [((2, channels, wide), BF16)],
+    first_own, partial = call(
+        first_own_kernel,
+        "first_own",
+        [((rows, channels, wide), BF16), ((2, channels, wide), F32)],
+        8,
+        flops=2 * wide * channels * depth * (3 * rows - 2),
+        inputs=[whole] * 2,
+    )(*in_vmem(in_turned, field))
+    (first,) = call(
+        first_rest_kernel,
+        "first_rest",
+        [((rows, channels, wide), BF16)],
         8,
         [pltpu.VMEM((2 * depth, wide), BF16)],
-        flops=2 * 2 * wide * channels * 3 * depth,
-        inputs=[whole] * 4,
-    )(*in_vmem(low, high, in_turned, field))
-    outer_before = lax.ppermute(first_outer, "frames", later)
-    outer_after = lax.ppermute(first_outer, "frames", earlier)
-
-    time_rows, mid_rows, up_rows, first_outer, _ = lax.optimization_barrier(
+        flops=2 * 2 * wide * channels * depth,
+        inputs=[scalars] + [whole] * 5,
+        aliases={5: 0},
+    )(flags, *in_vmem(inside_row, across_row, in_turned, partial, first_own))
+    hopped = lax.ppermute(first, "frames", hops)
+    outer = lax.ppermute(first, "frames", outer_frames)
+    middle = lax.ppermute(first, "frames", middle_frames)
+
+    time_rows, mid_rows, up_rows, first = lax.optimization_barrier(
         (
             time_weight.reshape(depth, channels),
             mid_weight.reshape(3 * depth, inner),
             jnp.swapaxes(up_weight, 2, 3),
-            first_outer,
-            hopped,
+            first,
         )
     )
     time_turned, mid_turned, skip_weight, phase_weight = call(
@@ -418,7 +440,9 @@
         inputs=[anywhere] * 3,
     )(in_hbm(time_rows), in_hbm(mid_rows), in_hbm(up_rows))
 
-    skip, to_previous, to_next = call(
+    hopped, time_turned = lax.optimization_barrier((hopped, time_turned))
+    relayed = lax.ppermute(hopped, "frames", relays)
+    skip, inside_rows, across_rows = call(
         skip_kernel,
         "skip",
         [
@@ -428,22 +452,10 @@
         ],
         8,
         flops=2 * rows * wide * depth * channels,
-        inputs=[scalars] + [whole] * 8,
-    )(
-        flags,
-        *in_vmem(
-            first_inner,
-            first_outer,
-            inner_before,
-            outer_before,
-            inner_after,
-            outer_after,
-            relayed,
-            time_turned,
-        ),
-    )
-    from_previous = lax.ppermute(to_next, "frames", down)
-    from_next = lax.ppermute(to_previous, "frames", up)
+        inputs=[scalars] + [whole] * 5,
+    )(flags, *in_vmem(first, outer, middle, relayed, time_turned))
+    from_across = lax.ppermute(across_rows, "frames", across)
+    from_inside = lax.ppermute(inside_rows, "frames", inside)
 
     mixed, middle = call(
         lambda *refs: own_kernel(*refs, half=width // 2),
@@ -453,7 +465,7 @@
         [pltpu.VMEM((rows * depth, wide), BF16), pltpu.VMEM((depth, wide), BF16)],
         flops=2 * wide * depth * (3 * inner + (3 * rows - 2) * channels),
         inputs=[whole] * 4,
-    )(*in_vmem(skip, to_previous, mid_turned, skip_weight))
+    )(*in_vmem(skip, inside_rows, mid_turned, skip_weight))
 
     (out,) = call(
         last_kernel,
@@ -473,7 +485,7 @@
     )(
         flags,
         *in_vmem(
-            mixed, middle, from_previous, from_next, mid_turned, skip_weight, phase_weight, field
+            mixed, middle, from_inside, from_across, mid_turned, skip_weight, phase_weight, field
         ),
     )
     return jnp.swapaxes(out, 2, 3)

time: 61.9 us -> 56.5 us (0.913)
  the two profiles are of different devices: /device:TPU:0 before, /device:TPU:15 now
where the time goes in v3:
time: 56.5 us; the launch traced here: 56.2 us
  Pallas kernels  24.7 us (44%)
  waiting for transfers between devices  19.9 us (35%)
  starting transfers between devices  11.4 us (20%)
    ppermute x1, waiting for transfers between devices, body(): middle = lax.ppermute(first, 'frames', middle_frames)  12 us
    pallas_call x1, Pallas kernels, body(): call(weights_kernel, 'weights', [((channels, depth), BF16), ((inner, 3 *...  6.91 us
    pallas_call x1, Pallas kernels, body(): call(last_kernel, 'last', [(turned.shape, BF16)], 20, [pltpu.VMEM((depth,...  5.48 us
    ppermute x1, waiting for transfers between devices, body(): from_across = lax.ppermute(across_rows, 'frames', across)  4.01 us
    ppermute x1, waiting for transfers between devices, body(): outer = lax.ppermute(first, 'frames', outer_frames)  3.9 us
    pallas_call x1, Pallas kernels, body(): call(lambda *refs: own_kernel(*refs, half=width // 2), 'own_rows', [((row...  3.09 us
    ppermute x1, starting transfers between devices, body(): across_row = lax.ppermute(across_rim, 'frames', across)  3.05 us
    pallas_call x1, Pallas kernels, body(): call(prepare_kernel, 'prepare', [((channels, 3 * depth), BF16), ((rows *...  2.78 us
  transfers between devices with their start and end apart: 8, of which 3 were waited for; matrix products, arithmetic and copies ran while one was open for 0% of the time, Pallas kernels for 26%

profile of v3, /device:TPU:15, one launch (start us, length us, event | category | flops | bytes accessed | tf_op | source)
XLA Modules:
  0.0 56.2 jit_solution(10718353732014551242)
XLA Ops:
  0.0 0.1 stack.35.flag_ref
  0.1 1.6 %rims.1 = (bf16[2,320,128]{2,1,0:T(8,128)(2,1)S(1)}, bf16[2,320,128]{2,1,0:T(8,128)(2,1)S(1)}) custom-call(s32[5]{0:T(128)S(1)} %stack.35.flag_ref, bf16[2,4,320,128]{3,2,1,0:T(8,128)(2,1)} %bitcast.13), custom_call_target="tpu_custom_call" | custom-call | bytes 1048576 | tf_op jit(solution)/shard_map/rims/pallas_call | solution.py:369
  1.6 0.7 %collective-permute-start = (bf16[2,320,128]{2,1,0:T(8,128)(2,1)S(1)}, bf16[2,320,128]{2,1,0:T(8,128)(2,1)S(1)}, u32[]{:S(2)}, u32[]{:S(2)}) collective-permute-start(bf16[2,320,128]{2,1,0:T(8,128)(2,1)S(1)} %get-tuple-element.26), channel_id=1, source_target_pairs={{0,1},{1,0},{2,3},{3,2},{4,5},{5,4},{6,7},{7,6},{8,9},{9,8},{10,11... | collective-permute-start | bytes 491528 | tf_op jit(solution)/shard_map/ppermute | solution.py:377
  2.4 3.0 %collective-permute-start.1 = (bf16[2,320,128]{2,1,0:T(8,128)(2,1)S(1)}, bf16[2,320,128]{2,1,0:T(8,128)(2,1)S(1)}, u32[]{:S(2)}, u32[]{:S(2)}) collective-permute-start(bf16[2,320,128]{2,1,0:T(8,128)(2,1)S(1)} %get-tuple-element.27), channel_id=1, source_target_pairs={{3,4},{4,3},{7,8},{8,7},{11,12},{12,11},{15,0},{0,15},{19,20},{20,... | collective-permute-start | bytes 491528 | tf_op jit(solution)/shard_map/ppermute | solution.py:378
  5.4 2.8 %prepare.1 = (bf16[320,2880]{1,0:T(8,128)(2,1)S(1)}, bf16[3840,256]{1,0:T(8,128)(2,1)S(1)}) custom-call(bf16[2,4,320,128]{3,2,1,0:T(8,128)(2,1)} %bitcast.14, bf16[2880,320]{1,0:T(8,128)(2,1)} %bitcast.15), custom_call_target="tpu_custom_call" | custom-call | flops 167772160 | bytes 1048576 | tf_op jit(solution)/shard_map/prepare/pallas_call | solution.py:379
  8.2 1.9 %first_own.1 = (bf16[4,320,256]{2,1,0:T(8,128)(2,1)S(1)}, f32[2,320,256]{2,1,0:T(8,128)S(1)}) custom-call(bf16[320,2880]{1,0:T(8,128)(2,1)S(1)} %get-tuple-element.28.turned_ref, bf16[3840,256]{1,0:T(8,128)(2,1)S(1)} %get-tuple-element.29.field_ref), custom_call_target="tpu_custom_call" | custom-call | flops 1572864000 | bytes 1048576 | tf_op jit(solution)/shard_map/first_own/pallas_call | solution.py:393
  10.2 0.0 collective-permute-done.inside_ref
  10.2 0.0 collective-permute-done.1.across_ref
  10.2 1.5 %first_rest.1.first_ref = bf16[4,320,256]{2,1,0:T(8,128)(2,1)S(1)} custom-call(s32[5]{0:T(128)S(1)} %stack.35.flag_ref, bf16[2,320,128]{2,1,0:T(8,128)(2,1)S(1)} %collective-permute-done.inside_ref, bf16[2,320,128]{2,1,0:T(8,128)(2,1)S(1)} %collective-permute-done.1.across_ref, ...), custom_call_target="tpu_custom_call", output_to_operand_aliasing={{}: (5, {})} | custom-call | flops 314572800 | bytes 1048576 | tf_op jit(solution)/shard_map/first_rest/pallas_call | solution.py:401
  11.7 0.7 %collective-permute-start.4 = (bf16[4,320,256]{2,1,0:T(8,128)(2,1)S(1)}, bf16[4,320,256]{2,1,0:T(8,128)(2,1)S(1)}, u32[]{:S(2)}, u32[]{:S(2)}) collective-permute-start(bf16[4,320,256]{2,1,0:T(8,128)(2,1)S(1)} %first_rest.1.first_ref), channel_id=1, source_target_pairs={{14,13},{2,1},{30,29},{18,17}} | collective-permute-start | bytes 1966088 | tf_op jit(solution)/shard_map/ppermute | solution.py:411
  12.4 2.1 %collective-permute-start.3 = (bf16[4,320,256]{2,1,0:T(8,128)(2,1)S(1)}, bf16[4,320,256]{2,1,0:T(8,128)(2,1)S(1)}, u32[]{:S(2)}, u32[]{:S(2)}) collective-permute-start(bf16[4,320,256]{2,1,0:T(8,128)(2,1)S(1)} %first_rest.1.first_ref), channel_id=1, source_target_pairs={{2,6},{6,2},{3,7},{7,3},{4,8},{8,4},{5,9},{9,5},{18,22},{22,18},{1... | collective-permute-start | bytes 1966088 | tf_op jit(solution)/shard_map/ppermute | solution.py:413
  14.5 1.9 %collective-permute-start.2 = (bf16[4,320,256]{2,1,0:T(8,128)(2,1)S(1)}, bf16[4,320,256]{2,1,0:T(8,128)(2,1)S(1)}, u32[]{:S(2)}, u32[]{:S(2)}) collective-permute-start(bf16[4,320,256]{2,1,0:T(8,128)(2,1)S(1)} %first_rest.1.first_ref), channel_id=1, source_target_pairs={{0,4},{4,0},{1,5},{5,1},{6,10},{10,6},{7,11},{11,7},{8,12},{12,8},... | collective-permute-start | bytes 1966088 | tf_op jit(solution)/shard_map/ppermute | solution.py:412
  16.4 6.9 %weights.1 = (bf16[320,960]{1,0:T(8,128)(2,1)S(1)}, bf16[640,2880]{1,0:T(8,128)(2,1)S(1)}, bf16[320,2880]{1,0:T(8,128)(2,1)S(1)}, bf16[4,320,2560]{2,1,0:T(8,128)(2,1)S(1)}) custom-call(bf16[960,320]{1,0:T(8,128)(2,1)} %bitcast.16, bf16[2880,640]{1,0:T(8,128)(2,1)} %bitcast.12, bf16[3,3,320,960]{3,2,1,0:T(8,128)(2,1)} %bitcast.11), custom_call_target="tpu_custom_call" | custom-call | flops 2000000000 | bytes 1048576 | tf_op jit(solution)/shard_map/weights/pallas_call | solution.py:423
  23.3 0.0 collective-permute-done.4
  23.3 0.7 %collective-permute-start.5 = (bf16[4,320,256]{2,1,0:T(8,128)(2,1)S(1)}, bf16[4,320,256]{2,1,0:T(8,128)(2,1)S(1)}, u32[]{:S(2)}, u32[]{:S(2)}) collective-permute-start(bf16[4,320,256]{2,1,0:T(8,128)(2,1)S(1)} %collective-permute-done.4), channel_id=1, source_target_pairs={{13,2},{1,14},{29,18},{17,30}} | collective-permute-start | bytes 1966088 | tf_op jit(solution)/shard_map/ppermute | solution.py:444
  24.0 12.0 %collective-permute-done.3.middle_ref = bf16[4,320,256]{2,1,0:T(8,128)(2,1)S(1)} collective-permute-done((bf16[4,320,256]{2,1,0:T(8,128)(2,1)S(1)}, bf16[4,320,256]{2,1,0:T(8,128)(2,1)S(1)}, u32[]{:S(2)}, u32[]{:S(2)}) %collective-permute-start.3) | collective-permute-done | bytes 655392 | tf_op jit(solution)/shard_map/ppermute | solution.py:413
  36.0 3.9 %collective-permute-done.2.outer_ref = bf16[4,320,256]{2,1,0:T(8,128)(2,1)S(1)} collective-permute-done((bf16[4,320,256]{2,1,0:T(8,128)(2,1)S(1)}, bf16[4,320,256]{2,1,0:T(8,128)(2,1)S(1)}, u32[]{:S(2)}, u32[]{:S(2)}) %collective-permute-start.2) | collective-permute-done | bytes 655392 | tf_op jit(solution)/shard_map/ppermute | solution.py:412
  39.9 0.0 collective-permute-done.5.relayed_ref
  39.9 1.5 %skip.1 = (bf16[4,320,256]{2,1,0:T(8,128)(2,1)S(1)}, bf16[2,320,256]{2,1,0:T(8,128)(2,1)S(1)}, bf16[2,320,256]{2,1,0:T(8,128)(2,1)S(1)}) custom-call(s32[5]{0:T(128)S(1)} %stack.35.flag_ref, bf16[4,320,256]{2,1,0:T(8,128)(2,1)S(1)} %first_rest.1.first_ref, bf16[4,320,256]{2,1,0:T(8,128)(2,1)S(1)} %collective-permute-done.2.outer_ref, ...), custom_call_target="tpu_custom_call" | custom-call | flops 629145600 | bytes 1048576 | tf_op jit(solution)/shard_map/skip/pallas_call | solution.py:445
  41.5 2.1 %collective-permute-start.7 = (bf16[2,320,256]{2,1,0:T(8,128)(2,1)S(1)}, bf16[2,320,256]{2,1,0:T(8,128)(2,1)S(1)}, u32[]{:S(2)}, u32[]{:S(2)}) collective-permute-start(bf16[2,320,256]{2,1,0:T(8,128)(2,1)S(1)} %get-tuple-element.45), channel_id=1, source_target_pairs={{3,4},{4,3},{7,8},{8,7},{11,12},{12,11},{15,0},{0,15},{19,20},{20,... | collective-permute-start | bytes 983048 | tf_op jit(solution)/shard_map/ppermute | solution.py:457
  43.6 0.1 collective-permute-start.6
  43.7 3.1 %own_rows.1 = (f32[4,320,256]{2,1,0:T(8,128)S(1)}, f32[640,512]{1,0:T(8,128)S(1)}) custom-call(bf16[4,320,256]{2,1,0:T(8,128)(2,1)S(1)} %get-tuple-element.39.refs_0_, bf16[2,320,256]{2,1,0:T(8,128)(2,1)S(1)} %get-tuple-element.40.refs_1_, bf16[640,2880]{1,0:T(8,128)(2,1)S(1)} %get-tuple-element.41.refs_2_.mid_ref, ...), custom_call_target="tpu_custom_call" | custom-call | flops 2516582400 | bytes 1048576 | tf_op jit(solution)/shard_map/own_rows/pallas_call | solution.py:460
  46.7 4.0 %collective-permute-done.7.across_ref = bf16[2,320,256]{2,1,0:T(8,128)(2,1)S(1)} collective-permute-done((bf16[2,320,256]{2,1,0:T(8,128)(2,1)S(1)}, bf16[2,320,256]{2,1,0:T(8,128)(2,1)S(1)}, u32[]{:S(2)}, u32[]{:S(2)}) %collective-permute-start.7) | collective-permute-done | bytes 327712 | tf_op jit(solution)/shard_map/ppermute | solution.py:457
  50.8 0.0 collective-permute-done.6.inside_ref
  50.8 5.5 %last.1 = bf16[2,4,320,128]{3,2,1,0:T(8,128)(2,1)} custom-call(s32[5]{0:T(128)S(1)} %stack.35.flag_ref, f32[4,320,256]{2,1,0:T(8,128)S(1)} %get-tuple-element.43.mixed_ref, f32[640,512]{1,0:T(8,128)S(1)} %get-tuple-element.44.middle_ref, bf16[2,320,256]{2,1,0:T(8,128)(2,1)S(1)} %collective-permute-done.6.inside_ref, ...), custom_call_target="tpu_custom_call" | custom-call | flops 2936012800 | bytes 1048576 | tf_op jit(solution)/shard_map/last/pallas_call | solution.py:470
Async XLA Ops:
  1.6 8.5 %collective-permute-start = (bf16[2,320,128]{2,1,0:T(8,128)(2,1)S(1)}, bf16[2,320,128]{2,1,0:T(8,128)(2,1)S(1)}, u32[]{:S(2)}, u32[]{:S(2)}) collective-permute-start(bf16[2,320,128]{2,1,0:T(8,128)(2,1)S(1)} %get-tuple-element.26), channel_id=1, source_target_pairs={{0,1},{1,0},{2,3},{3,2},{4,5},{5,4},{6,7},{7,6},{8,9},{9,8},{10,11... | collective-permute-start | bytes 491528 | tf_op jit(solution)/shard_map/ppermute | solution.py:377
  2.4 7.8 %collective-permute-start.1 = (bf16[2,320,128]{2,1,0:T(8,128)(2,1)S(1)}, bf16[2,320,128]{2,1,0:T(8,128)(2,1)S(1)}, u32[]{:S(2)}, u32[]{:S(2)}) collective-permute-start(bf16[2,320,128]{2,1,0:T(8,128)(2,1)S(1)} %get-tuple-element.27), channel_id=1, source_target_pairs={{3,4},{4,3},{7,8},{8,7},{11,12},{12,11},{15,0},{0,15},{19,20},{20,... | collective-permute-start | bytes 491528 | tf_op jit(solution)/shard_map/ppermute | solution.py:378
  11.7 11.6 %collective-permute-start.4 = (bf16[4,320,256]{2,1,0:T(8,128)(2,1)S(1)}, bf16[4,320,256]{2,1,0:T(8,128)(2,1)S(1)}, u32[]{:S(2)}, u32[]{:S(2)}) collective-permute-start(bf16[4,320,256]{2,1,0:T(8,128)(2,1)S(1)} %first_rest.1.first_ref), channel_id=1, source_target_pairs={{14,13},{2,1},{30,29},{18,17}} | collective-permute-start | bytes 1966088 | tf_op jit(solution)/shard_map/ppermute | solution.py:411
  12.4 23.6 %collective-permute-start.3 = (bf16[4,320,256]{2,1,0:T(8,128)(2,1)S(1)}, bf16[4,320,256]{2,1,0:T(8,128)(2,1)S(1)}, u32[]{:S(2)}, u32[]{:S(2)}) collective-permute-start(bf16[4,320,256]{2,1,0:T(8,128)(2,1)S(1)} %first_rest.1.first_ref), channel_id=1, source_target_pairs={{2,6},{6,2},{3,7},{7,3},{4,8},{8,4},{5,9},{9,5},{18,22},{22,18},{1... | collective-permute-start | bytes 1966088 | tf_op jit(solution)/shard_map/ppermute | solution.py:413
  14.5 25.4 %collective-permute-start.2 = (bf16[4,320,256]{2,1,0:T(8,128)(2,1)S(1)}, bf16[4,320,256]{2,1,0:T(8,128)(2,1)S(1)}, u32[]{:S(2)}, u32[]{:S(2)}) collective-permute-start(bf16[4,320,256]{2,1,0:T(8,128)(2,1)S(1)} %first_rest.1.first_ref), channel_id=1, source_target_pairs={{0,4},{4,0},{1,5},{5,1},{6,10},{10,6},{7,11},{11,7},{8,12},{12,8},... | collective-permute-start | bytes 1966088 | tf_op jit(solution)/shard_map/ppermute | solution.py:412
  23.3 16.6 %collective-permute-start.5 = (bf16[4,320,256]{2,1,0:T(8,128)(2,1)S(1)}, bf16[4,320,256]{2,1,0:T(8,128)(2,1)S(1)}, u32[]{:S(2)}, u32[]{:S(2)}) collective-permute-start(bf16[4,320,256]{2,1,0:T(8,128)(2,1)S(1)} %collective-permute-done.4), channel_id=1, source_target_pairs={{13,2},{1,14},{29,18},{17,30}} | collective-permute-start | bytes 1966088 | tf_op jit(solution)/shard_map/ppermute | solution.py:444
  41.5 9.3 %collective-permute-start.7 = (bf16[2,320,256]{2,1,0:T(8,128)(2,1)S(1)}, bf16[2,320,256]{2,1,0:T(8,128)(2,1)S(1)}, u32[]{:S(2)}, u32[]{:S(2)}) collective-permute-start(bf16[2,320,256]{2,1,0:T(8,128)(2,1)S(1)} %get-tuple-element.45), channel_id=1, source_target_pairs={{3,4},{4,3},{7,8},{8,7},{11,12},{12,11},{15,0},{0,15},{19,20},{20,... | collective-permute-start | bytes 983048 | tf_op jit(solution)/shard_map/ppermute | solution.py:457
  43.6 7.2 %collective-permute-start.6 = (bf16[2,320,256]{2,1,0:T(8,128)(2,1)S(1)}, bf16[2,320,256]{2,1,0:T(8,128)(2,1)S(1)}, u32[]{:S(2)}, u32[]{:S(2)}) collective-permute-start(bf16[2,320,256]{2,1,0:T(8,128)(2,1)S(1)} %get-tuple-element.40.refs_1_), channel_id=1, source_target_pairs={{0,1},{1,0},{2,3},{3,2},{4,5},{5,4},{6,7},{7,6},{8,9},{9,8},{10,11... | collective-permute-start | bytes 983048 | tf_op jit(solution)/shard_map/ppermute | solution.py:458

commit v4 on v3

--- a/solution.py
+++ b/solution.py
@@ -64,12 +64,20 @@
         field[base + tap * channels : base + (tap + 1) * channels, lane_base : lane_base + lanes] = block
 
 
-def rims_kernel(flag_ref, latent_hbm, inside_ref, across_ref, sems):
+def fetch_kernel(
+    flag_ref, latent_hbm, weight_hbm, inside_ref, across_ref, latent_ref, weight_ref, sems
+):
     last = latent_hbm.shape[1] - 1
     odd = flag_ref[2]
+    pieces = [
+        (latent_hbm.at[:, last * odd], across_ref),
+        (latent_hbm.at[:, last * (1 - odd)], inside_ref),
+        (latent_hbm, latent_ref),
+        (weight_hbm, weight_ref),
+    ]
     gets = [
-        pltpu.make_async_copy(latent_hbm.at[:, row], ref, sems.at[at])
-        for at, (row, ref) in enumerate(((last * (1 - odd), inside_ref), (last * odd, across_ref)))
+        pltpu.make_async_copy(source, target, sems.at[n])
+        for n, (source, target) in enumerate(pieces)
     ]
     for get in gets:
         get.start()
@@ -77,51 +85,17 @@
         get.wait()
 
 
-def prepare_kernel(
-    latent_hbm, weight_hbm, turned_ref, field_ref, latent, weight, latent_sem, weight_sem
-):
-    clips, rows, channels, width = latent.shape
-    taps = weight.shape[0]
-    get_latent = pltpu.make_async_copy(latent_hbm, latent, latent_sem)
-    get_latent.start()
-    cuts = list(range(0, taps, 1024)) + [taps]
-    gets = [
-        pltpu.make_async_copy(weight_hbm.at[a:b], weight.at[a:b], weight_sem.at[n])
-        for n, (a, b) in enumerate(zip(cuts, cuts[1:]))
-    ]
-    for get in gets:
-        get.start()
+def prepare_kernel(latent_ref, weight_ref, turned_ref, field_ref):
+    clips, rows, channels, width = latent_ref.shape
     pick = sort_pick(width, clips)
-    get_latent.wait()
     for row in range(rows):
-        value = dot(jnp.concatenate([latent[clip, row] for clip in range(clips)], axis=1), pick)
+        value = dot(jnp.concatenate([latent_ref[clip, row] for clip in range(clips)], axis=1), pick)
         lanes = value.shape[1] // 2
         store_taps(field_ref, row * 3 * channels, value[:, :lanes], value[:, lanes:], width // 2)
-    for get, a, b in zip(gets, cuts, cuts[1:]):
-        get.wait()
-        turned_ref[:, a:b] = weight[a:b, :].T
-
-
-def first_own_kernel(turned_ref, field_ref, first_ref, partial_ref):
-    rows, channels, _ = first_ref.shape
-    depth = 3 * channels
-    for row in range(rows):
-        start, stop = max(row - 1, 0), min(row + 2, rows)
-        total = dot(
-            turned_ref[:, (start - row + 1) * depth : (stop - row + 1) * depth],
-            field_ref[start * depth : stop * depth, :],
-        )
-        if row == 0:
-            partial_ref[0] = total
-        elif row == rows - 1:
-            partial_ref[1] = total
-        else:
-            first_ref[row] = silu(total).astype(BF16)
-
-
-def first_rest_kernel(
-    flag_ref, inside_ref, across_ref, turned_ref, partial_ref, own_ref, first_ref, rim
-):
+    turned_ref[...] = weight_ref[...].T
+
+
+def first_kernel(flag_ref, inside_ref, across_ref, turned_ref, field_ref, first_ref, rim):
     clips, channels, width = inside_ref.shape
     depth = 3 * channels
     rows = first_ref.shape[0]
@@ -133,10 +107,17 @@
         value = dot(jnp.concatenate(blocks, axis=1), pick)
         lanes = value.shape[1] // 2
         store_taps(rim, at * depth, value[:, :lanes], value[:, lanes:], width // 2)
-    top = partial_ref[0] + dot(turned_ref[:, :depth], rim[:depth, :])
-    first_ref[0] = silu(top).astype(BF16)
-    bottom = partial_ref[1] + dot(turned_ref[:, 2 * depth :], rim[depth:, :])
-    first_ref[rows - 1] = silu(bottom).astype(BF16)
+    for row in list(range(1, rows - 1)) + [0, rows - 1]:
+        start, stop = max(row - 1, 0), min(row + 2, rows)
+        total = dot(
+            turned_ref[:, (start - row + 1) * depth : (stop - row + 1) * depth],
+            field_ref[start * depth : stop * depth, :],
+        )
+        if row == 0:
+            total += dot(turned_ref[:, :depth], rim[:depth, :])
+        if row == rows - 1:
+            total += dot(turned_ref[:, 2 * depth :], rim[depth:, :])
+        first_ref[row] = silu(total).astype(BF16)
 
 
 def weights_kernel(
@@ -366,14 +347,19 @@
     scalars = pl.BlockSpec(memory_space=pltpu.SMEM)
     turned = jnp.swapaxes(latents, 2, 3)
 
-    inside_rim, across_rim = call(
-        rims_kernel,
-        "rims",
-        [((clips, channels, width), BF16)] * 2,
+    inside_rim, across_rim, latent, in_rows = call(
+        fetch_kernel,
+        "fetch",
+        [
+            ((clips, channels, width), BF16),
+            ((clips, channels, width), BF16),
+            (turned.shape, BF16),
+            ((3 * depth, channels), BF16),
+        ],
         1,
-        [pltpu.SemaphoreType.DMA((2,))],
-        inputs=[scalars, anywhere],
-    )(flags, in_hbm(turned))
+        [pltpu.SemaphoreType.DMA((4,))],
+        inputs=[scalars, anywhere, anywhere],
+    )(flags, in_hbm(turned), in_hbm(in_weight.reshape(3 * depth, channels)))
     inside_row = lax.ppermute(inside_rim, "frames", inside)
     across_row = lax.ppermute(across_rim, "frames", across)
     in_turned, field = call(
@@ -381,33 +367,18 @@
         "prepare",
         [((channels, 3 * depth), BF16), ((rows * depth, wide), BF16)],
         8,
-        [
-            pltpu.VMEM(turned.shape, BF16),
-            pltpu.VMEM((3 * depth, channels), BF16),
-            pltpu.SemaphoreType.DMA(()),
-            pltpu.SemaphoreType.DMA((-(-3 * depth // 1024),)),
-        ],
         flops=2 * rows * wide * channels * wide,
-        inputs=[anywhere, anywhere],
-    )(in_hbm(turned), in_hbm(in_weight.reshape(3 * depth, channels)))
-    first_own, partial = call(
-        first_own_kernel,
-        "first_own",
-        [((rows, channels, wide), BF16), ((2, channels, wide), F32)],
-        8,
-        flops=2 * wide * channels * depth * (3 * rows - 2),
         inputs=[whole] * 2,
-    )(*in_vmem(in_turned, field))
+    )(*in_vmem(latent, in_rows))
     (first,) = call(
-        first_rest_kernel,
-        "first_rest",
+        first_kernel,
+        "first",
         [((rows, channels, wide), BF16)],
         8,
         [pltpu.VMEM((2 * depth, wide), BF16)],
-        flops=2 * 2 * wide * channels * depth,
-        inputs=[scalars] + [whole] * 5,
-        aliases={5: 0},
-    )(flags, *in_vmem(inside_row, across_row, in_turned, partial, first_own))
+        flops=2 * rows * wide * channels * 3 * depth,
+        inputs=[scalars] + [whole] * 4,
+    )(flags, *in_vmem(inside_row, across_row, in_turned, field))
     hopped = lax.ppermute(first, "frames", hops)
     outer = lax.ppermute(first, "frames", outer_frames)
     middle = lax.ppermute(first, "frames", middle_frames)

time: 56.5 us -> 55.4 us (0.981)
  Pallas kernels: 24.7 us -> 23.5 us
    ppermute x1, waiting for transfers between devices: 12 us -> 8.42 us  [body(): middle = lax.ppermute(first, 'frames', middle_frames)]
    ppermute x1, waiting for transfers between devices: 0.01 us -> 3.52 us  [body(): across_row = lax.ppermute(across_rim, 'frames', across)]
    pallas_call x1, Pallas kernels: 2.78 us -> 0.94 us  [body(): call(prepare_kernel, 'prepare', [((channels, 3 * depth), BF16), ((rows *...]
    pallas_call x3 -> x2, Pallas kernels: 4.95 us -> 5.59 us  [the longest x1 3.01 us: body(): call(first_kernel, 'first', [((rows, channels, wide), BF16)], 8, [pltpu.V...]
  transfers between devices with their start and end apart: 8 -> 8, of which waited for: 3 -> 4; matrix products, arithmetic and copies ran while one was open for 0% -> 0% of each run, Pallas kernels for 26% -> 20%
where the time goes in v4:
time: 55.4 us; the launch traced here: 55.1 us
  Pallas kernels  23.5 us (42%)
  waiting for transfers between devices  20.1 us (36%)
  starting transfers between devices  11.4 us (21%)
    ppermute x1, waiting for transfers between devices, body(): middle = lax.ppermute(first, 'frames', middle_frames)  8.42 us
    pallas_call x1, Pallas kernels, body(): call(weights_kernel, 'weights', [((channels, depth), BF16), ((inner, 3 *...  6.91 us
    pallas_call x1, Pallas kernels, body(): call(last_kernel, 'last', [(turned.shape, BF16)], 20, [pltpu.VMEM((depth,...  5.47 us
    ppermute x1, waiting for transfers between devices, body(): outer = lax.ppermute(first, 'frames', outer_frames)  4.1 us
    ppermute x1, waiting for transfers between devices, body(): from_across = lax.ppermute(across_rows, 'frames', across)  4.01 us
    ppermute x1, waiting for transfers between devices, body(): across_row = lax.ppermute(across_rim, 'frames', across)  3.52 us
    pallas_call x1, Pallas kernels, body(): call(lambda *refs: own_kernel(*refs, half=width // 2), 'own_rows', [((row...  3.09 us
    ppermute x1, starting transfers between devices, body(): across_row = lax.ppermute(across_rim, 'frames', across)  3.05 us
  transfers between devices with their start and end apart: 8, of which 4 were waited for; matrix products, arithmetic and copies ran while one was open for 0% of the time, Pallas kernels for 20%

profile of v4, /device:TPU:15, one launch (start us, length us, event | category | flops | bytes accessed | tf_op | source)
XLA Modules:
  0.0 55.1 jit_solution(7759517650516534579)
XLA Ops:
  0.0 0.1 stack.35.flag_ref
  0.1 2.6 %fetch.1 = (bf16[2,320,128]{2,1,0:T(8,128)(2,1)S(1)}, bf16[2,320,128]{2,1,0:T(8,128)(2,1)S(1)}, bf16[2,4,320,128]{3,2,1,0:T(8,128)(2,1)S(1)}, bf16[2880,320]{1,0:T(8,128)(2,1)S(1)}) custom-call(s32[5]{0:T(128)S(1)} %stack.35.flag_ref, bf16[2,4,320,128]{3,2,1,0:T(8,128)(2,1)} %bitcast.15, bf16[2880,320]{1,0:T(8,128)(2,1)} %bitcast.13), custom_call_target="tpu_custom_call" | custom-call | bytes 1048576 | tf_op jit(solution)/shard_map/fetch/pallas_call | solution.py:350
  2.7 0.7 %collective-permute-start = (bf16[2,320,128]{2,1,0:T(8,128)(2,1)S(1)}, bf16[2,320,128]{2,1,0:T(8,128)(2,1)S(1)}, u32[]{:S(2)}, u32[]{:S(2)}) collective-permute-start(bf16[2,320,128]{2,1,0:T(8,128)(2,1)S(1)} %get-tuple-element.26), channel_id=1, source_target_pairs={{0,1},{1,0},{2,3},{3,2},{4,5},{5,4},{6,7},{7,6},{8,9},{9,8},{10,11... | collective-permute-start | bytes 491528 | tf_op jit(solution)/shard_map/ppermute | solution.py:363
  3.4 3.0 %collective-permute-start.1 = (bf16[2,320,128]{2,1,0:T(8,128)(2,1)S(1)}, bf16[2,320,128]{2,1,0:T(8,128)(2,1)S(1)}, u32[]{:S(2)}, u32[]{:S(2)}) collective-permute-start(bf16[2,320,128]{2,1,0:T(8,128)(2,1)S(1)} %get-tuple-element.27), channel_id=1, source_target_pairs={{3,4},{4,3},{7,8},{8,7},{11,12},{12,11},{15,0},{0,15},{19,20},{20,... | collective-permute-start | bytes 491528 | tf_op jit(solution)/shard_map/ppermute | solution.py:364
  6.5 0.9 %prepare.1 = (bf16[320,2880]{1,0:T(8,128)(2,1)S(1)}, bf16[3840,256]{1,0:T(8,128)(2,1)S(1)}) custom-call(bf16[2,4,320,128]{3,2,1,0:T(8,128)(2,1)S(1)} %get-tuple-element.28.latent_ref, bf16[2880,320]{1,0:T(8,128)(2,1)S(1)} %get-tuple-element.29.weight_ref), custom_call_target="tpu_custom_call" | custom-call | flops 167772160 | bytes 1048576 | tf_op jit(solution)/shard_map/prepare/pallas_call | solution.py:365
  7.4 0.0 collective-permute-done.inside_ref
  7.4 3.5 %collective-permute-done.1.across_ref = bf16[2,320,128]{2,1,0:T(8,128)(2,1)S(1)} collective-permute-done((bf16[2,320,128]{2,1,0:T(8,128)(2,1)S(1)}, bf16[2,320,128]{2,1,0:T(8,128)(2,1)S(1)}, u32[]{:S(2)}, u32[]{:S(2)}) %collective-permute-start.1) | collective-permute-done | bytes 163872 | tf_op jit(solution)/shard_map/ppermute | solution.py:364
  10.9 3.0 %first.1.first_ref = bf16[4,320,256]{2,1,0:T(8,128)(2,1)S(1)} custom-call(s32[5]{0:T(128)S(1)} %stack.35.flag_ref, bf16[2,320,128]{2,1,0:T(8,128)(2,1)S(1)} %collective-permute-done.inside_ref, bf16[2,320,128]{2,1,0:T(8,128)(2,1)S(1)} %collective-permute-done.1.across_ref, bf16[320,2880]{1,0:T(8,128)(2,1)S(1)} %get-tuple-element.30.turned_ref, ...), custom_call_target="tpu_custom_call" | custom-call | flops 1887436800 | bytes 1048576 | tf_op jit(solution)/shard_map/first/pallas_call | solution.py:373
  14.0 0.7 %collective-permute-start.4 = (bf16[4,320,256]{2,1,0:T(8,128)(2,1)S(1)}, bf16[4,320,256]{2,1,0:T(8,128)(2,1)S(1)}, u32[]{:S(2)}, u32[]{:S(2)}) collective-permute-start(bf16[4,320,256]{2,1,0:T(8,128)(2,1)S(1)} %first.1.first_ref), channel_id=1, source_target_pairs={{14,13},{2,1},{30,29},{18,17}} | collective-permute-start | bytes 1966088 | tf_op jit(solution)/shard_map/ppermute | solution.py:382
  14.7 2.1 %collective-permute-start.3 = (bf16[4,320,256]{2,1,0:T(8,128)(2,1)S(1)}, bf16[4,320,256]{2,1,0:T(8,128)(2,1)S(1)}, u32[]{:S(2)}, u32[]{:S(2)}) collective-permute-start(bf16[4,320,256]{2,1,0:T(8,128)(2,1)S(1)} %first.1.first_ref), channel_id=1, source_target_pairs={{2,6},{6,2},{3,7},{7,3},{4,8},{8,4},{5,9},{9,5},{18,22},{22,18},{1... | collective-permute-start | bytes 1966088 | tf_op jit(solution)/shard_map/ppermute | solution.py:384
  16.8 1.9 %collective-permute-start.2 = (bf16[4,320,256]{2,1,0:T(8,128)(2,1)S(1)}, bf16[4,320,256]{2,1,0:T(8,128)(2,1)S(1)}, u32[]{:S(2)}, u32[]{:S(2)}) collective-permute-start(bf16[4,320,256]{2,1,0:T(8,128)(2,1)S(1)} %first.1.first_ref), channel_id=1, source_target_pairs={{0,4},{4,0},{1,5},{5,1},{6,10},{10,6},{7,11},{11,7},{8,12},{12,8},... | collective-permute-start | bytes 1966088 | tf_op jit(solution)/shard_map/ppermute | solution.py:383
  18.7 6.9 %weights.1 = (bf16[320,960]{1,0:T(8,128)(2,1)S(1)}, bf16[640,2880]{1,0:T(8,128)(2,1)S(1)}, bf16[320,2880]{1,0:T(8,128)(2,1)S(1)}, bf16[4,320,2560]{2,1,0:T(8,128)(2,1)S(1)}) custom-call(bf16[960,320]{1,0:T(8,128)(2,1)} %bitcast.14, bf16[2880,640]{1,0:T(8,128)(2,1)} %bitcast.12, bf16[3,3,320,960]{3,2,1,0:T(8,128)(2,1)} %bitcast.11), custom_call_target="tpu_custom_call" | custom-call | flops 2000000000 | bytes 1048576 | tf_op jit(solution)/shard_map/weights/pallas_call | solution.py:394
  25.6 0.0 collective-permute-done.4
  25.6 0.7 %collective-permute-start.5 = (bf16[4,320,256]{2,1,0:T(8,128)(2,1)S(1)}, bf16[4,320,256]{2,1,0:T(8,128)(2,1)S(1)}, u32[]{:S(2)}, u32[]{:S(2)}) collective-permute-start(bf16[4,320,256]{2,1,0:T(8,128)(2,1)S(1)} %collective-permute-done.4), channel_id=1, source_target_pairs={{13,2},{1,14},{29,18},{17,30}} | collective-permute-start | bytes 1966088 | tf_op jit(solution)/shard_map/ppermute | solution.py:415
  26.3 8.4 %collective-permute-done.3.middle_ref = bf16[4,320,256]{2,1,0:T(8,128)(2,1)S(1)} collective-permute-done((bf16[4,320,256]{2,1,0:T(8,128)(2,1)S(1)}, bf16[4,320,256]{2,1,0:T(8,128)(2,1)S(1)}, u32[]{:S(2)}, u32[]{:S(2)}) %collective-permute-start.3) | collective-permute-done | bytes 655392 | tf_op jit(solution)/shard_map/ppermute | solution.py:384
  34.7 4.1 %collective-permute-done.2.outer_ref = bf16[4,320,256]{2,1,0:T(8,128)(2,1)S(1)} collective-permute-done((bf16[4,320,256]{2,1,0:T(8,128)(2,1)S(1)}, bf16[4,320,256]{2,1,0:T(8,128)(2,1)S(1)}, u32[]{:S(2)}, u32[]{:S(2)}) %collective-permute-start.2) | collective-permute-done | bytes 655392 | tf_op jit(solution)/shard_map/ppermute | solution.py:383
  38.8 0.0 collective-permute-done.5.relayed_ref
  38.8 1.5 %skip.1 = (bf16[4,320,256]{2,1,0:T(8,128)(2,1)S(1)}, bf16[2,320,256]{2,1,0:T(8,128)(2,1)S(1)}, bf16[2,320,256]{2,1,0:T(8,128)(2,1)S(1)}) custom-call(s32[5]{0:T(128)S(1)} %stack.35.flag_ref, bf16[4,320,256]{2,1,0:T(8,128)(2,1)S(1)} %first.1.first_ref, bf16[4,320,256]{2,1,0:T(8,128)(2,1)S(1)} %collective-permute-done.2.outer_ref, ...), custom_call_target="tpu_custom_call" | custom-call | flops 629145600 | bytes 1048576 | tf_op jit(solution)/shard_map/skip/pallas_call | solution.py:416
  40.4 2.1 %collective-permute-start.7 = (bf16[2,320,256]{2,1,0:T(8,128)(2,1)S(1)}, bf16[2,320,256]{2,1,0:T(8,128)(2,1)S(1)}, u32[]{:S(2)}, u32[]{:S(2)}) collective-permute-start(bf16[2,320,256]{2,1,0:T(8,128)(2,1)S(1)} %get-tuple-element.45), channel_id=1, source_target_pairs={{3,4},{4,3},{7,8},{8,7},{11,12},{12,11},{15,0},{0,15},{19,20},{20,... | collective-permute-start | bytes 983048 | tf_op jit(solution)/shard_map/ppermute | solution.py:428
  42.5 0.1 collective-permute-start.6
  42.5 3.1 %own_rows.1 = (f32[4,320,256]{2,1,0:T(8,128)S(1)}, f32[640,512]{1,0:T(8,128)S(1)}) custom-call(bf16[4,320,256]{2,1,0:T(8,128)(2,1)S(1)} %get-tuple-element.39.refs_0_, bf16[2,320,256]{2,1,0:T(8,128)(2,1)S(1)} %get-tuple-element.40.refs_1_, bf16[640,2880]{1,0:T(8,128)(2,1)S(1)} %get-tuple-element.41.refs_2_.mid_ref, ...), custom_call_target="tpu_custom_call" | custom-call | flops 2516582400 | bytes 1048576 | tf_op jit(solution)/shard_map/own_rows/pallas_call | solution.py:431
  45.6 4.0 %collective-permute-done.7.across_ref = bf16[2,320,256]{2,1,0:T(8,128)(2,1)S(1)} collective-permute-done((bf16[2,320,256]{2,1,0:T(8,128)(2,1)S(1)}, bf16[2,320,256]{2,1,0:T(8,128)(2,1)S(1)}, u32[]{:S(2)}, u32[]{:S(2)}) %collective-permute-start.7) | collective-permute-done | bytes 327712 | tf_op jit(solution)/shard_map/ppermute | solution.py:428
  49.6 0.0 collective-permute-done.6.inside_ref
  49.6 5.5 %last.1 = bf16[2,4,320,128]{3,2,1,0:T(8,128)(2,1)} custom-call(s32[5]{0:T(128)S(1)} %stack.35.flag_ref, f32[4,320,256]{2,1,0:T(8,128)S(1)} %get-tuple-element.43.mixed_ref, f32[640,512]{1,0:T(8,128)S(1)} %get-tuple-element.44.middle_ref, bf16[2,320,256]{2,1,0:T(8,128)(2,1)S(1)} %collective-permute-done.6.inside_ref, ...), custom_call_target="tpu_custom_call" | custom-call | flops 2936012800 | bytes 1048576 | tf_op jit(solution)/shard_map/last/pallas_call | solution.py:441
Async XLA Ops:
  2.7 4.7 %collective-permute-start = (bf16[2,320,128]{2,1,0:T(8,128)(2,1)S(1)}, bf16[2,320,128]{2,1,0:T(8,128)(2,1)S(1)}, u32[]{:S(2)}, u32[]{:S(2)}) collective-permute-start(bf16[2,320,128]{2,1,0:T(8,128)(2,1)S(1)} %get-tuple-element.26), channel_id=1, source_target_pairs={{0,1},{1,0},{2,3},{3,2},{4,5},{5,4},{6,7},{7,6},{8,9},{9,8},{10,11... | collective-permute-start | bytes 491528 | tf_op jit(solution)/shard_map/ppermute | solution.py:363
  3.4 7.5 %collective-permute-start.1 = (bf16[2,320,128]{2,1,0:T(8,128)(2,1)S(1)}, bf16[2,320,128]{2,1,0:T(8,128)(2,1)S(1)}, u32[]{:S(2)}, u32[]{:S(2)}) collective-permute-start(bf16[2,320,128]{2,1,0:T(8,128)(2,1)S(1)} %get-tuple-element.27), channel_id=1, source_target_pairs={{3,4},{4,3},{7,8},{8,7},{11,12},{12,11},{15,0},{0,15},{19,20},{20,... | collective-permute-start | bytes 491528 | tf_op jit(solution)/shard_map/ppermute | solution.py:364
  14.0 11.6 %collective-permute-start.4 = (bf16[4,320,256]{2,1,0:T(8,128)(2,1)S(1)}, bf16[4,320,256]{2,1,0:T(8,128)(2,1)S(1)}, u32[]{:S(2)}, u32[]{:S(2)}) collective-permute-start(bf16[4,320,256]{2,1,0:T(8,128)(2,1)S(1)} %first.1.first_ref), channel_id=1, source_target_pairs={{14,13},{2,1},{30,29},{18,17}} | collective-permute-start | bytes 1966088 | tf_op jit(solution)/shard_map/ppermute | solution.py:382
  14.7 20.1 %collective-permute-start.3 = (bf16[4,320,256]{2,1,0:T(8,128)(2,1)S(1)}, bf16[4,320,256]{2,1,0:T(8,128)(2,1)S(1)}, u32[]{:S(2)}, u32[]{:S(2)}) collective-permute-start(bf16[4,320,256]{2,1,0:T(8,128)(2,1)S(1)} %first.1.first_ref), channel_id=1, source_target_pairs={{2,6},{6,2},{3,7},{7,3},{4,8},{8,4},{5,9},{9,5},{18,22},{22,18},{1... | collective-permute-start | bytes 1966088 | tf_op jit(solution)/shard_map/ppermute | solution.py:384
  16.8 22.1 %collective-permute-start.2 = (bf16[4,320,256]{2,1,0:T(8,128)(2,1)S(1)}, bf16[4,320,256]{2,1,0:T(8,128)(2,1)S(1)}, u32[]{:S(2)}, u32[]{:S(2)}) collective-permute-start(bf16[4,320,256]{2,1,0:T(8,128)(2,1)S(1)} %first.1.first_ref), channel_id=1, source_target_pairs={{0,4},{4,0},{1,5},{5,1},{6,10},{10,6},{7,11},{11,7},{8,12},{12,8},... | collective-permute-start | bytes 1966088 | tf_op jit(solution)/shard_map/ppermute | solution.py:383
  25.6 13.2 %collective-permute-start.5 = (bf16[4,320,256]{2,1,0:T(8,128)(2,1)S(1)}, bf16[4,320,256]{2,1,0:T(8,128)(2,1)S(1)}, u32[]{:S(2)}, u32[]{:S(2)}) collective-permute-start(bf16[4,320,256]{2,1,0:T(8,128)(2,1)S(1)} %collective-permute-done.4), channel_id=1, source_target_pairs={{13,2},{1,14},{29,18},{17,30}} | collective-permute-start | bytes 1966088 | tf_op jit(solution)/shard_map/ppermute | solution.py:415
  40.4 9.3 %collective-permute-start.7 = (bf16[2,320,256]{2,1,0:T(8,128)(2,1)S(1)}, bf16[2,320,256]{2,1,0:T(8,128)(2,1)S(1)}, u32[]{:S(2)}, u32[]{:S(2)}) collective-permute-start(bf16[2,320,256]{2,1,0:T(8,128)(2,1)S(1)} %get-tuple-element.45), channel_id=1, source_target_pairs={{3,4},{4,3},{7,8},{8,7},{11,12},{12,11},{15,0},{0,15},{19,20},{20,... | collective-permute-start | bytes 983048 | tf_op jit(solution)/shard_map/ppermute | solution.py:428
  42.5 7.2 %collective-permute-start.6 = (bf16[2,320,256]{2,1,0:T(8,128)(2,1)S(1)}, bf16[2,320,256]{2,1,0:T(8,128)(2,1)S(1)}, u32[]{:S(2)}, u32[]{:S(2)}) collective-permute-start(bf16[2,320,256]{2,1,0:T(8,128)(2,1)S(1)} %get-tuple-element.40.refs_1_), channel_id=1, source_target_pairs={{0,1},{1,0},{2,3},{3,2},{4,5},{5,4},{6,7},{7,6},{8,9},{9,8},{10,11... | collective-permute-start | bytes 983048 | tf_op jit(solution)/shard_map/ppermute | solution.py:429

commit v5 on v4

--- a/solution.py
+++ b/solution.py
@@ -1,3 +1,5 @@
+import functools
+
 import jax
 import jax.numpy as jnp
 from jax import lax
@@ -10,6 +12,11 @@
 BF16 = jnp.bfloat16
 F32 = jnp.float32
 MIB = 1024 * 1024
+
+
+def place(bands):
+    index = lax.axis_index("frames") + bands // 2
+    return lax.rem(index, bands), lax.rem(lax.div(index, bands), FRAMES)
 
 
 def dot(left, right):
@@ -65,10 +72,10 @@
 
 
 def fetch_kernel(
-    flag_ref, latent_hbm, weight_hbm, inside_ref, across_ref, latent_ref, weight_ref, sems
+    latent_hbm, weight_hbm, inside_ref, across_ref, latent_ref, weight_ref, sems, *, bands
 ):
     last = latent_hbm.shape[1] - 1
-    odd = flag_ref[2]
+    odd = lax.rem(place(bands)[0], 2)
     pieces = [
         (latent_hbm.at[:, last * odd], across_ref),
         (latent_hbm.at[:, last * (1 - odd)], inside_ref),
@@ -95,12 +102,12 @@
     turned_ref[...] = weight_ref[...].T
 
 
-def first_kernel(flag_ref, inside_ref, across_ref, turned_ref, field_ref, first_ref, rim):
+def first_kernel(inside_ref, across_ref, turned_ref, field_ref, first_ref, rim, *, bands):
     clips, channels, width = inside_ref.shape
     depth = 3 * channels
     rows = first_ref.shape[0]
     pick = sort_pick(width, clips)
-    odd = flag_ref[2] != 0
+    odd = lax.rem(place(bands)[0], 2) == 1
     for at in range(2):
         one, other = (inside_ref, across_ref) if at == 0 else (across_ref, inside_ref)
         blocks = [jnp.where(odd, one[clip], other[clip]) for clip in range(clips)]
@@ -160,16 +167,18 @@
 
 
 def skip_kernel(
-    flag_ref, first_ref, outer_ref, middle_ref, relayed_ref, weight_ref,
-    skip_ref, inside_ref, across_ref,
+    first_ref, outer_ref, middle_ref, relayed_ref, weight_ref, skip_ref, inside_ref, across_ref,
+    *, bands
 ):
     rows, _, wide = skip_ref.shape
     lanes = wide // 2
-    odd_band, odd_frame = flag_ref[2] != 0, flag_ref[3] != 0
+    band, frame = place(bands)
+    odd_band, odd_frame = lax.rem(band, 2) == 1, lax.rem(frame, 2) == 1
+    is_relayed = jnp.logical_and(jnp.logical_and(frame < 2, band < bands // 2), lax.rem(band, 2) == 0)
     skips = []
     for row in range(rows):
         centre, middle = first_ref[row], middle_ref[row]
-        outer = jnp.where(flag_ref[4] != 0, relayed_ref[row], outer_ref[row])
+        outer = jnp.where(is_relayed, relayed_ref[row], outer_ref[row])
         before = jnp.where(odd_frame, outer, middle)
         after = jnp.where(odd_frame, middle, outer)
         stacked = jnp.concatenate([before, centre, after], axis=0)
@@ -210,8 +219,8 @@
 
 
 def last_kernel(
-    flag_ref, mixed_ref, middle_ref, inside_ref, across_ref, mid_ref, skip_weight, phase_weight, field_ref,
-    out_ref, low_field, high_field, cross_field, rims, middle_field,
+    mixed_ref, middle_ref, inside_ref, across_ref, mid_ref, skip_weight, phase_weight, field_ref,
+    out_ref, low_field, high_field, cross_field, rims, middle_field, *, bands
 ):
     rows, channels, wide = mixed_ref.shape
     clips, _, _, width = out_ref.shape
@@ -219,7 +228,8 @@
     inner = mid_ref.shape[0]
     depth = 3 * channels
 
-    odd = flag_ref[2] != 0
+    band = place(bands)[0]
+    odd = lax.rem(band, 2) == 1
     lows = [jnp.where(odd, inside_ref[at], across_ref[at]) for at in range(2)]
     highs = [jnp.where(odd, across_ref[at], inside_ref[at]) for at in range(2)]
     for target, pair, inward in ((low_field, lows[1], 1), (high_field, highs[1], 0)):
@@ -238,7 +248,7 @@
         middle_ref[:, 2 * lanes : 3 * lanes] + below[:, :lanes],
         middle_ref[:, 3 * lanes :] + below[:, lanes:] + cross[:, lanes:],
     ]
-    kept = (flag_ref[0] == 0, None, None, flag_ref[1] == 0)
+    kept = (band != 0, None, None, band != bands - 1)
     for at, (value, keep) in enumerate(zip(middles, kept)):
         value = silu(value)
         if keep is not None:
@@ -333,22 +343,16 @@
     hops = [(i, i - offset + 1) for i, _ in relayed_pairs]
     relays = [(i - offset + 1, j) for i, j in relayed_pairs]
     outer_frames = [pair for pair in outer_frames if pair not in relayed_pairs]
-    index = lax.axis_index("frames")
-    band, frame = band_of(index), frame_of(index)
-    is_relayed = jnp.logical_and(jnp.logical_and(frame < 2, band < offset), band % 2 == 0)
-    flags = jnp.stack([band == 0, band == bands - 1, band % 2, frame % 2, is_relayed]).astype(jnp.int32)
-
     clips, rows, width, channels = latents.shape
     inner = mid_weight.shape[3]
     wide = clips * width
     depth = 3 * channels
     anywhere = pl.BlockSpec(memory_space=pl.ANY)
     whole = pl.BlockSpec(memory_space=pltpu.VMEM)
-    scalars = pl.BlockSpec(memory_space=pltpu.SMEM)
     turned = jnp.swapaxes(latents, 2, 3)
 
     inside_rim, across_rim, latent, in_rows = call(
-        fetch_kernel,
+        functools.partial(fetch_kernel, bands=bands),
         "fetch",
         [
             ((clips, channels, width), BF16),
@@ -358,8 +362,8 @@
         ],
         1,
         [pltpu.SemaphoreType.DMA((4,))],
-        inputs=[scalars, anywhere, anywhere],
-    )(flags, in_hbm(turned), in_hbm(in_weight.reshape(3 * depth, channels)))
+        inputs=[anywhere, anywhere],
+    )(in_hbm(turned), in_hbm(in_weight.reshape(3 * depth, channels)))
     inside_row = lax.ppermute(inside_rim, "frames", inside)
     across_row = lax.ppermute(across_rim, "frames", across)
     in_turned, field = call(
@@ -371,14 +375,14 @@
         inputs=[whole] * 2,
     )(*in_vmem(latent, in_rows))
     (first,) = call(
-        first_kernel,
+        functools.partial(first_kernel, bands=bands),
         "first",
         [((rows, channels, wide), BF16)],
         8,
         [pltpu.VMEM((2 * depth, wide), BF16)],
         flops=2 * rows * wide * channels * 3 * depth,
-        inputs=[scalars] + [whole] * 4,
-    )(flags, *in_vmem(inside_row, across_row, in_turned, field))
+        inputs=[whole] * 4,
+    )(*in_vmem(inside_row, across_row, in_turned, field))
     hopped = lax.ppermute(first, "frames", hops)
     outer = lax.ppermute(first, "frames", outer_frames)
     middle = lax.ppermute(first, "frames", middle_frames)
@@ -414,7 +418,7 @@
     hopped, time_turned = lax.optimization_barrier((hopped, time_turned))
     relayed = lax.ppermute(hopped, "frames", relays)
     skip, inside_rows, across_rows = call(
-        skip_kernel,
+        functools.partial(skip_kernel, bands=bands),
         "skip",
         [
             ((rows, channels, wide), BF16),
@@ -423,8 +427,8 @@
         ],
         8,
         flops=2 * rows * wide * depth * channels,
-        inputs=[scalars] + [whole] * 5,
-    )(flags, *in_vmem(first, outer, middle, relayed, time_turned))
+        inputs=[whole] * 5,
+    )(*in_vmem(first, outer, middle, relayed, time_turned))
     from_across = lax.ppermute(across_rows, "frames", across)
     from_inside = lax.ppermute(inside_rows, "frames", inside)
 
@@ -439,7 +443,7 @@
     )(*in_vmem(skip, inside_rows, mid_turned, skip_weight))
 
     (out,) = call(
-        last_kernel,
+        functools.partial(last_kernel, bands=bands),
         "last",
         [(turned.shape, BF16)],
         20,
@@ -452,9 +456,8 @@
         ],
         flops=2 * wide * (3 * depth * inner + 2 * depth * channels + rows * 4 * inner * channels),
         kept=False,
-        inputs=[scalars] + [whole] * 8,
+        inputs=[whole] * 8,
     )(
-        flags,
         *in_vmem(
             mixed, middle, from_inside, from_across, mid_turned, skip_weight, phase_weight, field
         ),

time: 55.4 us -> 52.9 us (0.955)
  Pallas kernels: 23.5 us -> 21.1 us
    pallas_call x4, Pallas kernels: 12.6 us -> 10.2 us  [the longest x1 4.75 us: body(): call(functools.partial(last_kernel, bands=bands), 'last', [(turned.shape,...]
  transfers between devices with their start and end apart: 8 -> 8, of which waited for: 4 -> 4; matrix products, arithmetic and copies ran while one was open for 0% -> 0% of each run, Pallas kernels for 20% -> 21%
where the time goes in v5:
time: 52.9 us; the launch traced here: 52.7 us
  Pallas kernels  21.1 us (40%)
  waiting for transfers between devices  20.1 us (38%)
  starting transfers between devices  11.4 us (22%)
    ppermute x1, waiting for transfers between devices, body(): middle = lax.ppermute(first, 'frames', middle_frames)  8.42 us
    pallas_call x1, Pallas kernels, body(): call(weights_kernel, 'weights', [((channels, depth), BF16), ((inner, 3 *...  6.91 us
    pallas_call x1, Pallas kernels, body(): call(functools.partial(last_kernel, bands=bands), 'last', [(turned.shape,...  4.75 us
    ppermute x1, waiting for transfers between devices, body(): outer = lax.ppermute(first, 'frames', outer_frames)  4.1 us
    ppermute x1, waiting for transfers between devices, body(): from_across = lax.ppermute(across_rows, 'frames', across)  4.08 us
    ppermute x1, waiting for transfers between devices, body(): across_row = lax.ppermute(across_rim, 'frames', across)  3.52 us
    ppermute x1, starting transfers between devices, body(): across_row = lax.ppermute(across_rim, 'frames', across)  3.05 us
    pallas_call x1, Pallas kernels, body(): call(lambda *refs: own_kernel(*refs, half=width // 2), 'own_rows', [((row...  3.02 us
  transfers between devices with their start and end apart: 8, of which 4 were waited for; matrix products, arithmetic and copies ran while one was open for 0% of the time, Pallas kernels for 21%

profile of v5, /device:TPU:15, one launch (start us, length us, event | category | flops | bytes accessed | tf_op | source)
XLA Modules:
  0.0 52.7 jit_solution(4516803582508918541)
XLA Ops:
  0.0 2.0 %fetch.1 = (bf16[2,320,128]{2,1,0:T(8,128)(2,1)S(1)}, bf16[2,320,128]{2,1,0:T(8,128)(2,1)S(1)}, bf16[2,4,320,128]{3,2,1,0:T(8,128)(2,1)S(1)}, bf16[2880,320]{1,0:T(8,128)(2,1)S(1)}) custom-call(bf16[2,4,320,128]{3,2,1,0:T(8,128)(2,1)} %bitcast.10, bf16[2880,320]{1,0:T(8,128)(2,1)} %bitcast.8), custom_call_target="tpu_custom_call" | custom-call | bytes 1048576 | tf_op jit(solution)/shard_map/fetch/pallas_call | solution.py:354
  2.0 0.7 %collective-permute-start = (bf16[2,320,128]{2,1,0:T(8,128)(2,1)S(1)}, bf16[2,320,128]{2,1,0:T(8,128)(2,1)S(1)}, u32[]{:S(2)}, u32[]{:S(2)}) collective-permute-start(bf16[2,320,128]{2,1,0:T(8,128)(2,1)S(1)} %get-tuple-element.26), channel_id=1, source_target_pairs={{0,1},{1,0},{2,3},{3,2},{4,5},{5,4},{6,7},{7,6},{8,9},{9,8},{10,11... | collective-permute-start | bytes 491528 | tf_op jit(solution)/shard_map/ppermute | solution.py:367
  2.8 3.0 %collective-permute-start.1 = (bf16[2,320,128]{2,1,0:T(8,128)(2,1)S(1)}, bf16[2,320,128]{2,1,0:T(8,128)(2,1)S(1)}, u32[]{:S(2)}, u32[]{:S(2)}) collective-permute-start(bf16[2,320,128]{2,1,0:T(8,128)(2,1)S(1)} %get-tuple-element.27), channel_id=1, source_target_pairs={{3,4},{4,3},{7,8},{8,7},{11,12},{12,11},{15,0},{0,15},{19,20},{20,... | collective-permute-start | bytes 491528 | tf_op jit(solution)/shard_map/ppermute | solution.py:368
  5.8 0.9 %prepare.1 = (bf16[320,2880]{1,0:T(8,128)(2,1)S(1)}, bf16[3840,256]{1,0:T(8,128)(2,1)S(1)}) custom-call(bf16[2,4,320,128]{3,2,1,0:T(8,128)(2,1)S(1)} %get-tuple-element.28.latent_ref, bf16[2880,320]{1,0:T(8,128)(2,1)S(1)} %get-tuple-element.29.weight_ref), custom_call_target="tpu_custom_call" | custom-call | flops 167772160 | bytes 1048576 | tf_op jit(solution)/shard_map/prepare/pallas_call | solution.py:369
  6.8 0.0 collective-permute-done.inside_ref
  6.8 3.5 %collective-permute-done.1.across_ref = bf16[2,320,128]{2,1,0:T(8,128)(2,1)S(1)} collective-permute-done((bf16[2,320,128]{2,1,0:T(8,128)(2,1)S(1)}, bf16[2,320,128]{2,1,0:T(8,128)(2,1)S(1)}, u32[]{:S(2)}, u32[]{:S(2)}) %collective-permute-start.1) | collective-permute-done | bytes 163872 | tf_op jit(solution)/shard_map/ppermute | solution.py:368
  10.3 2.5 %first.1.first_ref = bf16[4,320,256]{2,1,0:T(8,128)(2,1)S(1)} custom-call(bf16[2,320,128]{2,1,0:T(8,128)(2,1)S(1)} %collective-permute-done.inside_ref, bf16[2,320,128]{2,1,0:T(8,128)(2,1)S(1)} %collective-permute-done.1.across_ref, bf16[320,2880]{1,0:T(8,128)(2,1)S(1)} %get-tuple-element.30.turned_ref, bf16[3840,256]{1,0:T(8,128)(2,1)S(1)} %get-tuple-element.31.field_ref), custom_call_target="tpu_custom_call" | custom-call | flops 1887436800 | bytes 1048576 | tf_op jit(solution)/shard_map/first/pallas_call | solution.py:377
  12.8 0.7 %collective-permute-start.4 = (bf16[4,320,256]{2,1,0:T(8,128)(2,1)S(1)}, bf16[4,320,256]{2,1,0:T(8,128)(2,1)S(1)}, u32[]{:S(2)}, u32[]{:S(2)}) collective-permute-start(bf16[4,320,256]{2,1,0:T(8,128)(2,1)S(1)} %first.1.first_ref), channel_id=1, source_target_pairs={{14,13},{2,1},{30,29},{18,17}} | collective-permute-start | bytes 1966088 | tf_op jit(solution)/shard_map/ppermute | solution.py:386
  13.5 2.1 %collective-permute-start.3 = (bf16[4,320,256]{2,1,0:T(8,128)(2,1)S(1)}, bf16[4,320,256]{2,1,0:T(8,128)(2,1)S(1)}, u32[]{:S(2)}, u32[]{:S(2)}) collective-permute-start(bf16[4,320,256]{2,1,0:T(8,128)(2,1)S(1)} %first.1.first_ref), channel_id=1, source_target_pairs={{2,6},{6,2},{3,7},{7,3},{4,8},{8,4},{5,9},{9,5},{18,22},{22,18},{1... | collective-permute-start | bytes 1966088 | tf_op jit(solution)/shard_map/ppermute | solution.py:388
  15.6 1.9 %collective-permute-start.2 = (bf16[4,320,256]{2,1,0:T(8,128)(2,1)S(1)}, bf16[4,320,256]{2,1,0:T(8,128)(2,1)S(1)}, u32[]{:S(2)}, u32[]{:S(2)}) collective-permute-start(bf16[4,320,256]{2,1,0:T(8,128)(2,1)S(1)} %first.1.first_ref), channel_id=1, source_target_pairs={{0,4},{4,0},{1,5},{5,1},{6,10},{10,6},{7,11},{11,7},{8,12},{12,8},... | collective-permute-start | bytes 1966088 | tf_op jit(solution)/shard_map/ppermute | solution.py:387
  17.5 6.9 %weights.1 = (bf16[320,960]{1,0:T(8,128)(2,1)S(1)}, bf16[640,2880]{1,0:T(8,128)(2,1)S(1)}, bf16[320,2880]{1,0:T(8,128)(2,1)S(1)}, bf16[4,320,2560]{2,1,0:T(8,128)(2,1)S(1)}) custom-call(bf16[960,320]{1,0:T(8,128)(2,1)} %bitcast.9, bf16[2880,640]{1,0:T(8,128)(2,1)} %bitcast.7, bf16[3,3,320,960]{3,2,1,0:T(8,128)(2,1)} %bitcast.6), custom_call_target="tpu_custom_call" | custom-call | flops 2000000000 | bytes 1048576 | tf_op jit(solution)/shard_map/weights/pallas_call | solution.py:398
  24.4 0.0 collective-permute-done.4
  24.4 0.7 %collective-permute-start.5 = (bf16[4,320,256]{2,1,0:T(8,128)(2,1)S(1)}, bf16[4,320,256]{2,1,0:T(8,128)(2,1)S(1)}, u32[]{:S(2)}, u32[]{:S(2)}) collective-permute-start(bf16[4,320,256]{2,1,0:T(8,128)(2,1)S(1)} %collective-permute-done.4), channel_id=1, source_target_pairs={{13,2},{1,14},{29,18},{17,30}} | collective-permute-start | bytes 1966088 | tf_op jit(solution)/shard_map/ppermute | solution.py:419
  25.1 8.4 %collective-permute-done.3.middle_ref = bf16[4,320,256]{2,1,0:T(8,128)(2,1)S(1)} collective-permute-done((bf16[4,320,256]{2,1,0:T(8,128)(2,1)S(1)}, bf16[4,320,256]{2,1,0:T(8,128)(2,1)S(1)}, u32[]{:S(2)}, u32[]{:S(2)}) %collective-permute-start.3) | collective-permute-done | bytes 655392 | tf_op jit(solution)/shard_map/ppermute | solution.py:388
  33.6 4.1 %collective-permute-done.2.outer_ref = bf16[4,320,256]{2,1,0:T(8,128)(2,1)S(1)} collective-permute-done((bf16[4,320,256]{2,1,0:T(8,128)(2,1)S(1)}, bf16[4,320,256]{2,1,0:T(8,128)(2,1)S(1)}, u32[]{:S(2)}, u32[]{:S(2)}) %collective-permute-start.2) | collective-permute-done | bytes 655392 | tf_op jit(solution)/shard_map/ppermute | solution.py:387
  37.7 0.0 collective-permute-done.5.relayed_ref
  37.7 1.0 %skip.1 = (bf16[4,320,256]{2,1,0:T(8,128)(2,1)S(1)}, bf16[2,320,256]{2,1,0:T(8,128)(2,1)S(1)}, bf16[2,320,256]{2,1,0:T(8,128)(2,1)S(1)}) custom-call(bf16[4,320,256]{2,1,0:T(8,128)(2,1)S(1)} %first.1.first_ref, bf16[4,320,256]{2,1,0:T(8,128)(2,1)S(1)} %collective-permute-done.2.outer_ref, bf16[4,320,256]{2,1,0:T(8,128)(2,1)S(1)} %collective-permute-done.3.middle_ref, ...), custom_call_target="tpu_custom_call" | custom-call | flops 629145600 | bytes 1048576 | tf_op jit(solution)/shard_map/skip/pallas_call | solution.py:420
  38.6 2.1 %collective-permute-start.7 = (bf16[2,320,256]{2,1,0:T(8,128)(2,1)S(1)}, bf16[2,320,256]{2,1,0:T(8,128)(2,1)S(1)}, u32[]{:S(2)}, u32[]{:S(2)}) collective-permute-start(bf16[2,320,256]{2,1,0:T(8,128)(2,1)S(1)} %get-tuple-element.45), channel_id=1, source_target_pairs={{3,4},{4,3},{7,8},{8,7},{11,12},{12,11},{15,0},{0,15},{19,20},{20,... | collective-permute-start | bytes 983048 | tf_op jit(solution)/shard_map/ppermute | solution.py:432
  40.7 0.1 collective-permute-start.6
  40.8 3.0 %own_rows.1 = (f32[4,320,256]{2,1,0:T(8,128)S(1)}, f32[640,512]{1,0:T(8,128)S(1)}) custom-call(bf16[4,320,256]{2,1,0:T(8,128)(2,1)S(1)} %get-tuple-element.39.refs_0_, bf16[2,320,256]{2,1,0:T(8,128)(2,1)S(1)} %get-tuple-element.40.refs_1_, bf16[640,2880]{1,0:T(8,128)(2,1)S(1)} %get-tuple-element.41.refs_2_.mid_ref, ...), custom_call_target="tpu_custom_call" | custom-call | flops 2516582400 | bytes 1048576 | tf_op jit(solution)/shard_map/own_rows/pallas_call | solution.py:435
  43.9 4.1 %collective-permute-done.7.across_ref = bf16[2,320,256]{2,1,0:T(8,128)(2,1)S(1)} collective-permute-done((bf16[2,320,256]{2,1,0:T(8,128)(2,1)S(1)}, bf16[2,320,256]{2,1,0:T(8,128)(2,1)S(1)}, u32[]{:S(2)}, u32[]{:S(2)}) %collective-permute-start.7) | collective-permute-done | bytes 327712 | tf_op jit(solution)/shard_map/ppermute | solution.py:432
  47.9 0.0 collective-permute-done.6.inside_ref
  47.9 4.7 %last.1 = bf16[2,4,320,128]{3,2,1,0:T(8,128)(2,1)} custom-call(f32[4,320,256]{2,1,0:T(8,128)S(1)} %get-tuple-element.43.mixed_ref, f32[640,512]{1,0:T(8,128)S(1)} %get-tuple-element.44.middle_ref, bf16[2,320,256]{2,1,0:T(8,128)(2,1)S(1)} %collective-permute-done.6.inside_ref, bf16[2,320,256]{2,1,0:T(8,128)(2,1)S(1)} %collective-permute-done.7.across_ref, ...), custom_call_target="tpu_custom_call" | custom-call | flops 2936012800 | bytes 1048576 | tf_op jit(solution)/shard_map/last/pallas_call | solution.py:445
Async XLA Ops:
  2.0 4.7 %collective-permute-start = (bf16[2,320,128]{2,1,0:T(8,128)(2,1)S(1)}, bf16[2,320,128]{2,1,0:T(8,128)(2,1)S(1)}, u32[]{:S(2)}, u32[]{:S(2)}) collective-permute-start(bf16[2,320,128]{2,1,0:T(8,128)(2,1)S(1)} %get-tuple-element.26), channel_id=1, source_target_pairs={{0,1},{1,0},{2,3},{3,2},{4,5},{5,4},{6,7},{7,6},{8,9},{9,8},{10,11... | collective-permute-start | bytes 491528 | tf_op jit(solution)/shard_map/ppermute | solution.py:367
  2.8 7.5 %collective-permute-start.1 = (bf16[2,320,128]{2,1,0:T(8,128)(2,1)S(1)}, bf16[2,320,128]{2,1,0:T(8,128)(2,1)S(1)}, u32[]{:S(2)}, u32[]{:S(2)}) collective-permute-start(bf16[2,320,128]{2,1,0:T(8,128)(2,1)S(1)} %get-tuple-element.27), channel_id=1, source_target_pairs={{3,4},{4,3},{7,8},{8,7},{11,12},{12,11},{15,0},{0,15},{19,20},{20,... | collective-permute-start | bytes 491528 | tf_op jit(solution)/shard_map/ppermute | solution.py:368
  12.8 11.6 %collective-permute-start.4 = (bf16[4,320,256]{2,1,0:T(8,128)(2,1)S(1)}, bf16[4,320,256]{2,1,0:T(8,128)(2,1)S(1)}, u32[]{:S(2)}, u32[]{:S(2)}) collective-permute-start(bf16[4,320,256]{2,1,0:T(8,128)(2,1)S(1)} %first.1.first_ref), channel_id=1, source_target_pairs={{14,13},{2,1},{30,29},{18,17}} | collective-permute-start | bytes 1966088 | tf_op jit(solution)/shard_map/ppermute | solution.py:386
  13.5 20.1 %collective-permute-start.3 = (bf16[4,320,256]{2,1,0:T(8,128)(2,1)S(1)}, bf16[4,320,256]{2,1,0:T(8,128)(2,1)S(1)}, u32[]{:S(2)}, u32[]{:S(2)}) collective-permute-start(bf16[4,320,256]{2,1,0:T(8,128)(2,1)S(1)} %first.1.first_ref), channel_id=1, source_target_pairs={{2,6},{6,2},{3,7},{7,3},{4,8},{8,4},{5,9},{9,5},{18,22},{22,18},{1... | collective-permute-start | bytes 1966088 | tf_op jit(solution)/shard_map/ppermute | solution.py:388
  15.6 22.1 %collective-permute-start.2 = (bf16[4,320,256]{2,1,0:T(8,128)(2,1)S(1)}, bf16[4,320,256]{2,1,0:T(8,128)(2,1)S(1)}, u32[]{:S(2)}, u32[]{:S(2)}) collective-permute-start(bf16[4,320,256]{2,1,0:T(8,128)(2,1)S(1)} %first.1.first_ref), channel_id=1, source_target_pairs={{0,4},{4,0},{1,5},{5,1},{6,10},{10,6},{7,11},{11,7},{8,12},{12,8},... | collective-permute-start | bytes 1966088 | tf_op jit(solution)/shard_map/ppermute | solution.py:387
  24.4 13.2 %collective-permute-start.5 = (bf16[4,320,256]{2,1,0:T(8,128)(2,1)S(1)}, bf16[4,320,256]{2,1,0:T(8,128)(2,1)S(1)}, u32[]{:S(2)}, u32[]{:S(2)}) collective-permute-start(bf16[4,320,256]{2,1,0:T(8,128)(2,1)S(1)} %collective-permute-done.4), channel_id=1, source_target_pairs={{13,2},{1,14},{29,18},{17,30}} | collective-permute-start | bytes 1966088 | tf_op jit(solution)/shard_map/ppermute | solution.py:419
  38.6 9.3 %collective-permute-start.7 = (bf16[2,320,256]{2,1,0:T(8,128)(2,1)S(1)}, bf16[2,320,256]{2,1,0:T(8,128)(2,1)S(1)}, u32[]{:S(2)}, u32[]{:S(2)}) collective-permute-start(bf16[2,320,256]{2,1,0:T(8,128)(2,1)S(1)} %get-tuple-element.45), channel_id=1, source_target_pairs={{3,4},{4,3},{7,8},{8,7},{11,12},{12,11},{15,0},{0,15},{19,20},{20,... | collective-permute-start | bytes 983048 | tf_op jit(solution)/shard_map/ppermute | solution.py:432
  40.7 7.2 %collective-permute-start.6 = (bf16[2,320,256]{2,1,0:T(8,128)(2,1)S(1)}, bf16[2,320,256]{2,1,0:T(8,128)(2,1)S(1)}, u32[]{:S(2)}, u32[]{:S(2)}) collective-permute-start(bf16[2,320,256]{2,1,0:T(8,128)(2,1)S(1)} %get-tuple-element.40.refs_1_), channel_id=1, source_target_pairs={{0,1},{1,0},{2,3},{3,2},{4,5},{5,4},{6,7},{7,6},{8,9},{9,8},{10,11... | collective-permute-start | bytes 983048 | tf_op jit(solution)/shard_map/ppermute | solution.py:433

commit v6 on v5

--- a/solution.py
+++ b/solution.py
@@ -167,7 +167,7 @@
 
 
 def skip_kernel(
-    first_ref, outer_ref, middle_ref, relayed_ref, weight_ref, skip_ref, inside_ref, across_ref,
+    first_ref, middle_ref, outer_ref, relayed_ref, weight_ref, skip_ref, inside_ref, across_ref,
     *, bands
 ):
     rows, _, wide = skip_ref.shape
@@ -384,8 +384,8 @@
         inputs=[whole] * 4,
     )(*in_vmem(inside_row, across_row, in_turned, field))
     hopped = lax.ppermute(first, "frames", hops)
+    middle = lax.ppermute(first, "frames", middle_frames)
     outer = lax.ppermute(first, "frames", outer_frames)
-    middle = lax.ppermute(first, "frames", middle_frames)
 
     time_rows, mid_rows, up_rows, first = lax.optimization_barrier(
         (
@@ -428,7 +428,7 @@
         8,
         flops=2 * rows * wide * depth * channels,
         inputs=[whole] * 5,
-    )(*in_vmem(first, outer, middle, relayed, time_turned))
+    )(*in_vmem(first, middle, outer, relayed, time_turned))
     from_across = lax.ppermute(across_rows, "frames", across)
     from_inside = lax.ppermute(inside_rows, "frames", inside)
 

time: 52.9 us -> 52.3 us (0.989)
  waiting for transfers between devices: 20.1 us -> 12.3 us
  starting transfers between devices: 11.4 us -> 18.5 us
    ppermute x1, waiting for transfers between devices: 8.42 us -> 3.54 us  [body(): middle = lax.ppermute(first, 'frames', middle_frames)]
    ppermute x1, starting transfers between devices: 2.08 us -> 6.36 us  [body(): middle = lax.ppermute(first, 'frames', middle_frames)]
    ppermute x1, waiting for transfers between devices: 4.08 us -> 2.5 us  [body(): from_across = lax.ppermute(across_rows, 'frames', across)]
    ppermute x1, starting transfers between devices: 2.1 us -> 3.68 us  [body(): from_across = lax.ppermute(across_rows, 'frames', across)]
    ppermute x1, waiting for transfers between devices: 4.1 us -> 2.75 us  [body(): outer = lax.ppermute(first, 'frames', outer_frames)]
    ppermute x1, starting transfers between devices: 1.92 us -> 3.2 us  [body(): outer = lax.ppermute(first, 'frames', outer_frames)]
where the time goes in v6:
time: 52.3 us; the launch traced here: 52 us
  Pallas kernels  21.1 us (40%)
  starting transfers between devices  18.5 us (35%)
  waiting for transfers between devices  12.3 us (24%)
    pallas_call x1, Pallas kernels, body(): call(weights_kernel, 'weights', [((channels, depth), BF16), ((inner, 3 *...  6.91 us
    ppermute x1, starting transfers between devices, body(): middle = lax.ppermute(first, 'frames', middle_frames)  6.36 us
    pallas_call x1, Pallas kernels, body(): call(functools.partial(last_kernel, bands=bands), 'last', [(turned.shape,...  4.75 us
    ppermute x1, starting transfers between devices, body(): from_across = lax.ppermute(across_rows, 'frames', across)  3.68 us
    ppermute x1, waiting for transfers between devices, body(): middle = lax.ppermute(first, 'frames', middle_frames)  3.54 us
    ppermute x1, waiting for transfers between devices, body(): across_row = lax.ppermute(across_rim, 'frames', across)  3.52 us
    ppermute x1, starting transfers between devices, body(): outer = lax.ppermute(first, 'frames', outer_frames)  3.2 us
    ppermute x1, starting transfers between devices, body(): across_row = lax.ppermute(across_rim, 'frames', across)  3.05 us
  transfers between devices with their start and end apart: 8, of which 4 were waited for; matrix products, arithmetic and copies ran while one was open for 0% of the time, Pallas kernels for 21%

profile of v6, /device:TPU:15, one launch (start us, length us, event | category | flops | bytes accessed | tf_op | source)
XLA Modules:
  0.0 52.0 jit_solution(15769086325112436391)
XLA Ops:
  0.0 2.0 %fetch.1 = (bf16[2,320,128]{2,1,0:T(8,128)(2,1)S(1)}, bf16[2,320,128]{2,1,0:T(8,128)(2,1)S(1)}, bf16[2,4,320,128]{3,2,1,0:T(8,128)(2,1)S(1)}, bf16[2880,320]{1,0:T(8,128)(2,1)S(1)}) custom-call(bf16[2,4,320,128]{3,2,1,0:T(8,128)(2,1)} %bitcast.10, bf16[2880,320]{1,0:T(8,128)(2,1)} %bitcast.8), custom_call_target="tpu_custom_call" | custom-call | bytes 1048576 | tf_op jit(solution)/shard_map/fetch/pallas_call | solution.py:354
  2.0 0.7 %collective-permute-start = (bf16[2,320,128]{2,1,0:T(8,128)(2,1)S(1)}, bf16[2,320,128]{2,1,0:T(8,128)(2,1)S(1)}, u32[]{:S(2)}, u32[]{:S(2)}) collective-permute-start(bf16[2,320,128]{2,1,0:T(8,128)(2,1)S(1)} %get-tuple-element.26), channel_id=1, source_target_pairs={{0,1},{1,0},{2,3},{3,2},{4,5},{5,4},{6,7},{7,6},{8,9},{9,8},{10,11... | collective-permute-start | bytes 491528 | tf_op jit(solution)/shard_map/ppermute | solution.py:367
  2.8 3.0 %collective-permute-start.1 = (bf16[2,320,128]{2,1,0:T(8,128)(2,1)S(1)}, bf16[2,320,128]{2,1,0:T(8,128)(2,1)S(1)}, u32[]{:S(2)}, u32[]{:S(2)}) collective-permute-start(bf16[2,320,128]{2,1,0:T(8,128)(2,1)S(1)} %get-tuple-element.27), channel_id=1, source_target_pairs={{3,4},{4,3},{7,8},{8,7},{11,12},{12,11},{15,0},{0,15},{19,20},{20,... | collective-permute-start | bytes 491528 | tf_op jit(solution)/shard_map/ppermute | solution.py:368
  5.8 0.9 %prepare.1 = (bf16[320,2880]{1,0:T(8,128)(2,1)S(1)}, bf16[3840,256]{1,0:T(8,128)(2,1)S(1)}) custom-call(bf16[2,4,320,128]{3,2,1,0:T(8,128)(2,1)S(1)} %get-tuple-element.28.latent_ref, bf16[2880,320]{1,0:T(8,128)(2,1)S(1)} %get-tuple-element.29.weight_ref), custom_call_target="tpu_custom_call" | custom-call | flops 167772160 | bytes 1048576 | tf_op jit(solution)/shard_map/prepare/pallas_call | solution.py:369
  6.8 0.0 collective-permute-done.inside_ref
  6.8 3.5 %collective-permute-done.1.across_ref = bf16[2,320,128]{2,1,0:T(8,128)(2,1)S(1)} collective-permute-done((bf16[2,320,128]{2,1,0:T(8,128)(2,1)S(1)}, bf16[2,320,128]{2,1,0:T(8,128)(2,1)S(1)}, u32[]{:S(2)}, u32[]{:S(2)}) %collective-permute-start.1) | collective-permute-done | bytes 163872 | tf_op jit(solution)/shard_map/ppermute | solution.py:368
  10.3 2.5 %first.1.first_ref = bf16[4,320,256]{2,1,0:T(8,128)(2,1)S(1)} custom-call(bf16[2,320,128]{2,1,0:T(8,128)(2,1)S(1)} %collective-permute-done.inside_ref, bf16[2,320,128]{2,1,0:T(8,128)(2,1)S(1)} %collective-permute-done.1.across_ref, bf16[320,2880]{1,0:T(8,128)(2,1)S(1)} %get-tuple-element.30.turned_ref, bf16[3840,256]{1,0:T(8,128)(2,1)S(1)} %get-tuple-element.31.field_ref), custom_call_target="tpu_custom_call" | custom-call | flops 1887436800 | bytes 1048576 | tf_op jit(solution)/shard_map/first/pallas_call | solution.py:377
  12.8 0.7 %collective-permute-start.4 = (bf16[4,320,256]{2,1,0:T(8,128)(2,1)S(1)}, bf16[4,320,256]{2,1,0:T(8,128)(2,1)S(1)}, u32[]{:S(2)}, u32[]{:S(2)}) collective-permute-start(bf16[4,320,256]{2,1,0:T(8,128)(2,1)S(1)} %first.1.first_ref), channel_id=1, source_target_pairs={{14,13},{2,1},{30,29},{18,17}} | collective-permute-start | bytes 1966088 | tf_op jit(solution)/shard_map/ppermute | solution.py:386
  13.5 3.2 %collective-permute-start.3 = (bf16[4,320,256]{2,1,0:T(8,128)(2,1)S(1)}, bf16[4,320,256]{2,1,0:T(8,128)(2,1)S(1)}, u32[]{:S(2)}, u32[]{:S(2)}) collective-permute-start(bf16[4,320,256]{2,1,0:T(8,128)(2,1)S(1)} %first.1.first_ref), channel_id=1, source_target_pairs={{0,4},{4,0},{1,5},{5,1},{6,10},{10,6},{7,11},{11,7},{8,12},{12,8},... | collective-permute-start | bytes 1966088 | tf_op jit(solution)/shard_map/ppermute | solution.py:388
  16.7 6.4 %collective-permute-start.2 = (bf16[4,320,256]{2,1,0:T(8,128)(2,1)S(1)}, bf16[4,320,256]{2,1,0:T(8,128)(2,1)S(1)}, u32[]{:S(2)}, u32[]{:S(2)}) collective-permute-start(bf16[4,320,256]{2,1,0:T(8,128)(2,1)S(1)} %first.1.first_ref), channel_id=1, source_target_pairs={{2,6},{6,2},{3,7},{7,3},{4,8},{8,4},{5,9},{9,5},{18,22},{22,18},{1... | collective-permute-start | bytes 1966088 | tf_op jit(solution)/shard_map/ppermute | solution.py:387
  23.1 6.9 %weights.1 = (bf16[320,960]{1,0:T(8,128)(2,1)S(1)}, bf16[640,2880]{1,0:T(8,128)(2,1)S(1)}, bf16[320,2880]{1,0:T(8,128)(2,1)S(1)}, bf16[4,320,2560]{2,1,0:T(8,128)(2,1)S(1)}) custom-call(bf16[960,320]{1,0:T(8,128)(2,1)} %bitcast.9, bf16[2880,640]{1,0:T(8,128)(2,1)} %bitcast.7, bf16[3,3,320,960]{3,2,1,0:T(8,128)(2,1)} %bitcast.6), custom_call_target="tpu_custom_call" | custom-call | flops 2000000000 | bytes 1048576 | tf_op jit(solution)/shard_map/weights/pallas_call | solution.py:398
  30.0 0.0 collective-permute-done.4
  30.0 0.7 %collective-permute-start.5 = (bf16[4,320,256]{2,1,0:T(8,128)(2,1)S(1)}, bf16[4,320,256]{2,1,0:T(8,128)(2,1)S(1)}, u32[]{:S(2)}, u32[]{:S(2)}) collective-permute-start(bf16[4,320,256]{2,1,0:T(8,128)(2,1)S(1)} %collective-permute-done.4), channel_id=1, source_target_pairs={{13,2},{1,14},{29,18},{17,30}} | collective-permute-start | bytes 1966088 | tf_op jit(solution)/shard_map/ppermute | solution.py:419
  30.7 2.7 %collective-permute-done.3.outer_ref = bf16[4,320,256]{2,1,0:T(8,128)(2,1)S(1)} collective-permute-done((bf16[4,320,256]{2,1,0:T(8,128)(2,1)S(1)}, bf16[4,320,256]{2,1,0:T(8,128)(2,1)S(1)}, u32[]{:S(2)}, u32[]{:S(2)}) %collective-permute-start.3) | collective-permute-done | bytes 655392 | tf_op jit(solution)/shard_map/ppermute | solution.py:388
  33.5 3.5 %collective-permute-done.2.middle_ref = bf16[4,320,256]{2,1,0:T(8,128)(2,1)S(1)} collective-permute-done((bf16[4,320,256]{2,1,0:T(8,128)(2,1)S(1)}, bf16[4,320,256]{2,1,0:T(8,128)(2,1)S(1)}, u32[]{:S(2)}, u32[]{:S(2)}) %collective-permute-start.2) | collective-permute-done | bytes 655392 | tf_op jit(solution)/shard_map/ppermute | solution.py:387
  37.0 0.0 collective-permute-done.5.relayed_ref
  37.0 1.0 %skip.1 = (bf16[4,320,256]{2,1,0:T(8,128)(2,1)S(1)}, bf16[2,320,256]{2,1,0:T(8,128)(2,1)S(1)}, bf16[2,320,256]{2,1,0:T(8,128)(2,1)S(1)}) custom-call(bf16[4,320,256]{2,1,0:T(8,128)(2,1)S(1)} %first.1.first_ref, bf16[4,320,256]{2,1,0:T(8,128)(2,1)S(1)} %collective-permute-done.2.middle_ref, bf16[4,320,256]{2,1,0:T(8,128)(2,1)S(1)} %collective-permute-done.3.outer_ref, ...), custom_call_target="tpu_custom_call" | custom-call | flops 629145600 | bytes 1048576 | tf_op jit(solution)/shard_map/skip/pallas_call | solution.py:420
  38.0 3.7 %collective-permute-start.7 = (bf16[2,320,256]{2,1,0:T(8,128)(2,1)S(1)}, bf16[2,320,256]{2,1,0:T(8,128)(2,1)S(1)}, u32[]{:S(2)}, u32[]{:S(2)}) collective-permute-start(bf16[2,320,256]{2,1,0:T(8,128)(2,1)S(1)} %get-tuple-element.45), channel_id=1, source_target_pairs={{3,4},{4,3},{7,8},{8,7},{11,12},{12,11},{15,0},{0,15},{19,20},{20,... | collective-permute-start | bytes 983048 | tf_op jit(solution)/shard_map/ppermute | solution.py:432
  41.7 0.1 collective-permute-start.6
  41.7 3.0 %own_rows.1 = (f32[4,320,256]{2,1,0:T(8,128)S(1)}, f32[640,512]{1,0:T(8,128)S(1)}) custom-call(bf16[4,320,256]{2,1,0:T(8,128)(2,1)S(1)} %get-tuple-element.39.refs_0_, bf16[2,320,256]{2,1,0:T(8,128)(2,1)S(1)} %get-tuple-element.40.refs_1_, bf16[640,2880]{1,0:T(8,128)(2,1)S(1)} %get-tuple-element.41.refs_2_.mid_ref, ...), custom_call_target="tpu_custom_call" | custom-call | flops 2516582400 | bytes 1048576 | tf_op jit(solution)/shard_map/own_rows/pallas_call | solution.py:435
  44.8 2.5 %collective-permute-done.7.across_ref = bf16[2,320,256]{2,1,0:T(8,128)(2,1)S(1)} collective-permute-done((bf16[2,320,256]{2,1,0:T(8,128)(2,1)S(1)}, bf16[2,320,256]{2,1,0:T(8,128)(2,1)S(1)}, u32[]{:S(2)}, u32[]{:S(2)}) %collective-permute-start.7) | collective-permute-done | bytes 327712 | tf_op jit(solution)/shard_map/ppermute | solution.py:432
  47.3 0.0 collective-permute-done.6.inside_ref
  47.3 4.7 %last.1 = bf16[2,4,320,128]{3,2,1,0:T(8,128)(2,1)} custom-call(f32[4,320,256]{2,1,0:T(8,128)S(1)} %get-tuple-element.43.mixed_ref, f32[640,512]{1,0:T(8,128)S(1)} %get-tuple-element.44.middle_ref, bf16[2,320,256]{2,1,0:T(8,128)(2,1)S(1)} %collective-permute-done.6.inside_ref, bf16[2,320,256]{2,1,0:T(8,128)(2,1)S(1)} %collective-permute-done.7.across_ref, ...), custom_call_target="tpu_custom_call" | custom-call | flops 2936012800 | bytes 1048576 | tf_op jit(solution)/shard_map/last/pallas_call | solution.py:445
Async XLA Ops:
  2.0 4.7 %collective-permute-start = (bf16[2,320,128]{2,1,0:T(8,128)(2,1)S(1)}, bf16[2,320,128]{2,1,0:T(8,128)(2,1)S(1)}, u32[]{:S(2)}, u32[]{:S(2)}) collective-permute-start(bf16[2,320,128]{2,1,0:T(8,128)(2,1)S(1)} %get-tuple-element.26), channel_id=1, source_target_pairs={{0,1},{1,0},{2,3},{3,2},{4,5},{5,4},{6,7},{7,6},{8,9},{9,8},{10,11... | collective-permute-start | bytes 491528 | tf_op jit(solution)/shard_map/ppermute | solution.py:367
  2.8 7.5 %collective-permute-start.1 = (bf16[2,320,128]{2,1,0:T(8,128)(2,1)S(1)}, bf16[2,320,128]{2,1,0:T(8,128)(2,1)S(1)}, u32[]{:S(2)}, u32[]{:S(2)}) collective-permute-start(bf16[2,320,128]{2,1,0:T(8,128)(2,1)S(1)} %get-tuple-element.27), channel_id=1, source_target_pairs={{3,4},{4,3},{7,8},{8,7},{11,12},{12,11},{15,0},{0,15},{19,20},{20,... | collective-permute-start | bytes 491528 | tf_op jit(solution)/shard_map/ppermute | solution.py:368
  12.8 17.2 %collective-permute-start.4 = (bf16[4,320,256]{2,1,0:T(8,128)(2,1)S(1)}, bf16[4,320,256]{2,1,0:T(8,128)(2,1)S(1)}, u32[]{:S(2)}, u32[]{:S(2)}) collective-permute-start(bf16[4,320,256]{2,1,0:T(8,128)(2,1)S(1)} %first.1.first_ref), channel_id=1, source_target_pairs={{14,13},{2,1},{30,29},{18,17}} | collective-permute-start | bytes 1966088 | tf_op jit(solution)/shard_map/ppermute | solution.py:386
  13.5 20.0 %collective-permute-start.3 = (bf16[4,320,256]{2,1,0:T(8,128)(2,1)S(1)}, bf16[4,320,256]{2,1,0:T(8,128)(2,1)S(1)}, u32[]{:S(2)}, u32[]{:S(2)}) collective-permute-start(bf16[4,320,256]{2,1,0:T(8,128)(2,1)S(1)} %first.1.first_ref), channel_id=1, source_target_pairs={{0,4},{4,0},{1,5},{5,1},{6,10},{10,6},{7,11},{11,7},{8,12},{12,8},... | collective-permute-start | bytes 1966088 | tf_op jit(solution)/shard_map/ppermute | solution.py:388
  16.7 20.3 %collective-permute-start.2 = (bf16[4,320,256]{2,1,0:T(8,128)(2,1)S(1)}, bf16[4,320,256]{2,1,0:T(8,128)(2,1)S(1)}, u32[]{:S(2)}, u32[]{:S(2)}) collective-permute-start(bf16[4,320,256]{2,1,0:T(8,128)(2,1)S(1)} %first.1.first_ref), channel_id=1, source_target_pairs={{2,6},{6,2},{3,7},{7,3},{4,8},{8,4},{5,9},{9,5},{18,22},{22,18},{1... | collective-permute-start | bytes 1966088 | tf_op jit(solution)/shard_map/ppermute | solution.py:387
  30.0 7.0 %collective-permute-start.5 = (bf16[4,320,256]{2,1,0:T(8,128)(2,1)S(1)}, bf16[4,320,256]{2,1,0:T(8,128)(2,1)S(1)}, u32[]{:S(2)}, u32[]{:S(2)}) collective-permute-start(bf16[4,320,256]{2,1,0:T(8,128)(2,1)S(1)} %collective-permute-done.4), channel_id=1, source_target_pairs={{13,2},{1,14},{29,18},{17,30}} | collective-permute-start | bytes 1966088 | tf_op jit(solution)/shard_map/ppermute | solution.py:419
  38.0 9.3 %collective-permute-start.7 = (bf16[2,320,256]{2,1,0:T(8,128)(2,1)S(1)}, bf16[2,320,256]{2,1,0:T(8,128)(2,1)S(1)}, u32[]{:S(2)}, u32[]{:S(2)}) collective-permute-start(bf16[2,320,256]{2,1,0:T(8,128)(2,1)S(1)} %get-tuple-element.45), channel_id=1, source_target_pairs={{3,4},{4,3},{7,8},{8,7},{11,12},{12,11},{15,0},{0,15},{19,20},{20,... | collective-permute-start | bytes 983048 | tf_op jit(solution)/shard_map/ppermute | solution.py:432
  41.7 5.6 %collective-permute-start.6 = (bf16[2,320,256]{2,1,0:T(8,128)(2,1)S(1)}, bf16[2,320,256]{2,1,0:T(8,128)(2,1)S(1)}, u32[]{:S(2)}, u32[]{:S(2)}) collective-permute-start(bf16[2,320,256]{2,1,0:T(8,128)(2,1)S(1)} %get-tuple-element.40.refs_1_), channel_id=1, source_target_pairs={{0,1},{1,0},{2,3},{3,2},{4,5},{5,4},{6,7},{7,6},{8,9},{9,8},{10,11... | collective-permute-start | bytes 983048 | tf_op jit(solution)/shard_map/ppermute | solution.py:433

commit v7 on v6

--- a/solution.py
+++ b/solution.py
@@ -167,7 +167,7 @@
 
 
 def skip_kernel(
-    first_ref, middle_ref, outer_ref, relayed_ref, weight_ref, skip_ref, inside_ref, across_ref,
+    first_ref, second_swap, first_swap, relayed_ref, weight_ref, skip_ref, inside_ref, across_ref,
     *, bands
 ):
     rows, _, wide = skip_ref.shape
@@ -175,12 +175,18 @@
     band, frame = place(bands)
     odd_band, odd_frame = lax.rem(band, 2) == 1, lax.rem(frame, 2) == 1
     is_relayed = jnp.logical_and(jnp.logical_and(frame < 2, band < bands // 2), lax.rem(band, 2) == 0)
+    upper = band < bands // 2
+    first_is_before = upper == odd_frame
+    is_host = jnp.logical_and(
+        jnp.logical_not(upper), jnp.logical_or(frame == 0, frame == FRAMES - 1)
+    )
     skips = []
     for row in range(rows):
-        centre, middle = first_ref[row], middle_ref[row]
-        outer = jnp.where(is_relayed, relayed_ref[row], outer_ref[row])
-        before = jnp.where(odd_frame, outer, middle)
-        after = jnp.where(odd_frame, middle, outer)
+        centre, second = first_ref[row], second_swap[row]
+        first = jnp.where(is_host, jnp.zeros((), BF16), first_swap[row])
+        first = jnp.where(is_relayed, relayed_ref[row], first)
+        before = jnp.where(first_is_before, first, second)
+        after = jnp.where(first_is_before, second, first)
         stacked = jnp.concatenate([before, centre, after], axis=0)
         skip = (centre.astype(F32) + dot(weight_ref[...], stacked)).astype(BF16)
         skip_ref[row] = skip
@@ -383,9 +389,11 @@
         flops=2 * rows * wide * channels * 3 * depth,
         inputs=[whole] * 4,
     )(*in_vmem(inside_row, across_row, in_turned, field))
-    hopped = lax.ppermute(first, "frames", hops)
-    middle = lax.ppermute(first, "frames", middle_frames)
-    outer = lax.ppermute(first, "frames", outer_frames)
+    of_bands = lambda pairs, upper: [pair for pair in pairs if (band_of(pair[0]) < offset) == upper]
+    first_pairs = of_bands(outer_frames, True) + of_bands(middle_frames, False) + hops
+    second_pairs = of_bands(middle_frames, True) + of_bands(outer_frames, False)
+    first_swap = lax.ppermute(first, "frames", first_pairs)
+    second_swap = lax.ppermute(first, "frames", second_pairs)
 
     time_rows, mid_rows, up_rows, first = lax.optimization_barrier(
         (
@@ -415,7 +423,7 @@
         inputs=[anywhere] * 3,
     )(in_hbm(time_rows), in_hbm(mid_rows), in_hbm(up_rows))
 
-    hopped, time_turned = lax.optimization_barrier((hopped, time_turned))
+    hopped, time_turned = lax.optimization_barrier((first_swap, time_turned))
     relayed = lax.ppermute(hopped, "frames", relays)
     skip, inside_rows, across_rows = call(
         functools.partial(skip_kernel, bands=bands),
@@ -428,7 +436,7 @@
         8,
         flops=2 * rows * wide * depth * channels,
         inputs=[whole] * 5,
-    )(*in_vmem(first, middle, outer, relayed, time_turned))
+    )(*in_vmem(first, second_swap, first_swap, relayed, time_turned))
     from_across = lax.ppermute(across_rows, "frames", across)
     from_inside = lax.ppermute(inside_rows, "frames", inside)
 

time: 52.3 us -> 51.6 us (0.987)
  starting transfers between devices: 18.5 us -> 15.9 us
  waiting for transfers between devices: 12.3 us -> 14.3 us
    ppermute x1, starting transfers between devices: 3.68 us -> 2.1 us  [body(): from_across = lax.ppermute(across_rows, 'frames', across)]
    ppermute x1, waiting for transfers between devices: 2.5 us -> 4.08 us  [body(): from_across = lax.ppermute(across_rows, 'frames', across)]
    ppermute x3 -> x2, starting transfers between devices: 10.3 us -> 9.21 us  [the longest x1 6 us: body(): second_swap = lax.ppermute(first, 'frames', second_pairs)]
    ppermute x3 -> x2, waiting for transfers between devices: 6.29 us -> 6.67 us  [the longest x1 3.83 us: body(): first_swap = lax.ppermute(first, 'frames', first_pairs)]
  transfers between devices with their start and end apart: 8 -> 7, of which waited for: 4 -> 4; matrix products, arithmetic and copies ran while one was open for 0% -> 0% of each run, Pallas kernels for 21% -> 21%
where the time goes in v7:
time: 51.6 us; the launch traced here: 51.3 us
  Pallas kernels  21.1 us (41%)
  starting transfers between devices  15.9 us (31%)
  waiting for transfers between devices  14.3 us (28%)
    pallas_call x1, Pallas kernels, body(): call(weights_kernel, 'weights', [((channels, depth), BF16), ((inner, 3 *...  6.91 us
    ppermute x1, starting transfers between devices, body(): second_swap = lax.ppermute(first, 'frames', second_pairs)  6 us
    pallas_call x1, Pallas kernels, body(): call(functools.partial(last_kernel, bands=bands), 'last', [(turned.shape,...  4.76 us
    ppermute x1, waiting for transfers between devices, body(): from_across = lax.ppermute(across_rows, 'frames', across)  4.08 us
    ppermute x1, waiting for transfers between devices, body(): first_swap = lax.ppermute(first, 'frames', first_pairs)  3.83 us
    ppermute x1, waiting for transfers between devices, body(): across_row = lax.ppermute(across_rim, 'frames', across)  3.52 us
    ppermute x1, starting transfers between devices, body(): first_swap = lax.ppermute(first, 'frames', first_pairs)  3.2 us
    ppermute x1, starting transfers between devices, body(): across_row = lax.ppermute(across_rim, 'frames', across)  3.05 us
  transfers between devices with their start and end apart: 7, of which 4 were waited for; matrix products, arithmetic and copies ran while one was open for 0% of the time, Pallas kernels for 21%

profile of v7, /device:TPU:15, one launch (start us, length us, event | category | flops | bytes accessed | tf_op | source)
XLA Modules:
  0.0 51.3 jit_solution(11603465345908827499)
XLA Ops:
  0.0 2.0 %fetch.1 = (bf16[2,320,128]{2,1,0:T(8,128)(2,1)S(1)}, bf16[2,320,128]{2,1,0:T(8,128)(2,1)S(1)}, bf16[2,4,320,128]{3,2,1,0:T(8,128)(2,1)S(1)}, bf16[2880,320]{1,0:T(8,128)(2,1)S(1)}) custom-call(bf16[2,4,320,128]{3,2,1,0:T(8,128)(2,1)} %bitcast.10, bf16[2880,320]{1,0:T(8,128)(2,1)} %bitcast.8), custom_call_target="tpu_custom_call" | custom-call | bytes 1048576 | tf_op jit(solution)/shard_map/fetch/pallas_call | solution.py:360
  2.0 0.7 %collective-permute-start = (bf16[2,320,128]{2,1,0:T(8,128)(2,1)S(1)}, bf16[2,320,128]{2,1,0:T(8,128)(2,1)S(1)}, u32[]{:S(2)}, u32[]{:S(2)}) collective-permute-start(bf16[2,320,128]{2,1,0:T(8,128)(2,1)S(1)} %get-tuple-element.26), channel_id=1, source_target_pairs={{0,1},{1,0},{2,3},{3,2},{4,5},{5,4},{6,7},{7,6},{8,9},{9,8},{10,11... | collective-permute-start | bytes 491528 | tf_op jit(solution)/shard_map/ppermute | solution.py:373
  2.8 3.0 %collective-permute-start.1 = (bf16[2,320,128]{2,1,0:T(8,128)(2,1)S(1)}, bf16[2,320,128]{2,1,0:T(8,128)(2,1)S(1)}, u32[]{:S(2)}, u32[]{:S(2)}) collective-permute-start(bf16[2,320,128]{2,1,0:T(8,128)(2,1)S(1)} %get-tuple-element.27), channel_id=1, source_target_pairs={{3,4},{4,3},{7,8},{8,7},{11,12},{12,11},{15,0},{0,15},{19,20},{20,... | collective-permute-start | bytes 491528 | tf_op jit(solution)/shard_map/ppermute | solution.py:374
  5.8 0.9 %prepare.1 = (bf16[320,2880]{1,0:T(8,128)(2,1)S(1)}, bf16[3840,256]{1,0:T(8,128)(2,1)S(1)}) custom-call(bf16[2,4,320,128]{3,2,1,0:T(8,128)(2,1)S(1)} %get-tuple-element.28.latent_ref, bf16[2880,320]{1,0:T(8,128)(2,1)S(1)} %get-tuple-element.29.weight_ref), custom_call_target="tpu_custom_call" | custom-call | flops 167772160 | bytes 1048576 | tf_op jit(solution)/shard_map/prepare/pallas_call | solution.py:375
  6.8 0.0 collective-permute-done.inside_ref
  6.8 3.5 %collective-permute-done.1.across_ref = bf16[2,320,128]{2,1,0:T(8,128)(2,1)S(1)} collective-permute-done((bf16[2,320,128]{2,1,0:T(8,128)(2,1)S(1)}, bf16[2,320,128]{2,1,0:T(8,128)(2,1)S(1)}, u32[]{:S(2)}, u32[]{:S(2)}) %collective-permute-start.1) | collective-permute-done | bytes 163872 | tf_op jit(solution)/shard_map/ppermute | solution.py:374
  10.3 2.5 %first.1.first_ref = bf16[4,320,256]{2,1,0:T(8,128)(2,1)S(1)} custom-call(bf16[2,320,128]{2,1,0:T(8,128)(2,1)S(1)} %collective-permute-done.inside_ref, bf16[2,320,128]{2,1,0:T(8,128)(2,1)S(1)} %collective-permute-done.1.across_ref, bf16[320,2880]{1,0:T(8,128)(2,1)S(1)} %get-tuple-element.30.turned_ref, bf16[3840,256]{1,0:T(8,128)(2,1)S(1)} %get-tuple-element.31.field_ref), custom_call_target="tpu_custom_call" | custom-call | flops 1887436800 | bytes 1048576 | tf_op jit(solution)/shard_map/first/pallas_call | solution.py:383
  12.8 3.2 %collective-permute-start.3 = (bf16[4,320,256]{2,1,0:T(8,128)(2,1)S(1)}, bf16[4,320,256]{2,1,0:T(8,128)(2,1)S(1)}, u32[]{:S(2)}, u32[]{:S(2)}) collective-permute-start(bf16[4,320,256]{2,1,0:T(8,128)(2,1)S(1)} %first.1.first_ref), channel_id=1, source_target_pairs={{6,10},{10,6},{7,11},{11,7},{15,3},{3,15},{4,8},{8,4},{5,9},{9,5},... | collective-permute-start | bytes 1966088 | tf_op jit(solution)/shard_map/ppermute | solution.py:395
  16.0 6.0 %collective-permute-start.2 = (bf16[4,320,256]{2,1,0:T(8,128)(2,1)S(1)}, bf16[4,320,256]{2,1,0:T(8,128)(2,1)S(1)}, u32[]{:S(2)}, u32[]{:S(2)}) collective-permute-start(bf16[4,320,256]{2,1,0:T(8,128)(2,1)S(1)} %first.1.first_ref), channel_id=1, source_target_pairs={{2,6},{6,2},{3,7},{7,3},{0,4},{4,0},{1,5},{5,1},{8,12},{12,8},{9,1... | collective-permute-start | bytes 1966088 | tf_op jit(solution)/shard_map/ppermute | solution.py:396
  22.0 6.9 %weights.1 = (bf16[320,960]{1,0:T(8,128)(2,1)S(1)}, bf16[640,2880]{1,0:T(8,128)(2,1)S(1)}, bf16[320,2880]{1,0:T(8,128)(2,1)S(1)}, bf16[4,320,2560]{2,1,0:T(8,128)(2,1)S(1)}) custom-call(bf16[960,320]{1,0:T(8,128)(2,1)} %bitcast.9, bf16[2880,640]{1,0:T(8,128)(2,1)} %bitcast.7, bf16[3,3,320,960]{3,2,1,0:T(8,128)(2,1)} %bitcast.6), custom_call_target="tpu_custom_call" | custom-call | flops 2000000000 | bytes 1048576 | tf_op jit(solution)/shard_map/weights/pallas_call | solution.py:406
  28.9 3.8 %collective-permute-done.3.first_swap = bf16[4,320,256]{2,1,0:T(8,128)(2,1)S(1)} collective-permute-done((bf16[4,320,256]{2,1,0:T(8,128)(2,1)S(1)}, bf16[4,320,256]{2,1,0:T(8,128)(2,1)S(1)}, u32[]{:S(2)}, u32[]{:S(2)}) %collective-permute-start.3) | collective-permute-done | bytes 655392 | tf_op jit(solution)/shard_map/ppermute | solution.py:395
  32.7 0.7 %collective-permute-start.4 = (bf16[4,320,256]{2,1,0:T(8,128)(2,1)S(1)}, bf16[4,320,256]{2,1,0:T(8,128)(2,1)S(1)}, u32[]{:S(2)}, u32[]{:S(2)}) collective-permute-start(bf16[4,320,256]{2,1,0:T(8,128)(2,1)S(1)} %collective-permute-done.3.first_swap), channel_id=1, source_target_pairs={{13,2},{1,14},{29,18},{17,30}} | collective-permute-start | bytes 1966088 | tf_op jit(solution)/shard_map/ppermute | solution.py:427
  33.4 2.8 %collective-permute-done.2.second_swap = bf16[4,320,256]{2,1,0:T(8,128)(2,1)S(1)} collective-permute-done((bf16[4,320,256]{2,1,0:T(8,128)(2,1)S(1)}, bf16[4,320,256]{2,1,0:T(8,128)(2,1)S(1)}, u32[]{:S(2)}, u32[]{:S(2)}) %collective-permute-start.2) | collective-permute-done | bytes 655392 | tf_op jit(solution)/shard_map/ppermute | solution.py:396
  36.3 0.0 collective-permute-done.4.relayed_ref
  36.3 1.0 %skip.1 = (bf16[4,320,256]{2,1,0:T(8,128)(2,1)S(1)}, bf16[2,320,256]{2,1,0:T(8,128)(2,1)S(1)}, bf16[2,320,256]{2,1,0:T(8,128)(2,1)S(1)}) custom-call(bf16[4,320,256]{2,1,0:T(8,128)(2,1)S(1)} %first.1.first_ref, bf16[4,320,256]{2,1,0:T(8,128)(2,1)S(1)} %collective-permute-done.2.second_swap, bf16[4,320,256]{2,1,0:T(8,128)(2,1)S(1)} %collective-permute-done.3.first_swap, ...), custom_call_target="tpu_custom_call" | custom-call | flops 629145600 | bytes 1048576 | tf_op jit(solution)/shard_map/skip/pallas_call | solution.py:428
  37.3 2.1 %collective-permute-start.6 = (bf16[2,320,256]{2,1,0:T(8,128)(2,1)S(1)}, bf16[2,320,256]{2,1,0:T(8,128)(2,1)S(1)}, u32[]{:S(2)}, u32[]{:S(2)}) collective-permute-start(bf16[2,320,256]{2,1,0:T(8,128)(2,1)S(1)} %get-tuple-element.45), channel_id=1, source_target_pairs={{3,4},{4,3},{7,8},{8,7},{11,12},{12,11},{15,0},{0,15},{19,20},{20,... | collective-permute-start | bytes 983048 | tf_op jit(solution)/shard_map/ppermute | solution.py:440
  39.4 0.1 collective-permute-start.5
  39.5 3.0 %own_rows.1 = (f32[4,320,256]{2,1,0:T(8,128)S(1)}, f32[640,512]{1,0:T(8,128)S(1)}) custom-call(bf16[4,320,256]{2,1,0:T(8,128)(2,1)S(1)} %get-tuple-element.39.refs_0_, bf16[2,320,256]{2,1,0:T(8,128)(2,1)S(1)} %get-tuple-element.40.refs_1_, bf16[640,2880]{1,0:T(8,128)(2,1)S(1)} %get-tuple-element.41.refs_2_.mid_ref, ...), custom_call_target="tpu_custom_call" | custom-call | flops 2516582400 | bytes 1048576 | tf_op jit(solution)/shard_map/own_rows/pallas_call | solution.py:443
  42.5 4.1 %collective-permute-done.6.across_ref = bf16[2,320,256]{2,1,0:T(8,128)(2,1)S(1)} collective-permute-done((bf16[2,320,256]{2,1,0:T(8,128)(2,1)S(1)}, bf16[2,320,256]{2,1,0:T(8,128)(2,1)S(1)}, u32[]{:S(2)}, u32[]{:S(2)}) %collective-permute-start.6) | collective-permute-done | bytes 327712 | tf_op jit(solution)/shard_map/ppermute | solution.py:440
  46.6 0.0 collective-permute-done.5.inside_ref
  46.6 4.8 %last.1 = bf16[2,4,320,128]{3,2,1,0:T(8,128)(2,1)} custom-call(f32[4,320,256]{2,1,0:T(8,128)S(1)} %get-tuple-element.43.mixed_ref, f32[640,512]{1,0:T(8,128)S(1)} %get-tuple-element.44.middle_ref, bf16[2,320,256]{2,1,0:T(8,128)(2,1)S(1)} %collective-permute-done.5.inside_ref, bf16[2,320,256]{2,1,0:T(8,128)(2,1)S(1)} %collective-permute-done.6.across_ref, ...), custom_call_target="tpu_custom_call" | custom-call | flops 2936012800 | bytes 1048576 | tf_op jit(solution)/shard_map/last/pallas_call | solution.py:453
Async XLA Ops:
  2.0 4.7 %collective-permute-start = (bf16[2,320,128]{2,1,0:T(8,128)(2,1)S(1)}, bf16[2,320,128]{2,1,0:T(8,128)(2,1)S(1)}, u32[]{:S(2)}, u32[]{:S(2)}) collective-permute-start(bf16[2,320,128]{2,1,0:T(8,128)(2,1)S(1)} %get-tuple-element.26), channel_id=1, source_target_pairs={{0,1},{1,0},{2,3},{3,2},{4,5},{5,4},{6,7},{7,6},{8,9},{9,8},{10,11... | collective-permute-start | bytes 491528 | tf_op jit(solution)/shard_map/ppermute | solution.py:373
  2.8 7.5 %collective-permute-start.1 = (bf16[2,320,128]{2,1,0:T(8,128)(2,1)S(1)}, bf16[2,320,128]{2,1,0:T(8,128)(2,1)S(1)}, u32[]{:S(2)}, u32[]{:S(2)}) collective-permute-start(bf16[2,320,128]{2,1,0:T(8,128)(2,1)S(1)} %get-tuple-element.27), channel_id=1, source_target_pairs={{3,4},{4,3},{7,8},{8,7},{11,12},{12,11},{15,0},{0,15},{19,20},{20,... | collective-permute-start | bytes 491528 | tf_op jit(solution)/shard_map/ppermute | solution.py:374
  12.8 20.0 %collective-permute-start.3 = (bf16[4,320,256]{2,1,0:T(8,128)(2,1)S(1)}, bf16[4,320,256]{2,1,0:T(8,128)(2,1)S(1)}, u32[]{:S(2)}, u32[]{:S(2)}) collective-permute-start(bf16[4,320,256]{2,1,0:T(8,128)(2,1)S(1)} %first.1.first_ref), channel_id=1, source_target_pairs={{6,10},{10,6},{7,11},{11,7},{15,3},{3,15},{4,8},{8,4},{5,9},{9,5},... | collective-permute-start | bytes 1966088 | tf_op jit(solution)/shard_map/ppermute | solution.py:395
  16.0 20.3 %collective-permute-start.2 = (bf16[4,320,256]{2,1,0:T(8,128)(2,1)S(1)}, bf16[4,320,256]{2,1,0:T(8,128)(2,1)S(1)}, u32[]{:S(2)}, u32[]{:S(2)}) collective-permute-start(bf16[4,320,256]{2,1,0:T(8,128)(2,1)S(1)} %first.1.first_ref), channel_id=1, source_target_pairs={{2,6},{6,2},{3,7},{7,3},{0,4},{4,0},{1,5},{5,1},{8,12},{12,8},{9,1... | collective-permute-start | bytes 1966088 | tf_op jit(solution)/shard_map/ppermute | solution.py:396
  32.7 3.5 %collective-permute-start.4 = (bf16[4,320,256]{2,1,0:T(8,128)(2,1)S(1)}, bf16[4,320,256]{2,1,0:T(8,128)(2,1)S(1)}, u32[]{:S(2)}, u32[]{:S(2)}) collective-permute-start(bf16[4,320,256]{2,1,0:T(8,128)(2,1)S(1)} %collective-permute-done.3.first_swap), channel_id=1, source_target_pairs={{13,2},{1,14},{29,18},{17,30}} | collective-permute-start | bytes 1966088 | tf_op jit(solution)/shard_map/ppermute | solution.py:427
  37.3 9.3 %collective-permute-start.6 = (bf16[2,320,256]{2,1,0:T(8,128)(2,1)S(1)}, bf16[2,320,256]{2,1,0:T(8,128)(2,1)S(1)}, u32[]{:S(2)}, u32[]{:S(2)}) collective-permute-start(bf16[2,320,256]{2,1,0:T(8,128)(2,1)S(1)} %get-tuple-element.45), channel_id=1, source_target_pairs={{3,4},{4,3},{7,8},{8,7},{11,12},{12,11},{15,0},{0,15},{19,20},{20,... | collective-permute-start | bytes 983048 | tf_op jit(solution)/shard_map/ppermute | solution.py:440
  39.4 7.2 %collective-permute-start.5 = (bf16[2,320,256]{2,1,0:T(8,128)(2,1)S(1)}, bf16[2,320,256]{2,1,0:T(8,128)(2,1)S(1)}, u32[]{:S(2)}, u32[]{:S(2)}) collective-permute-start(bf16[2,320,256]{2,1,0:T(8,128)(2,1)S(1)} %get-tuple-element.40.refs_1_), channel_id=1, source_target_pairs={{0,1},{1,0},{2,3},{3,2},{4,5},{5,4},{6,7},{7,6},{8,9},{9,8},{10,11... | collective-permute-start | bytes 983048 | tf_op jit(solution)/shard_map/ppermute | solution.py:441

commit v8 on v7

--- a/solution.py
+++ b/solution.py
@@ -273,24 +273,22 @@
     for row_phase in range(2):
         phases = []
         for column_phase in range(2):
-            total = None
-            for tap in range(2):
-                sides = [
-                    middle_field[
-                        (row_phase + tap + at) * block
-                        + column_phase * inner : (row_phase + tap + at) * block
-                        + (column_phase + 2) * inner,
-                        :,
-                    ]
-                    for at in range(rows // 2)
-                ]
-                part = dot(
-                    phase_weight[
-                        2 * row_phase + column_phase, :, tap * 2 * inner : (tap + 1) * 2 * inner
+            start = column_phase * inner
+            taps = [
+                jnp.concatenate(
+                    [
+                        middle_field[
+                            (row_phase + tap + at) * block + start : (row_phase + tap + at) * block
+                            + start + 2 * inner,
+                            :,
+                        ]
+                        for at in range(rows // 2)
                     ],
-                    jnp.concatenate(sides, axis=1),
+                    axis=1,
                 )
-                total = part if total is None else total + part
+                for tap in range(2)
+            ]
+            total = dot(phase_weight[2 * row_phase + column_phase], jnp.concatenate(taps, axis=0))
             phases.append(total)
         for at in range(rows // 2):
             row = 2 * at + row_phase

time: 51.6 us -> 51.4 us (level)
  no operation moved by 1% of the time
where the time goes in v8:
time: 51.4 us; the launch traced here: 51.2 us
  Pallas kernels  20.9 us (41%)
  starting transfers between devices  15.9 us (31%)
  waiting for transfers between devices  14.3 us (28%)
    pallas_call x1, Pallas kernels, body(): call(weights_kernel, 'weights', [((channels, depth), BF16), ((inner, 3 *...  6.91 us
    ppermute x1, starting transfers between devices, body(): second_swap = lax.ppermute(first, 'frames', second_pairs)  6 us
    pallas_call x1, Pallas kernels, body(): call(functools.partial(last_kernel, bands=bands), 'last', [(turned.shape,...  4.62 us
    ppermute x1, waiting for transfers between devices, body(): from_across = lax.ppermute(across_rows, 'frames', across)  4.08 us
    ppermute x1, waiting for transfers between devices, body(): first_swap = lax.ppermute(first, 'frames', first_pairs)  3.83 us
    ppermute x1, waiting for transfers between devices, body(): across_row = lax.ppermute(across_rim, 'frames', across)  3.52 us
    ppermute x1, starting transfers between devices, body(): first_swap = lax.ppermute(first, 'frames', first_pairs)  3.2 us
    ppermute x1, starting transfers between devices, body(): across_row = lax.ppermute(across_rim, 'frames', across)  3.05 us
  transfers between devices with their start and end apart: 7, of which 4 were waited for; matrix products, arithmetic and copies ran while one was open for 0% of the time, Pallas kernels for 21%

profile of v8, /device:TPU:15, one launch (start us, length us, event | category | flops | bytes accessed | tf_op | source)
XLA Modules:
  0.0 51.2 jit_solution(1858466198752808400)
XLA Ops:
  0.0 2.0 %fetch.1 = (bf16[2,320,128]{2,1,0:T(8,128)(2,1)S(1)}, bf16[2,320,128]{2,1,0:T(8,128)(2,1)S(1)}, bf16[2,4,320,128]{3,2,1,0:T(8,128)(2,1)S(1)}, bf16[2880,320]{1,0:T(8,128)(2,1)S(1)}) custom-call(bf16[2,4,320,128]{3,2,1,0:T(8,128)(2,1)} %bitcast.10, bf16[2880,320]{1,0:T(8,128)(2,1)} %bitcast.8), custom_call_target="tpu_custom_call" | custom-call | bytes 1048576 | tf_op jit(solution)/shard_map/fetch/pallas_call | solution.py:358
  2.0 0.7 %collective-permute-start = (bf16[2,320,128]{2,1,0:T(8,128)(2,1)S(1)}, bf16[2,320,128]{2,1,0:T(8,128)(2,1)S(1)}, u32[]{:S(2)}, u32[]{:S(2)}) collective-permute-start(bf16[2,320,128]{2,1,0:T(8,128)(2,1)S(1)} %get-tuple-element.26), channel_id=1, source_target_pairs={{0,1},{1,0},{2,3},{3,2},{4,5},{5,4},{6,7},{7,6},{8,9},{9,8},{10,11... | collective-permute-start | bytes 491528 | tf_op jit(solution)/shard_map/ppermute | solution.py:371
  2.8 3.0 %collective-permute-start.1 = (bf16[2,320,128]{2,1,0:T(8,128)(2,1)S(1)}, bf16[2,320,128]{2,1,0:T(8,128)(2,1)S(1)}, u32[]{:S(2)}, u32[]{:S(2)}) collective-permute-start(bf16[2,320,128]{2,1,0:T(8,128)(2,1)S(1)} %get-tuple-element.27), channel_id=1, source_target_pairs={{3,4},{4,3},{7,8},{8,7},{11,12},{12,11},{15,0},{0,15},{19,20},{20,... | collective-permute-start | bytes 491528 | tf_op jit(solution)/shard_map/ppermute | solution.py:372
  5.8 0.9 %prepare.1 = (bf16[320,2880]{1,0:T(8,128)(2,1)S(1)}, bf16[3840,256]{1,0:T(8,128)(2,1)S(1)}) custom-call(bf16[2,4,320,128]{3,2,1,0:T(8,128)(2,1)S(1)} %get-tuple-element.28.latent_ref, bf16[2880,320]{1,0:T(8,128)(2,1)S(1)} %get-tuple-element.29.weight_ref), custom_call_target="tpu_custom_call" | custom-call | flops 167772160 | bytes 1048576 | tf_op jit(solution)/shard_map/prepare/pallas_call | solution.py:373
  6.8 0.0 collective-permute-done.inside_ref
  6.8 3.5 %collective-permute-done.1.across_ref = bf16[2,320,128]{2,1,0:T(8,128)(2,1)S(1)} collective-permute-done((bf16[2,320,128]{2,1,0:T(8,128)(2,1)S(1)}, bf16[2,320,128]{2,1,0:T(8,128)(2,1)S(1)}, u32[]{:S(2)}, u32[]{:S(2)}) %collective-permute-start.1) | collective-permute-done | bytes 163872 | tf_op jit(solution)/shard_map/ppermute | solution.py:372
  10.3 2.5 %first.1.first_ref = bf16[4,320,256]{2,1,0:T(8,128)(2,1)S(1)} custom-call(bf16[2,320,128]{2,1,0:T(8,128)(2,1)S(1)} %collective-permute-done.inside_ref, bf16[2,320,128]{2,1,0:T(8,128)(2,1)S(1)} %collective-permute-done.1.across_ref, bf16[320,2880]{1,0:T(8,128)(2,1)S(1)} %get-tuple-element.30.turned_ref, bf16[3840,256]{1,0:T(8,128)(2,1)S(1)} %get-tuple-element.31.field_ref), custom_call_target="tpu_custom_call" | custom-call | flops 1887436800 | bytes 1048576 | tf_op jit(solution)/shard_map/first/pallas_call | solution.py:381
  12.8 3.2 %collective-permute-start.3 = (bf16[4,320,256]{2,1,0:T(8,128)(2,1)S(1)}, bf16[4,320,256]{2,1,0:T(8,128)(2,1)S(1)}, u32[]{:S(2)}, u32[]{:S(2)}) collective-permute-start(bf16[4,320,256]{2,1,0:T(8,128)(2,1)S(1)} %first.1.first_ref), channel_id=1, source_target_pairs={{6,10},{10,6},{7,11},{11,7},{15,3},{3,15},{4,8},{8,4},{5,9},{9,5},... | collective-permute-start | bytes 1966088 | tf_op jit(solution)/shard_map/ppermute | solution.py:393
  16.0 6.0 %collective-permute-start.2 = (bf16[4,320,256]{2,1,0:T(8,128)(2,1)S(1)}, bf16[4,320,256]{2,1,0:T(8,128)(2,1)S(1)}, u32[]{:S(2)}, u32[]{:S(2)}) collective-permute-start(bf16[4,320,256]{2,1,0:T(8,128)(2,1)S(1)} %first.1.first_ref), channel_id=1, source_target_pairs={{2,6},{6,2},{3,7},{7,3},{0,4},{4,0},{1,5},{5,1},{8,12},{12,8},{9,1... | collective-permute-start | bytes 1966088 | tf_op jit(solution)/shard_map/ppermute | solution.py:394
  22.0 6.9 %weights.1 = (bf16[320,960]{1,0:T(8,128)(2,1)S(1)}, bf16[640,2880]{1,0:T(8,128)(2,1)S(1)}, bf16[320,2880]{1,0:T(8,128)(2,1)S(1)}, bf16[4,320,2560]{2,1,0:T(8,128)(2,1)S(1)}) custom-call(bf16[960,320]{1,0:T(8,128)(2,1)} %bitcast.9, bf16[2880,640]{1,0:T(8,128)(2,1)} %bitcast.7, bf16[3,3,320,960]{3,2,1,0:T(8,128)(2,1)} %bitcast.6), custom_call_target="tpu_custom_call" | custom-call | flops 2000000000 | bytes 1048576 | tf_op jit(solution)/shard_map/weights/pallas_call | solution.py:404
  28.9 3.8 %collective-permute-done.3.first_swap = bf16[4,320,256]{2,1,0:T(8,128)(2,1)S(1)} collective-permute-done((bf16[4,320,256]{2,1,0:T(8,128)(2,1)S(1)}, bf16[4,320,256]{2,1,0:T(8,128)(2,1)S(1)}, u32[]{:S(2)}, u32[]{:S(2)}) %collective-permute-start.3) | collective-permute-done | bytes 655392 | tf_op jit(solution)/shard_map/ppermute | solution.py:393
  32.7 0.7 %collective-permute-start.4 = (bf16[4,320,256]{2,1,0:T(8,128)(2,1)S(1)}, bf16[4,320,256]{2,1,0:T(8,128)(2,1)S(1)}, u32[]{:S(2)}, u32[]{:S(2)}) collective-permute-start(bf16[4,320,256]{2,1,0:T(8,128)(2,1)S(1)} %collective-permute-done.3.first_swap), channel_id=1, source_target_pairs={{13,2},{1,14},{29,18},{17,30}} | collective-permute-start | bytes 1966088 | tf_op jit(solution)/shard_map/ppermute | solution.py:425
  33.4 2.8 %collective-permute-done.2.second_swap = bf16[4,320,256]{2,1,0:T(8,128)(2,1)S(1)} collective-permute-done((bf16[4,320,256]{2,1,0:T(8,128)(2,1)S(1)}, bf16[4,320,256]{2,1,0:T(8,128)(2,1)S(1)}, u32[]{:S(2)}, u32[]{:S(2)}) %collective-permute-start.2) | collective-permute-done | bytes 655392 | tf_op jit(solution)/shard_map/ppermute | solution.py:394
  36.3 0.0 collective-permute-done.4.relayed_ref
  36.3 1.0 %skip.1 = (bf16[4,320,256]{2,1,0:T(8,128)(2,1)S(1)}, bf16[2,320,256]{2,1,0:T(8,128)(2,1)S(1)}, bf16[2,320,256]{2,1,0:T(8,128)(2,1)S(1)}) custom-call(bf16[4,320,256]{2,1,0:T(8,128)(2,1)S(1)} %first.1.first_ref, bf16[4,320,256]{2,1,0:T(8,128)(2,1)S(1)} %collective-permute-done.2.second_swap, bf16[4,320,256]{2,1,0:T(8,128)(2,1)S(1)} %collective-permute-done.3.first_swap, ...), custom_call_target="tpu_custom_call" | custom-call | flops 629145600 | bytes 1048576 | tf_op jit(solution)/shard_map/skip/pallas_call | solution.py:426
  37.3 2.1 %collective-permute-start.6 = (bf16[2,320,256]{2,1,0:T(8,128)(2,1)S(1)}, bf16[2,320,256]{2,1,0:T(8,128)(2,1)S(1)}, u32[]{:S(2)}, u32[]{:S(2)}) collective-permute-start(bf16[2,320,256]{2,1,0:T(8,128)(2,1)S(1)} %get-tuple-element.45), channel_id=1, source_target_pairs={{3,4},{4,3},{7,8},{8,7},{11,12},{12,11},{15,0},{0,15},{19,20},{20,... | collective-permute-start | bytes 983048 | tf_op jit(solution)/shard_map/ppermute | solution.py:438
  39.4 0.1 collective-permute-start.5
  39.5 3.0 %own_rows.1 = (f32[4,320,256]{2,1,0:T(8,128)S(1)}, f32[640,512]{1,0:T(8,128)S(1)}) custom-call(bf16[4,320,256]{2,1,0:T(8,128)(2,1)S(1)} %get-tuple-element.39.refs_0_, bf16[2,320,256]{2,1,0:T(8,128)(2,1)S(1)} %get-tuple-element.40.refs_1_, bf16[640,2880]{1,0:T(8,128)(2,1)S(1)} %get-tuple-element.41.refs_2_.mid_ref, ...), custom_call_target="tpu_custom_call" | custom-call | flops 2516582400 | bytes 1048576 | tf_op jit(solution)/shard_map/own_rows/pallas_call | solution.py:441
  42.5 4.1 %collective-permute-done.6.across_ref = bf16[2,320,256]{2,1,0:T(8,128)(2,1)S(1)} collective-permute-done((bf16[2,320,256]{2,1,0:T(8,128)(2,1)S(1)}, bf16[2,320,256]{2,1,0:T(8,128)(2,1)S(1)}, u32[]{:S(2)}, u32[]{:S(2)}) %collective-permute-start.6) | collective-permute-done | bytes 327712 | tf_op jit(solution)/shard_map/ppermute | solution.py:438
  46.6 0.0 collective-permute-done.5.inside_ref
  46.6 4.6 %last.1 = bf16[2,4,320,128]{3,2,1,0:T(8,128)(2,1)} custom-call(f32[4,320,256]{2,1,0:T(8,128)S(1)} %get-tuple-element.43.mixed_ref, f32[640,512]{1,0:T(8,128)S(1)} %get-tuple-element.44.middle_ref, bf16[2,320,256]{2,1,0:T(8,128)(2,1)S(1)} %collective-permute-done.5.inside_ref, bf16[2,320,256]{2,1,0:T(8,128)(2,1)S(1)} %collective-permute-done.6.across_ref, ...), custom_call_target="tpu_custom_call" | custom-call | flops 2936012800 | bytes 1048576 | tf_op jit(solution)/shard_map/last/pallas_call | solution.py:451
Async XLA Ops:
  2.0 4.7 %collective-permute-start = (bf16[2,320,128]{2,1,0:T(8,128)(2,1)S(1)}, bf16[2,320,128]{2,1,0:T(8,128)(2,1)S(1)}, u32[]{:S(2)}, u32[]{:S(2)}) collective-permute-start(bf16[2,320,128]{2,1,0:T(8,128)(2,1)S(1)} %get-tuple-element.26), channel_id=1, source_target_pairs={{0,1},{1,0},{2,3},{3,2},{4,5},{5,4},{6,7},{7,6},{8,9},{9,8},{10,11... | collective-permute-start | bytes 491528 | tf_op jit(solution)/shard_map/ppermute | solution.py:371
  2.8 7.5 %collective-permute-start.1 = (bf16[2,320,128]{2,1,0:T(8,128)(2,1)S(1)}, bf16[2,320,128]{2,1,0:T(8,128)(2,1)S(1)}, u32[]{:S(2)}, u32[]{:S(2)}) collective-permute-start(bf16[2,320,128]{2,1,0:T(8,128)(2,1)S(1)} %get-tuple-element.27), channel_id=1, source_target_pairs={{3,4},{4,3},{7,8},{8,7},{11,12},{12,11},{15,0},{0,15},{19,20},{20,... | collective-permute-start | bytes 491528 | tf_op jit(solution)/shard_map/ppermute | solution.py:372
  12.8 20.0 %collective-permute-start.3 = (bf16[4,320,256]{2,1,0:T(8,128)(2,1)S(1)}, bf16[4,320,256]{2,1,0:T(8,128)(2,1)S(1)}, u32[]{:S(2)}, u32[]{:S(2)}) collective-permute-start(bf16[4,320,256]{2,1,0:T(8,128)(2,1)S(1)} %first.1.first_ref), channel_id=1, source_target_pairs={{6,10},{10,6},{7,11},{11,7},{15,3},{3,15},{4,8},{8,4},{5,9},{9,5},... | collective-permute-start | bytes 1966088 | tf_op jit(solution)/shard_map/ppermute | solution.py:393
  16.0 20.3 %collective-permute-start.2 = (bf16[4,320,256]{2,1,0:T(8,128)(2,1)S(1)}, bf16[4,320,256]{2,1,0:T(8,128)(2,1)S(1)}, u32[]{:S(2)}, u32[]{:S(2)}) collective-permute-start(bf16[4,320,256]{2,1,0:T(8,128)(2,1)S(1)} %first.1.first_ref), channel_id=1, source_target_pairs={{2,6},{6,2},{3,7},{7,3},{0,4},{4,0},{1,5},{5,1},{8,12},{12,8},{9,1... | collective-permute-start | bytes 1966088 | tf_op jit(solution)/shard_map/ppermute | solution.py:394
  32.7 3.5 %collective-permute-start.4 = (bf16[4,320,256]{2,1,0:T(8,128)(2,1)S(1)}, bf16[4,320,256]{2,1,0:T(8,128)(2,1)S(1)}, u32[]{:S(2)}, u32[]{:S(2)}) collective-permute-start(bf16[4,320,256]{2,1,0:T(8,128)(2,1)S(1)} %collective-permute-done.3.first_swap), channel_id=1, source_target_pairs={{13,2},{1,14},{29,18},{17,30}} | collective-permute-start | bytes 1966088 | tf_op jit(solution)/shard_map/ppermute | solution.py:425
  37.3 9.3 %collective-permute-start.6 = (bf16[2,320,256]{2,1,0:T(8,128)(2,1)S(1)}, bf16[2,320,256]{2,1,0:T(8,128)(2,1)S(1)}, u32[]{:S(2)}, u32[]{:S(2)}) collective-permute-start(bf16[2,320,256]{2,1,0:T(8,128)(2,1)S(1)} %get-tuple-element.45), channel_id=1, source_target_pairs={{3,4},{4,3},{7,8},{8,7},{11,12},{12,11},{15,0},{0,15},{19,20},{20,... | collective-permute-start | bytes 983048 | tf_op jit(solution)/shard_map/ppermute | solution.py:438
  39.4 7.2 %collective-permute-start.5 = (bf16[2,320,256]{2,1,0:T(8,128)(2,1)S(1)}, bf16[2,320,256]{2,1,0:T(8,128)(2,1)S(1)}, u32[]{:S(2)}, u32[]{:S(2)}) collective-permute-start(bf16[2,320,256]{2,1,0:T(8,128)(2,1)S(1)} %get-tuple-element.40.refs_1_), channel_id=1, source_target_pairs={{0,1},{1,0},{2,3},{3,2},{4,5},{5,4},{6,7},{7,6},{8,9},{9,8},{10,11... | collective-permute-start | bytes 983048 | tf_op jit(solution)/shard_map/ppermute | solution.py:439

commit v9 on v8

--- a/solution.py
+++ b/solution.py
@@ -166,28 +166,13 @@
                     )
 
 
-def skip_kernel(
-    first_ref, second_swap, first_swap, relayed_ref, weight_ref, skip_ref, inside_ref, across_ref,
-    *, bands
-):
+def skip_rows(first_ref, before_of, after_of, weight_ref, skip_ref, inside_ref, across_ref, odd_band):
     rows, _, wide = skip_ref.shape
     lanes = wide // 2
-    band, frame = place(bands)
-    odd_band, odd_frame = lax.rem(band, 2) == 1, lax.rem(frame, 2) == 1
-    is_relayed = jnp.logical_and(jnp.logical_and(frame < 2, band < bands // 2), lax.rem(band, 2) == 0)
-    upper = band < bands // 2
-    first_is_before = upper == odd_frame
-    is_host = jnp.logical_and(
-        jnp.logical_not(upper), jnp.logical_or(frame == 0, frame == FRAMES - 1)
-    )
     skips = []
     for row in range(rows):
-        centre, second = first_ref[row], second_swap[row]
-        first = jnp.where(is_host, jnp.zeros((), BF16), first_swap[row])
-        first = jnp.where(is_relayed, relayed_ref[row], first)
-        before = jnp.where(first_is_before, first, second)
-        after = jnp.where(first_is_before, second, first)
-        stacked = jnp.concatenate([before, centre, after], axis=0)
+        centre = first_ref[row]
+        stacked = jnp.concatenate([before_of(row), centre, after_of(row)], axis=0)
         skip = (centre.astype(F32) + dot(weight_ref[...], stacked)).astype(BF16)
         skip_ref[row] = skip
         skips.append(skip)
@@ -199,6 +184,47 @@
         span = slice(pooled_row * lanes, (pooled_row + 1) * lanes)
         inside_ref[1, :, span] = pooled
         across_ref[1, :, span] = pooled
+
+
+def skip_lower_kernel(
+    first_ref, outer_ref, middle_ref, weight_ref, skip_ref, inside_ref, across_ref, *, bands
+):
+    band, frame = place(bands)
+    odd_frame = lax.rem(frame, 2) == 1
+    is_host = jnp.logical_or(frame == 0, frame == FRAMES - 1)
+
+    def middle(row):
+        return jnp.where(is_host, jnp.zeros((), BF16), middle_ref[row])
+
+    @pl.when(band >= bands // 2)
+    def _():
+        skip_rows(
+            first_ref,
+            lambda row: jnp.where(odd_frame, outer_ref[row], middle(row)),
+            lambda row: jnp.where(odd_frame, middle(row), outer_ref[row]),
+            weight_ref, skip_ref, inside_ref, across_ref, lax.rem(band, 2) == 1,
+        )
+
+
+def skip_upper_kernel(
+    first_ref, middle_ref, outer_ref, relayed_ref, weight_ref, old_skip, old_inside,
+    skip_ref, inside_ref, across_ref, *, bands
+):
+    band, frame = place(bands)
+    odd_frame = lax.rem(frame, 2) == 1
+    is_relayed = jnp.logical_and(frame < 2, lax.rem(band, 2) == 0)
+
+    def outer(row):
+        return jnp.where(is_relayed, relayed_ref[row], outer_ref[row])
+
+    @pl.when(band < bands // 2)
+    def _():
+        skip_rows(
+            first_ref,
+            lambda row: jnp.where(odd_frame, outer(row), middle_ref[row]),
+            lambda row: jnp.where(odd_frame, middle_ref[row], outer(row)),
+            weight_ref, skip_ref, inside_ref, across_ref, lax.rem(band, 2) == 1,
+        )
 
 
 def own_kernel(skip_ref, pair_ref, mid_ref, skip_weight, mixed_ref, middle_ref, field, pooled, *, half):
@@ -225,8 +251,8 @@
 
 
 def last_kernel(
-    mixed_ref, middle_ref, inside_ref, across_ref, mid_ref, skip_weight, phase_weight, field_ref,
-    out_ref, low_field, high_field, cross_field, rims, middle_field, *, bands
+    mixed_ref, middle_ref, inside_ref, lower_ref, upper_ref, mid_ref, skip_weight, phase_weight,
+    field_ref, out_ref, low_field, high_field, cross_field, rims, middle_field, *, bands
 ):
     rows, channels, wide = mixed_ref.shape
     clips, _, _, width = out_ref.shape
@@ -236,8 +262,9 @@
 
     band = place(bands)[0]
     odd = lax.rem(band, 2) == 1
-    lows = [jnp.where(odd, inside_ref[at], across_ref[at]) for at in range(2)]
-    highs = [jnp.where(odd, across_ref[at], inside_ref[at]) for at in range(2)]
+    across = [lower_ref[at] + upper_ref[at] for at in range(2)]
+    lows = [jnp.where(odd, inside_ref[at], across[at]) for at in range(2)]
+    highs = [jnp.where(odd, across[at], inside_ref[at]) for at in range(2)]
     for target, pair, inward in ((low_field, lows[1], 1), (high_field, highs[1], 0)):
         for at in range(2):
             row = pair[:, at * lanes : (at + 1) * lanes].astype(F32)
@@ -387,12 +414,11 @@
         flops=2 * rows * wide * channels * 3 * depth,
         inputs=[whole] * 4,
     )(*in_vmem(inside_row, across_row, in_turned, field))
-    of_bands = lambda pairs, upper: [pair for pair in pairs if (band_of(pair[0]) < offset) == upper]
-    first_pairs = of_bands(outer_frames, True) + of_bands(middle_frames, False) + hops
-    second_pairs = of_bands(middle_frames, True) + of_bands(outer_frames, False)
-    first_swap = lax.ppermute(first, "frames", first_pairs)
-    second_swap = lax.ppermute(first, "frames", second_pairs)
-
+    of_half = lambda pairs, upper: [pair for pair in pairs if (band_of(pair[0]) < offset) == upper]
+    lower_outer = lax.ppermute(first, "frames", of_half(outer_frames, False))
+    lower_middle = lax.ppermute(first, "frames", of_half(middle_frames, False) + hops)
+    upper_middle = lax.ppermute(first, "frames", of_half(middle_frames, True))
+    upper_outer = lax.ppermute(first, "frames", of_half(outer_frames, True))
     time_rows, mid_rows, up_rows, first = lax.optimization_barrier(
         (
             time_weight.reshape(depth, channels),
@@ -421,21 +447,32 @@
         inputs=[anywhere] * 3,
     )(in_hbm(time_rows), in_hbm(mid_rows), in_hbm(up_rows))
 
-    hopped, time_turned = lax.optimization_barrier((first_swap, time_turned))
+    hopped, time_turned = lax.optimization_barrier((lower_middle, time_turned))
     relayed = lax.ppermute(hopped, "frames", relays)
-    skip, inside_rows, across_rows = call(
-        functools.partial(skip_kernel, bands=bands),
-        "skip",
-        [
-            ((rows, channels, wide), BF16),
-            ((2, channels, wide), BF16),
-            ((2, channels, wide), BF16),
-        ],
+    skip_shapes = [
+        ((rows, channels, wide), BF16),
+        ((2, channels, wide), BF16),
+        ((2, channels, wide), BF16),
+    ]
+    skip, inside_rows, lower_rows = call(
+        functools.partial(skip_lower_kernel, bands=bands),
+        "skip_lower",
+        skip_shapes,
         8,
         flops=2 * rows * wide * depth * channels,
-        inputs=[whole] * 5,
-    )(*in_vmem(first, second_swap, first_swap, relayed, time_turned))
-    from_across = lax.ppermute(across_rows, "frames", across)
+        inputs=[whole] * 4,
+    )(*in_vmem(first, lower_outer, lower_middle, time_turned))
+    lower_across = lax.ppermute(lower_rows, "frames", of_half(across, False))
+    skip, inside_rows, upper_rows = call(
+        functools.partial(skip_upper_kernel, bands=bands),
+        "skip_upper",
+        skip_shapes,
+        8,
+        flops=2 * rows * wide * depth * channels,
+        inputs=[whole] * 7,
+        aliases={5: 0, 6: 1},
+    )(*in_vmem(first, upper_middle, upper_outer, relayed, time_turned, skip, inside_rows))
+    upper_across = lax.ppermute(upper_rows, "frames", of_half(across, True))
     from_inside = lax.ppermute(inside_rows, "frames", inside)
 
     mixed, middle = call(
@@ -462,10 +499,10 @@
         ],
         flops=2 * wide * (3 * depth * inner + 2 * depth * channels + rows * 4 * inner * channels),
         kept=False,
-        inputs=[whole] * 8,
+        inputs=[whole] * 9,
     )(
         *in_vmem(
-            mixed, middle, from_inside, from_across, mid_turned, skip_weight, phase_weight, field
+            mixed, middle, from_inside, lower_across, upper_across, mid_turned, skip_weight, phase_weight, field
         ),
     )
     return jnp.swapaxes(out, 2, 3)

time: 51.4 us -> 50.4 us (0.981)
  the two profiles are of different devices: /device:TPU:15 before, /device:TPU:18 now
where the time goes in v9:
time: 50.4 us; the launch traced here: 50.2 us
  Pallas kernels  21 us (42%)
  starting transfers between devices  16.5 us (33%)
  waiting for transfers between devices  12.5 us (25%)
    ppermute x1, waiting for transfers between devices, body(): upper_across = lax.ppermute(upper_rows, 'frames', of_half(across, True))  7.01 us
    pallas_call x1, Pallas kernels, body(): call(weights_kernel, 'weights', [((channels, depth), BF16), ((inner, 3 *...  6.91 us
    ppermute x1, starting transfers between devices, body(): lower_across = lax.ppermute(lower_rows, 'frames', of_half(across, False))  5.15 us
    pallas_call x1, Pallas kernels, body(): call(functools.partial(last_kernel, bands=bands), 'last', [(turned.shape,...  4.64 us
    ppermute x1, starting transfers between devices, body(): across_row = lax.ppermute(across_rim, 'frames', across)  3.4 us
    ppermute x1, waiting for transfers between devices, body(): across_row = lax.ppermute(across_rim, 'frames', across)  3.17 us
    pallas_call x1, Pallas kernels, body(): call(lambda *refs: own_kernel(*refs, half=width // 2), 'own_rows', [((row...  3.03 us
    pallas_call x1, Pallas kernels, body(): call(functools.partial(first_kernel, bands=bands), 'first', [((rows, chan...  2.45 us
  transfers between devices with their start and end apart: 10, of which 3 were waited for; matrix products, arithmetic and copies ran while one was open for 0% of the time, Pallas kernels for 24%

profile of v9, /device:TPU:18, one launch (start us, length us, event | category | flops | bytes accessed | tf_op | source)
XLA Modules:
  0.0 50.2 jit_solution(17682274817789945083)
XLA Ops:
  0.0 2.0 %fetch.1 = (bf16[2,320,128]{2,1,0:T(8,128)(2,1)S(1)}, bf16[2,320,128]{2,1,0:T(8,128)(2,1)S(1)}, bf16[2,4,320,128]{3,2,1,0:T(8,128)(2,1)S(1)}, bf16[2880,320]{1,0:T(8,128)(2,1)S(1)}) custom-call(bf16[2,4,320,128]{3,2,1,0:T(8,128)(2,1)} %bitcast.10, bf16[2880,320]{1,0:T(8,128)(2,1)} %bitcast.8), custom_call_target="tpu_custom_call" | custom-call | bytes 1048576 | tf_op jit(solution)/shard_map/fetch/pallas_call | solution.py:385
  2.0 0.1 collective-permute-start
  2.1 3.4 %collective-permute-start.1 = (bf16[2,320,128]{2,1,0:T(8,128)(2,1)S(1)}, bf16[2,320,128]{2,1,0:T(8,128)(2,1)S(1)}, u32[]{:S(2)}, u32[]{:S(2)}) collective-permute-start(bf16[2,320,128]{2,1,0:T(8,128)(2,1)S(1)} %get-tuple-element.30), channel_id=1, source_target_pairs={{3,4},{4,3},{7,8},{8,7},{11,12},{12,11},{15,0},{0,15},{19,20},{20,... | collective-permute-start | bytes 491528 | tf_op jit(solution)/shard_map/ppermute | solution.py:399
  5.5 0.9 %prepare.1 = (bf16[320,2880]{1,0:T(8,128)(2,1)S(1)}, bf16[3840,256]{1,0:T(8,128)(2,1)S(1)}) custom-call(bf16[2,4,320,128]{3,2,1,0:T(8,128)(2,1)S(1)} %get-tuple-element.31.latent_ref, bf16[2880,320]{1,0:T(8,128)(2,1)S(1)} %get-tuple-element.32.weight_ref), custom_call_target="tpu_custom_call" | custom-call | flops 167772160 | bytes 1048576 | tf_op jit(solution)/shard_map/prepare/pallas_call | solution.py:400
  6.5 0.0 collective-permute-done.inside_ref
  6.5 3.2 %collective-permute-done.1.across_ref = bf16[2,320,128]{2,1,0:T(8,128)(2,1)S(1)} collective-permute-done((bf16[2,320,128]{2,1,0:T(8,128)(2,1)S(1)}, bf16[2,320,128]{2,1,0:T(8,128)(2,1)S(1)}, u32[]{:S(2)}, u32[]{:S(2)}) %collective-permute-start.1) | collective-permute-done | bytes 163872 | tf_op jit(solution)/shard_map/ppermute | solution.py:399
  9.7 2.5 %first.1.first_ref = bf16[4,320,256]{2,1,0:T(8,128)(2,1)S(1)} custom-call(bf16[2,320,128]{2,1,0:T(8,128)(2,1)S(1)} %collective-permute-done.inside_ref, bf16[2,320,128]{2,1,0:T(8,128)(2,1)S(1)} %collective-permute-done.1.across_ref, bf16[320,2880]{1,0:T(8,128)(2,1)S(1)} %get-tuple-element.33.turned_ref, bf16[3840,256]{1,0:T(8,128)(2,1)S(1)} %get-tuple-element.34.field_ref), custom_call_target="tpu_custom_call" | custom-call | flops 1887436800 | bytes 1048576 | tf_op jit(solution)/shard_map/first/pallas_call | solution.py:408
  12.1 2.4 %collective-permute-start.4 = (bf16[4,320,256]{2,1,0:T(8,128)(2,1)S(1)}, bf16[4,320,256]{2,1,0:T(8,128)(2,1)S(1)}, u32[]{:S(2)}, u32[]{:S(2)}) collective-permute-start(bf16[4,320,256]{2,1,0:T(8,128)(2,1)S(1)} %first.1.first_ref), channel_id=1, source_target_pairs={{4,8},{8,4},{5,9},{9,5},{14,13},{2,1},{20,24},{24,20},{21,25},{25,... | collective-permute-start | bytes 1966088 | tf_op jit(solution)/shard_map/ppermute | solution.py:419
  14.5 1.9 %collective-permute-start.6 = (bf16[4,320,256]{2,1,0:T(8,128)(2,1)S(1)}, bf16[4,320,256]{2,1,0:T(8,128)(2,1)S(1)}, u32[]{:S(2)}, u32[]{:S(2)}) collective-permute-start(bf16[4,320,256]{2,1,0:T(8,128)(2,1)S(1)} %first.1.first_ref), channel_id=1, source_target_pairs={{0,4},{4,0},{1,5},{5,1},{8,12},{12,8},{9,13},{13,9},{16,20},{20,16... | collective-permute-start | bytes 1966088 | tf_op jit(solution)/shard_map/ppermute | solution.py:418
  16.4 0.7 %collective-permute-start.3 = (bf16[4,320,256]{2,1,0:T(8,128)(2,1)S(1)}, bf16[4,320,256]{2,1,0:T(8,128)(2,1)S(1)}, u32[]{:S(2)}, u32[]{:S(2)}) collective-permute-start(bf16[4,320,256]{2,1,0:T(8,128)(2,1)S(1)} %first.1.first_ref), channel_id=1, source_target_pairs={{6,10},{10,6},{7,11},{11,7},{15,3},{3,15},{22,26},{26,22},{23,27},... | collective-permute-start | bytes 1966088 | tf_op jit(solution)/shard_map/ppermute | solution.py:421
  17.1 0.7 %collective-permute-start.2 = (bf16[4,320,256]{2,1,0:T(8,128)(2,1)S(1)}, bf16[4,320,256]{2,1,0:T(8,128)(2,1)S(1)}, u32[]{:S(2)}, u32[]{:S(2)}) collective-permute-start(bf16[4,320,256]{2,1,0:T(8,128)(2,1)S(1)} %first.1.first_ref), channel_id=1, source_target_pairs={{2,6},{6,2},{3,7},{7,3},{18,22},{22,18},{19,23},{23,19}} | collective-permute-start | bytes 1966088 | tf_op jit(solution)/shard_map/ppermute | solution.py:420
  17.8 6.9 %weights.1 = (bf16[320,960]{1,0:T(8,128)(2,1)S(1)}, bf16[640,2880]{1,0:T(8,128)(2,1)S(1)}, bf16[320,2880]{1,0:T(8,128)(2,1)S(1)}, bf16[4,320,2560]{2,1,0:T(8,128)(2,1)S(1)}) custom-call(bf16[960,320]{1,0:T(8,128)(2,1)} %bitcast.9, bf16[2880,640]{1,0:T(8,128)(2,1)} %bitcast.7, bf16[3,3,320,960]{3,2,1,0:T(8,128)(2,1)} %bitcast.6), custom_call_target="tpu_custom_call" | custom-call | flops 2000000000 | bytes 1048576 | tf_op jit(solution)/shard_map/weights/pallas_call | solution.py:430
  24.8 2.3 %collective-permute-done.4.middle_ref = bf16[4,320,256]{2,1,0:T(8,128)(2,1)S(1)} collective-permute-done((bf16[4,320,256]{2,1,0:T(8,128)(2,1)S(1)}, bf16[4,320,256]{2,1,0:T(8,128)(2,1)S(1)}, u32[]{:S(2)}, u32[]{:S(2)}) %collective-permute-start.4) | collective-permute-done | bytes 655392 | tf_op jit(solution)/shard_map/ppermute | solution.py:419
  27.0 0.7 %collective-permute-start.5 = (bf16[4,320,256]{2,1,0:T(8,128)(2,1)S(1)}, bf16[4,320,256]{2,1,0:T(8,128)(2,1)S(1)}, u32[]{:S(2)}, u32[]{:S(2)}) collective-permute-start(bf16[4,320,256]{2,1,0:T(8,128)(2,1)S(1)} %collective-permute-done.4.middle_ref), channel_id=1, source_target_pairs={{13,2},{1,14},{29,18},{17,30}} | collective-permute-start | bytes 1966088 | tf_op jit(solution)/shard_map/ppermute | solution.py:451
  27.7 0.0 collective-permute-done.6.outer_ref
  27.7 1.0 %skip_lower.1 = (bf16[4,320,256]{2,1,0:T(8,128)(2,1)S(1)}, bf16[2,320,256]{2,1,0:T(8,128)(2,1)S(1)}, bf16[2,320,256]{2,1,0:T(8,128)(2,1)S(1)}) custom-call(bf16[4,320,256]{2,1,0:T(8,128)(2,1)S(1)} %first.1.first_ref, bf16[4,320,256]{2,1,0:T(8,128)(2,1)S(1)} %collective-permute-done.6.outer_ref, bf16[4,320,256]{2,1,0:T(8,128)(2,1)S(1)} %collective-permute-done.4.middle_ref, ...), custom_call_target="tpu_custom_call" | custom-call | flops 629145600 | bytes 1048576 | tf_op jit(solution)/shard_map/skip_lower/pallas_call | solution.py:457
  28.7 5.1 %collective-permute-start.8 = (bf16[2,320,256]{2,1,0:T(8,128)(2,1)S(1)}, bf16[2,320,256]{2,1,0:T(8,128)(2,1)S(1)}, u32[]{:S(2)}, u32[]{:S(2)}) collective-permute-start(bf16[2,320,256]{2,1,0:T(8,128)(2,1)S(1)} %get-tuple-element.50), channel_id=1, source_target_pairs={{4,3},{8,7},{12,11},{0,15},{20,19},{24,23},{28,27},{16,31}} | collective-permute-start | bytes 983048 | tf_op jit(solution)/shard_map/ppermute | solution.py:465
  33.9 0.0 collective-permute-done.3.outer_ref
  33.9 0.0 collective-permute-done.2.middle_ref
  33.9 0.0 collective-permute-done.5.relayed_ref
  33.9 1.5 %collective-permute-start.9 = (bf16[2,320,256]{2,1,0:T(8,128)(2,1)S(1)}, bf16[2,320,256]{2,1,0:T(8,128)(2,1)S(1)}, u32[]{:S(2)}, u32[]{:S(2)}) collective-permute-start(bf16[2,320,256]{2,1,0:T(8,128)(2,1)S(1)} %get-tuple-element.51), channel_id=1, source_target_pairs={{3,4},{7,8},{11,12},{15,0},{19,20},{23,24},{27,28},{31,16}} | collective-permute-start | bytes 983048 | tf_op jit(solution)/shard_map/ppermute | solution.py:475
  35.4 0.1 collective-permute-start.7
  35.5 3.0 %own_rows.1 = (f32[4,320,256]{2,1,0:T(8,128)S(1)}, f32[640,512]{1,0:T(8,128)S(1)}) custom-call(bf16[4,320,256]{2,1,0:T(8,128)(2,1)S(1)} %get-tuple-element.44.refs_0_, bf16[2,320,256]{2,1,0:T(8,128)(2,1)S(1)} %get-tuple-element.45.refs_1_, bf16[640,2880]{1,0:T(8,128)(2,1)S(1)} %get-tuple-element.46.refs_2_.mid_ref, ...), custom_call_target="tpu_custom_call" | custom-call | flops 2516582400 | bytes 1048576 | tf_op jit(solution)/shard_map/own_rows/pallas_call | solution.py:478
  38.5 0.0 collective-permute-done.8.lower_ref
  38.5 7.0 %collective-permute-done.9.upper_ref = bf16[2,320,256]{2,1,0:T(8,128)(2,1)S(1)} collective-permute-done((bf16[2,320,256]{2,1,0:T(8,128)(2,1)S(1)}, bf16[2,320,256]{2,1,0:T(8,128)(2,1)S(1)}, u32[]{:S(2)}, u32[]{:S(2)}) %collective-permute-start.9) | collective-permute-done | bytes 327712 | tf_op jit(solution)/shard_map/ppermute | solution.py:475
  45.5 0.0 collective-permute-done.7.inside_ref
  45.6 4.6 %last.1 = bf16[2,4,320,128]{3,2,1,0:T(8,128)(2,1)} custom-call(f32[4,320,256]{2,1,0:T(8,128)S(1)} %get-tuple-element.48.mixed_ref, f32[640,512]{1,0:T(8,128)S(1)} %get-tuple-element.49.middle_ref, bf16[2,320,256]{2,1,0:T(8,128)(2,1)S(1)} %collective-permute-done.7.inside_ref, bf16[2,320,256]{2,1,0:T(8,128)(2,1)S(1)} %collective-permute-done.8.lower_ref, ...), custom_call_target="tpu_custom_call" | custom-call | flops 2936012800 | bytes 1048576 | tf_op jit(solution)/shard_map/last/pallas_call | solution.py:488
  (1 shorter events, 0.0 us)
Async XLA Ops:
  2.0 4.4 %collective-permute-start = (bf16[2,320,128]{2,1,0:T(8,128)(2,1)S(1)}, bf16[2,320,128]{2,1,0:T(8,128)(2,1)S(1)}, u32[]{:S(2)}, u32[]{:S(2)}) collective-permute-start(bf16[2,320,128]{2,1,0:T(8,128)(2,1)S(1)} %get-tuple-element.29), channel_id=1, source_target_pairs={{0,1},{1,0},{2,3},{3,2},{4,5},{5,4},{6,7},{7,6},{8,9},{9,8},{10,11... | collective-permute-start | bytes 491528 | tf_op jit(solution)/shard_map/ppermute | solution.py:398
  2.1 7.5 %collective-permute-start.1 = (bf16[2,320,128]{2,1,0:T(8,128)(2,1)S(1)}, bf16[2,320,128]{2,1,0:T(8,128)(2,1)S(1)}, u32[]{:S(2)}, u32[]{:S(2)}) collective-permute-start(bf16[2,320,128]{2,1,0:T(8,128)(2,1)S(1)} %get-tuple-element.30), channel_id=1, source_target_pairs={{3,4},{4,3},{7,8},{8,7},{11,12},{12,11},{15,0},{0,15},{19,20},{20,... | collective-permute-start | bytes 491528 | tf_op jit(solution)/shard_map/ppermute | solution.py:399
  12.1 14.9 %collective-permute-start.4 = (bf16[4,320,256]{2,1,0:T(8,128)(2,1)S(1)}, bf16[4,320,256]{2,1,0:T(8,128)(2,1)S(1)}, u32[]{:S(2)}, u32[]{:S(2)}) collective-permute-start(bf16[4,320,256]{2,1,0:T(8,128)(2,1)S(1)} %first.1.first_ref), channel_id=1, source_target_pairs={{4,8},{8,4},{5,9},{9,5},{14,13},{2,1},{20,24},{24,20},{21,25},{25,... | collective-permute-start | bytes 1966088 | tf_op jit(solution)/shard_map/ppermute | solution.py:419
  14.5 13.2 %collective-permute-start.6 = (bf16[4,320,256]{2,1,0:T(8,128)(2,1)S(1)}, bf16[4,320,256]{2,1,0:T(8,128)(2,1)S(1)}, u32[]{:S(2)}, u32[]{:S(2)}) collective-permute-start(bf16[4,320,256]{2,1,0:T(8,128)(2,1)S(1)} %first.1.first_ref), channel_id=1, source_target_pairs={{0,4},{4,0},{1,5},{5,1},{8,12},{12,8},{9,13},{13,9},{16,20},{20,16... | collective-permute-start | bytes 1966088 | tf_op jit(solution)/shard_map/ppermute | solution.py:418
  16.4 17.5 %collective-permute-start.3 = (bf16[4,320,256]{2,1,0:T(8,128)(2,1)S(1)}, bf16[4,320,256]{2,1,0:T(8,128)(2,1)S(1)}, u32[]{:S(2)}, u32[]{:S(2)}) collective-permute-start(bf16[4,320,256]{2,1,0:T(8,128)(2,1)S(1)} %first.1.first_ref), channel_id=1, source_target_pairs={{6,10},{10,6},{7,11},{11,7},{15,3},{3,15},{22,26},{26,22},{23,27},... | collective-permute-start | bytes 1966088 | tf_op jit(solution)/shard_map/ppermute | solution.py:421
  17.1 16.8 %collective-permute-start.2 = (bf16[4,320,256]{2,1,0:T(8,128)(2,1)S(1)}, bf16[4,320,256]{2,1,0:T(8,128)(2,1)S(1)}, u32[]{:S(2)}, u32[]{:S(2)}) collective-permute-start(bf16[4,320,256]{2,1,0:T(8,128)(2,1)S(1)} %first.1.first_ref), channel_id=1, source_target_pairs={{2,6},{6,2},{3,7},{7,3},{18,22},{22,18},{19,23},{23,19}} | collective-permute-start | bytes 1966088 | tf_op jit(solution)/shard_map/ppermute | solution.py:420
  27.0 6.9 %collective-permute-start.5 = (bf16[4,320,256]{2,1,0:T(8,128)(2,1)S(1)}, bf16[4,320,256]{2,1,0:T(8,128)(2,1)S(1)}, u32[]{:S(2)}, u32[]{:S(2)}) collective-permute-start(bf16[4,320,256]{2,1,0:T(8,128)(2,1)S(1)} %collective-permute-done.4.middle_ref), channel_id=1, source_target_pairs={{13,2},{1,14},{29,18},{17,30}} | collective-permute-start | bytes 1966088 | tf_op jit(solution)/shard_map/ppermute | solution.py:451
  28.7 9.8 %collective-permute-start.8 = (bf16[2,320,256]{2,1,0:T(8,128)(2,1)S(1)}, bf16[2,320,256]{2,1,0:T(8,128)(2,1)S(1)}, u32[]{:S(2)}, u32[]{:S(2)}) collective-permute-start(bf16[2,320,256]{2,1,0:T(8,128)(2,1)S(1)} %get-tuple-element.50), channel_id=1, source_target_pairs={{4,3},{8,7},{12,11},{0,15},{20,19},{24,23},{28,27},{16,31}} | collective-permute-start | bytes 983048 | tf_op jit(solution)/shard_map/ppermute | solution.py:465
  33.9 11.6 %collective-permute-start.9 = (bf16[2,320,256]{2,1,0:T(8,128)(2,1)S(1)}, bf16[2,320,256]{2,1,0:T(8,128)(2,1)S(1)}, u32[]{:S(2)}, u32[]{:S(2)}) collective-permute-start(bf16[2,320,256]{2,1,0:T(8,128)(2,1)S(1)} %get-tuple-element.51), channel_id=1, source_target_pairs={{3,4},{7,8},{11,12},{15,0},{19,20},{23,24},{27,28},{31,16}} | collective-permute-start | bytes 983048 | tf_op jit(solution)/shard_map/ppermute | solution.py:475
  35.4 10.1 %collective-permute-start.7 = (bf16[2,320,256]{2,1,0:T(8,128)(2,1)S(1)}, bf16[2,320,256]{2,1,0:T(8,128)(2,1)S(1)}, u32[]{:S(2)}, u32[]{:S(2)}) collective-permute-start(bf16[2,320,256]{2,1,0:T(8,128)(2,1)S(1)} %get-tuple-element.45.refs_1_), channel_id=1, source_target_pairs={{0,1},{1,0},{2,3},{3,2},{4,5},{5,4},{6,7},{7,6},{8,9},{9,8},{10,11... | collective-permute-start | bytes 983048 | tf_op jit(solution)/shard_map/ppermute | solution.py:476

commit v10 on v9

--- a/solution.py
+++ b/solution.py
@@ -128,8 +128,8 @@
 
 
 def weights_kernel(
-    time_hbm, mid_hbm, up_hbm, time_out, mid_out, skip_out, phase_out,
-    time_rows, mid_rows, up_rows, sems,
+    time_hbm, mid_hbm, up_hbm, time_out, part_out, rest_out, outer_out, mid_out, skip_out, phase_out,
+    time_rows, mid_rows, up_rows, sems, *, bands
 ):
     taps, inner = mid_rows.shape
     channels = up_rows.shape[2]
@@ -145,6 +145,13 @@
         get.start()
     gets[0].wait()
     time_out[...] = time_rows[...].T
+    odd_frame = lax.rem(place(bands)[1], 2) == 1
+    size = time_rows.shape[1]
+    before, centre, after = [time_rows[at * size : (at + 1) * size, :] for at in range(3)]
+    outer = jnp.where(odd_frame, before, after)
+    part_out[...] = jnp.concatenate([centre, outer], axis=0).T
+    rest_out[...] = jnp.where(odd_frame, after, before).T
+    outer_out[...] = outer.T
     for get, a, b in zip(gets[1:-1], cuts, cuts[1:]):
         get.wait()
         mid_out[:, a:b] = mid_rows[a:b, :].T
@@ -166,19 +173,13 @@
                     )
 
 
-def skip_rows(first_ref, before_of, after_of, weight_ref, skip_ref, inside_ref, across_ref, odd_band):
-    rows, _, wide = skip_ref.shape
-    lanes = wide // 2
-    skips = []
-    for row in range(rows):
-        centre = first_ref[row]
-        stacked = jnp.concatenate([before_of(row), centre, after_of(row)], axis=0)
-        skip = (centre.astype(F32) + dot(weight_ref[...], stacked)).astype(BF16)
+def share_skip(skips, skip_ref, inside_ref, across_ref, odd_band):
+    lanes = skip_ref.shape[2] // 2
+    for row, skip in enumerate(skips):
         skip_ref[row] = skip
-        skips.append(skip)
     inside_ref[0] = jnp.where(odd_band, skips[0], skips[-1])
     across_ref[0] = jnp.where(odd_band, skips[-1], skips[0])
-    for pooled_row in range(rows // 2):
+    for pooled_row in range(len(skips) // 2):
         sums = skips[2 * pooled_row].astype(F32) + skips[2 * pooled_row + 1].astype(F32)
         pooled = ((sums[:, :lanes] + sums[:, lanes:]) * 0.25).astype(BF16)
         span = slice(pooled_row * lanes, (pooled_row + 1) * lanes)
@@ -198,33 +199,44 @@
 
     @pl.when(band >= bands // 2)
     def _():
-        skip_rows(
-            first_ref,
-            lambda row: jnp.where(odd_frame, outer_ref[row], middle(row)),
-            lambda row: jnp.where(odd_frame, middle(row), outer_ref[row]),
-            weight_ref, skip_ref, inside_ref, across_ref, lax.rem(band, 2) == 1,
-        )
+        skips = []
+        for row in range(first_ref.shape[0]):
+            centre, outer, inner = first_ref[row], outer_ref[row], middle(row)
+            before = jnp.where(odd_frame, outer, inner)
+            after = jnp.where(odd_frame, inner, outer)
+            stacked = jnp.concatenate([before, centre, after], axis=0)
+            skips.append((centre.astype(F32) + dot(weight_ref[...], stacked)).astype(BF16))
+        share_skip(skips, skip_ref, inside_ref, across_ref, lax.rem(band, 2) == 1)
+
+
+def skip_part_kernel(first_ref, outer_ref, weight_ref, partial_ref, *, bands):
+    @pl.when(place(bands)[0] < bands // 2)
+    def _():
+        for row in range(first_ref.shape[0]):
+            centre = first_ref[row]
+            stacked = jnp.concatenate([centre, outer_ref[row]], axis=0)
+            partial_ref[row] = centre.astype(F32) + dot(weight_ref[...], stacked)
 
 
 def skip_upper_kernel(
-    first_ref, middle_ref, outer_ref, relayed_ref, weight_ref, old_skip, old_inside,
+    partial_ref, middle_ref, relayed_ref, weight_ref, outer_weight, old_skip, old_inside,
     skip_ref, inside_ref, across_ref, *, bands
 ):
     band, frame = place(bands)
-    odd_frame = lax.rem(frame, 2) == 1
+    upper = band < bands // 2
     is_relayed = jnp.logical_and(frame < 2, lax.rem(band, 2) == 0)
 
-    def outer(row):
-        return jnp.where(is_relayed, relayed_ref[row], outer_ref[row])
-
-    @pl.when(band < bands // 2)
-    def _():
-        skip_rows(
-            first_ref,
-            lambda row: jnp.where(odd_frame, outer(row), middle_ref[row]),
-            lambda row: jnp.where(odd_frame, middle_ref[row], outer(row)),
-            weight_ref, skip_ref, inside_ref, across_ref, lax.rem(band, 2) == 1,
-        )
+    def add(with_relayed):
+        skips = []
+        for row in range(partial_ref.shape[0]):
+            total = partial_ref[row] + dot(weight_ref[...], middle_ref[row])
+            if with_relayed:
+                total += dot(outer_weight[...], relayed_ref[row])
+            skips.append(total.astype(BF16))
+        share_skip(skips, skip_ref, inside_ref, across_ref, lax.rem(band, 2) == 1)
+
+    pl.when(jnp.logical_and(upper, is_relayed))(lambda: add(True))
+    pl.when(jnp.logical_and(upper, jnp.logical_not(is_relayed)))(lambda: add(False))
 
 
 def own_kernel(skip_ref, pair_ref, mid_ref, skip_weight, mixed_ref, middle_ref, field, pooled, *, half):
@@ -251,7 +263,7 @@
 
 
 def last_kernel(
-    mixed_ref, middle_ref, inside_ref, lower_ref, upper_ref, mid_ref, skip_weight, phase_weight,
+    mixed_ref, middle_ref, upper_ref, lower_ref, inside_ref, mid_ref, skip_weight, phase_weight,
     field_ref, out_ref, low_field, high_field, cross_field, rims, middle_field, *, bands
 ):
     rows, channels, wide = mixed_ref.shape
@@ -340,7 +352,9 @@
         out_shape=shapes,
         scratch_shapes=list(scratch),
         compiler_params=pltpu.CompilerParams(vmem_limit_bytes=limit * MIB),
-        cost_estimate=pl.CostEstimate(flops=flops, bytes_accessed=1 << 20, transcendentals=0),
+        cost_estimate=pl.CostEstimate(
+            flops=flops or 0, bytes_accessed=0 if flops is None else 1 << 20, transcendentals=0
+        ),
         name=name,
         input_output_aliases=aliases or {},
         **specs,
@@ -427,11 +441,14 @@
             first,
         )
     )
-    time_turned, mid_turned, skip_weight, phase_weight = call(
-        weights_kernel,
+    time_turned, part_turned, rest_turned, outer_turned, mid_turned, skip_weight, phase_weight = call(
+        functools.partial(weights_kernel, bands=bands),
         "weights",
         [
             ((channels, depth), BF16),
+            ((channels, 2 * channels), BF16),
+            ((channels, channels), BF16),
+            ((channels, channels), BF16),
             ((inner, 3 * depth), BF16),
             ((channels, 3 * depth), BF16),
             ((4, channels, 4 * inner), BF16),
@@ -463,15 +480,27 @@
         inputs=[whole] * 4,
     )(*in_vmem(first, lower_outer, lower_middle, time_turned))
     lower_across = lax.ppermute(lower_rows, "frames", of_half(across, False))
+    (partial,) = call(
+        functools.partial(skip_part_kernel, bands=bands),
+        "skip_part",
+        [((rows, channels, wide), F32)],
+        8,
+        flops=None,
+        inputs=[whole] * 3,
+    )(*in_vmem(first, upper_outer, part_turned))
     skip, inside_rows, upper_rows = call(
         functools.partial(skip_upper_kernel, bands=bands),
         "skip_upper",
         skip_shapes,
         8,
-        flops=2 * rows * wide * depth * channels,
+        flops=2 * rows * wide * channels * channels,
         inputs=[whole] * 7,
         aliases={5: 0, 6: 1},
-    )(*in_vmem(first, upper_middle, upper_outer, relayed, time_turned, skip, inside_rows))
+    )(
+        *in_vmem(
+            partial, upper_middle, relayed, rest_turned, outer_turned, skip, inside_rows
+        )
+    )
     upper_across = lax.ppermute(upper_rows, "frames", of_half(across, True))
     from_inside = lax.ppermute(inside_rows, "frames", inside)
 
@@ -502,7 +531,7 @@
         inputs=[whole] * 9,
     )(
         *in_vmem(
-            mixed, middle, from_inside, lower_across, upper_across, mid_turned, skip_weight, phase_weight, field
+            mixed, middle, upper_across, lower_across, from_inside, mid_turned, skip_weight, phase_weight, field
         ),
     )
     return jnp.swapaxes(out, 2, 3)

time: 50.4 us -> 50 us (level)
    pallas_call x1 -> x2, Pallas kernels: 6.91 us -> 6.93 us  [the longest x1 6.91 us: body(): call(functools.partial(weights_kernel, bands=bands), 'weights', [((channe...]
where the time goes in v10:
time: 50 us; the launch traced here: 49.8 us
  Pallas kernels  21 us (42%)
  starting transfers between devices  16.6 us (33%)
  waiting for transfers between devices  12 us (24%)
    pallas_call x1, Pallas kernels, body(): call(functools.partial(weights_kernel, bands=bands), 'weights', [((channe...  6.91 us
    ppermute x1, waiting for transfers between devices, body(): upper_across = lax.ppermute(upper_rows, 'frames', of_half(across, True))  6.57 us
    ppermute x1, starting transfers between devices, body(): lower_across = lax.ppermute(lower_rows, 'frames', of_half(across, False))  5.18 us
    pallas_call x1, Pallas kernels, body(): call(functools.partial(last_kernel, bands=bands), 'last', [(turned.shape,...  4.64 us
    ppermute x1, starting transfers between devices, body(): across_row = lax.ppermute(across_rim, 'frames', across)  3.4 us
    ppermute x1, waiting for transfers between devices, body(): across_row = lax.ppermute(across_rim, 'frames', across)  3.17 us
    pallas_call x1, Pallas kernels, body(): call(lambda *refs: own_kernel(*refs, half=width // 2), 'own_rows', [((row...  3.02 us
    pallas_call x1, Pallas kernels, body(): call(functools.partial(first_kernel, bands=bands), 'first', [((rows, chan...  2.45 us
  transfers between devices with their start and end apart: 10, of which 3 were waited for; matrix products, arithmetic and copies ran while one was open for 0% of the time, Pallas kernels for 24%

profile of v10, /device:TPU:18, one launch (start us, length us, event | category | flops | bytes accessed | tf_op | source)
XLA Modules:
  0.0 49.8 jit_solution(4108447276617180957)
XLA Ops:
  0.0 2.0 %fetch.1 = (bf16[2,320,128]{2,1,0:T(8,128)(2,1)S(1)}, bf16[2,320,128]{2,1,0:T(8,128)(2,1)S(1)}, bf16[2,4,320,128]{3,2,1,0:T(8,128)(2,1)S(1)}, bf16[2880,320]{1,0:T(8,128)(2,1)S(1)}) custom-call(bf16[2,4,320,128]{3,2,1,0:T(8,128)(2,1)} %bitcast.10, bf16[2880,320]{1,0:T(8,128)(2,1)} %bitcast.8), custom_call_target="tpu_custom_call" | custom-call | bytes 1048576 | tf_op jit(solution)/shard_map/fetch/pallas_call | solution.py:399
  2.0 0.1 collective-permute-start
  2.1 3.4 %collective-permute-start.1 = (bf16[2,320,128]{2,1,0:T(8,128)(2,1)S(1)}, bf16[2,320,128]{2,1,0:T(8,128)(2,1)S(1)}, u32[]{:S(2)}, u32[]{:S(2)}) collective-permute-start(bf16[2,320,128]{2,1,0:T(8,128)(2,1)S(1)} %get-tuple-element.33), channel_id=1, source_target_pairs={{3,4},{4,3},{7,8},{8,7},{11,12},{12,11},{15,0},{0,15},{19,20},{20,... | collective-permute-start | bytes 491528 | tf_op jit(solution)/shard_map/ppermute | solution.py:413
  5.5 0.9 %prepare.1 = (bf16[320,2880]{1,0:T(8,128)(2,1)S(1)}, bf16[3840,256]{1,0:T(8,128)(2,1)S(1)}) custom-call(bf16[2,4,320,128]{3,2,1,0:T(8,128)(2,1)S(1)} %get-tuple-element.34.latent_ref, bf16[2880,320]{1,0:T(8,128)(2,1)S(1)} %get-tuple-element.35.weight_ref), custom_call_target="tpu_custom_call" | custom-call | flops 167772160 | bytes 1048576 | tf_op jit(solution)/shard_map/prepare/pallas_call | solution.py:414
  6.5 0.0 collective-permute-done.inside_ref
  6.5 3.2 %collective-permute-done.1.across_ref = bf16[2,320,128]{2,1,0:T(8,128)(2,1)S(1)} collective-permute-done((bf16[2,320,128]{2,1,0:T(8,128)(2,1)S(1)}, bf16[2,320,128]{2,1,0:T(8,128)(2,1)S(1)}, u32[]{:S(2)}, u32[]{:S(2)}) %collective-permute-start.1) | collective-permute-done | bytes 163872 | tf_op jit(solution)/shard_map/ppermute | solution.py:413
  9.7 2.5 %first.1.first_ref = bf16[4,320,256]{2,1,0:T(8,128)(2,1)S(1)} custom-call(bf16[2,320,128]{2,1,0:T(8,128)(2,1)S(1)} %collective-permute-done.inside_ref, bf16[2,320,128]{2,1,0:T(8,128)(2,1)S(1)} %collective-permute-done.1.across_ref, bf16[320,2880]{1,0:T(8,128)(2,1)S(1)} %get-tuple-element.36.turned_ref, bf16[3840,256]{1,0:T(8,128)(2,1)S(1)} %get-tuple-element.37.field_ref), custom_call_target="tpu_custom_call" | custom-call | flops 1887436800 | bytes 1048576 | tf_op jit(solution)/shard_map/first/pallas_call | solution.py:422
  12.1 2.4 %collective-permute-start.4 = (bf16[4,320,256]{2,1,0:T(8,128)(2,1)S(1)}, bf16[4,320,256]{2,1,0:T(8,128)(2,1)S(1)}, u32[]{:S(2)}, u32[]{:S(2)}) collective-permute-start(bf16[4,320,256]{2,1,0:T(8,128)(2,1)S(1)} %first.1.first_ref), channel_id=1, source_target_pairs={{4,8},{8,4},{5,9},{9,5},{14,13},{2,1},{20,24},{24,20},{21,25},{25,... | collective-permute-start | bytes 1966088 | tf_op jit(solution)/shard_map/ppermute | solution.py:433
  14.5 1.9 %collective-permute-start.6 = (bf16[4,320,256]{2,1,0:T(8,128)(2,1)S(1)}, bf16[4,320,256]{2,1,0:T(8,128)(2,1)S(1)}, u32[]{:S(2)}, u32[]{:S(2)}) collective-permute-start(bf16[4,320,256]{2,1,0:T(8,128)(2,1)S(1)} %first.1.first_ref), channel_id=1, source_target_pairs={{0,4},{4,0},{1,5},{5,1},{8,12},{12,8},{9,13},{13,9},{16,20},{20,16... | collective-permute-start | bytes 1966088 | tf_op jit(solution)/shard_map/ppermute | solution.py:432
  16.4 0.7 %collective-permute-start.2 = (bf16[4,320,256]{2,1,0:T(8,128)(2,1)S(1)}, bf16[4,320,256]{2,1,0:T(8,128)(2,1)S(1)}, u32[]{:S(2)}, u32[]{:S(2)}) collective-permute-start(bf16[4,320,256]{2,1,0:T(8,128)(2,1)S(1)} %first.1.first_ref), channel_id=1, source_target_pairs={{6,10},{10,6},{7,11},{11,7},{15,3},{3,15},{22,26},{26,22},{23,27},... | collective-permute-start | bytes 1966088 | tf_op jit(solution)/shard_map/ppermute | solution.py:435
  17.1 0.7 %collective-permute-start.3 = (bf16[4,320,256]{2,1,0:T(8,128)(2,1)S(1)}, bf16[4,320,256]{2,1,0:T(8,128)(2,1)S(1)}, u32[]{:S(2)}, u32[]{:S(2)}) collective-permute-start(bf16[4,320,256]{2,1,0:T(8,128)(2,1)S(1)} %first.1.first_ref), channel_id=1, source_target_pairs={{2,6},{6,2},{3,7},{7,3},{18,22},{22,18},{19,23},{23,19}} | collective-permute-start | bytes 1966088 | tf_op jit(solution)/shard_map/ppermute | solution.py:434
  17.8 6.9 %weights.1 = (bf16[320,960]{1,0:T(8,128)(2,1)S(1)}, bf16[320,640]{1,0:T(8,128)(2,1)S(1)}, bf16[320,320]{1,0:T(8,128)(2,1)S(1)}, bf16[320,320]{1,0:T(8,128)(2,1)S...) custom-call(bf16[960,320]{1,0:T(8,128)(2,1)} %bitcast.9, ...), custom_call_target="tpu_custom_call" | custom-call | flops 2000000000 | bytes 1048576 | tf_op jit(solution)/shard_map/weights/pallas_call | solution.py:444
  24.8 2.3 %collective-permute-done.4.middle_ref = bf16[4,320,256]{2,1,0:T(8,128)(2,1)S(1)} collective-permute-done((bf16[4,320,256]{2,1,0:T(8,128)(2,1)S(1)}, bf16[4,320,256]{2,1,0:T(8,128)(2,1)S(1)}, u32[]{:S(2)}, u32[]{:S(2)}) %collective-permute-start.4) | collective-permute-done | bytes 655392 | tf_op jit(solution)/shard_map/ppermute | solution.py:433
  27.0 0.7 %collective-permute-start.5 = (bf16[4,320,256]{2,1,0:T(8,128)(2,1)S(1)}, bf16[4,320,256]{2,1,0:T(8,128)(2,1)S(1)}, u32[]{:S(2)}, u32[]{:S(2)}) collective-permute-start(bf16[4,320,256]{2,1,0:T(8,128)(2,1)S(1)} %collective-permute-done.4.middle_ref), channel_id=1, source_target_pairs={{13,2},{1,14},{29,18},{17,30}} | collective-permute-start | bytes 1966088 | tf_op jit(solution)/shard_map/ppermute | solution.py:468
  27.7 0.0 collective-permute-done.6.outer_ref
  27.7 0.9 %skip_lower.1 = (bf16[4,320,256]{2,1,0:T(8,128)(2,1)S(1)}, bf16[2,320,256]{2,1,0:T(8,128)(2,1)S(1)}, bf16[2,320,256]{2,1,0:T(8,128)(2,1)S(1)}) custom-call(bf16[4,320,256]{2,1,0:T(8,128)(2,1)S(1)} %first.1.first_ref, bf16[4,320,256]{2,1,0:T(8,128)(2,1)S(1)} %collective-permute-done.6.outer_ref, bf16[4,320,256]{2,1,0:T(8,128)(2,1)S(1)} %collective-permute-done.4.middle_ref, ...), custom_call_target="tpu_custom_call" | custom-call | flops 629145600 | bytes 1048576 | tf_op jit(solution)/shard_map/skip_lower/pallas_call | solution.py:474
  28.7 5.2 %collective-permute-start.8 = (bf16[2,320,256]{2,1,0:T(8,128)(2,1)S(1)}, bf16[2,320,256]{2,1,0:T(8,128)(2,1)S(1)}, u32[]{:S(2)}, u32[]{:S(2)}) collective-permute-start(bf16[2,320,256]{2,1,0:T(8,128)(2,1)S(1)} %get-tuple-element.57), channel_id=1, source_target_pairs={{4,3},{8,7},{12,11},{0,15},{20,19},{24,23},{28,27},{16,31}} | collective-permute-start | bytes 983048 | tf_op jit(solution)/shard_map/ppermute | solution.py:482
  33.9 0.0 collective-permute-done.2.outer_ref
  33.9 0.0 collective-permute-done.3.middle_ref
  33.9 0.0 collective-permute-done.5.relayed_ref
  34.0 1.5 %collective-permute-start.7 = (bf16[2,320,256]{2,1,0:T(8,128)(2,1)S(1)}, bf16[2,320,256]{2,1,0:T(8,128)(2,1)S(1)}, u32[]{:S(2)}, u32[]{:S(2)}) collective-permute-start(bf16[2,320,256]{2,1,0:T(8,128)(2,1)S(1)} %get-tuple-element.56), channel_id=1, source_target_pairs={{3,4},{7,8},{11,12},{15,0},{19,20},{23,24},{27,28},{31,16}} | collective-permute-start | bytes 983048 | tf_op jit(solution)/shard_map/ppermute | solution.py:504
  35.4 0.1 collective-permute-start.9
  35.5 3.0 %own_rows.1 = (f32[4,320,256]{2,1,0:T(8,128)S(1)}, f32[640,512]{1,0:T(8,128)S(1)}) custom-call(bf16[4,320,256]{2,1,0:T(8,128)(2,1)S(1)} %get-tuple-element.50.refs_0_, bf16[2,320,256]{2,1,0:T(8,128)(2,1)S(1)} %get-tuple-element.51.refs_1_, bf16[640,2880]{1,0:T(8,128)(2,1)S(1)} %get-tuple-element.52.refs_2_.mid_ref, ...), custom_call_target="tpu_custom_call" | custom-call | flops 2516582400 | bytes 1048576 | tf_op jit(solution)/shard_map/own_rows/pallas_call | solution.py:507
  38.6 0.0 collective-permute-done.8.lower_ref
  38.6 6.6 %collective-permute-done.7.upper_ref = bf16[2,320,256]{2,1,0:T(8,128)(2,1)S(1)} collective-permute-done((bf16[2,320,256]{2,1,0:T(8,128)(2,1)S(1)}, bf16[2,320,256]{2,1,0:T(8,128)(2,1)S(1)}, u32[]{:S(2)}, u32[]{:S(2)}) %collective-permute-start.7) | collective-permute-done | bytes 327712 | tf_op jit(solution)/shard_map/ppermute | solution.py:504
  45.1 0.0 collective-permute-done.9.inside_ref
  45.1 4.6 %last.1 = bf16[2,4,320,128]{3,2,1,0:T(8,128)(2,1)} custom-call(f32[4,320,256]{2,1,0:T(8,128)S(1)} %get-tuple-element.54.mixed_ref, f32[640,512]{1,0:T(8,128)S(1)} %get-tuple-element.55.middle_ref, bf16[2,320,256]{2,1,0:T(8,128)(2,1)S(1)} %collective-permute-done.7.upper_ref, bf16[2,320,256]{2,1,0:T(8,128)(2,1)S(1)} %collective-permute-done.8.lower_ref, ...), custom_call_target="tpu_custom_call" | custom-call | flops 2936012800 | bytes 1048576 | tf_op jit(solution)/shard_map/last/pallas_call | solution.py:517
  (2 shorter events, 0.0 us)
Async XLA Ops:
  2.0 4.4 %collective-permute-start = (bf16[2,320,128]{2,1,0:T(8,128)(2,1)S(1)}, bf16[2,320,128]{2,1,0:T(8,128)(2,1)S(1)}, u32[]{:S(2)}, u32[]{:S(2)}) collective-permute-start(bf16[2,320,128]{2,1,0:T(8,128)(2,1)S(1)} %get-tuple-element.32), channel_id=1, source_target_pairs={{0,1},{1,0},{2,3},{3,2},{4,5},{5,4},{6,7},{7,6},{8,9},{9,8},{10,11... | collective-permute-start | bytes 491528 | tf_op jit(solution)/shard_map/ppermute | solution.py:412
  2.1 7.5 %collective-permute-start.1 = (bf16[2,320,128]{2,1,0:T(8,128)(2,1)S(1)}, bf16[2,320,128]{2,1,0:T(8,128)(2,1)S(1)}, u32[]{:S(2)}, u32[]{:S(2)}) collective-permute-start(bf16[2,320,128]{2,1,0:T(8,128)(2,1)S(1)} %get-tuple-element.33), channel_id=1, source_target_pairs={{3,4},{4,3},{7,8},{8,7},{11,12},{12,11},{15,0},{0,15},{19,20},{20,... | collective-permute-start | bytes 491528 | tf_op jit(solution)/shard_map/ppermute | solution.py:413
  12.1 14.9 %collective-permute-start.4 = (bf16[4,320,256]{2,1,0:T(8,128)(2,1)S(1)}, bf16[4,320,256]{2,1,0:T(8,128)(2,1)S(1)}, u32[]{:S(2)}, u32[]{:S(2)}) collective-permute-start(bf16[4,320,256]{2,1,0:T(8,128)(2,1)S(1)} %first.1.first_ref), channel_id=1, source_target_pairs={{4,8},{8,4},{5,9},{9,5},{14,13},{2,1},{20,24},{24,20},{21,25},{25,... | collective-permute-start | bytes 1966088 | tf_op jit(solution)/shard_map/ppermute | solution.py:433
  14.5 13.2 %collective-permute-start.6 = (bf16[4,320,256]{2,1,0:T(8,128)(2,1)S(1)}, bf16[4,320,256]{2,1,0:T(8,128)(2,1)S(1)}, u32[]{:S(2)}, u32[]{:S(2)}) collective-permute-start(bf16[4,320,256]{2,1,0:T(8,128)(2,1)S(1)} %first.1.first_ref), channel_id=1, source_target_pairs={{0,4},{4,0},{1,5},{5,1},{8,12},{12,8},{9,13},{13,9},{16,20},{20,16... | collective-permute-start | bytes 1966088 | tf_op jit(solution)/shard_map/ppermute | solution.py:432
  16.4 17.5 %collective-permute-start.2 = (bf16[4,320,256]{2,1,0:T(8,128)(2,1)S(1)}, bf16[4,320,256]{2,1,0:T(8,128)(2,1)S(1)}, u32[]{:S(2)}, u32[]{:S(2)}) collective-permute-start(bf16[4,320,256]{2,1,0:T(8,128)(2,1)S(1)} %first.1.first_ref), channel_id=1, source_target_pairs={{6,10},{10,6},{7,11},{11,7},{15,3},{3,15},{22,26},{26,22},{23,27},... | collective-permute-start | bytes 1966088 | tf_op jit(solution)/shard_map/ppermute | solution.py:435
  17.1 16.8 %collective-permute-start.3 = (bf16[4,320,256]{2,1,0:T(8,128)(2,1)S(1)}, bf16[4,320,256]{2,1,0:T(8,128)(2,1)S(1)}, u32[]{:S(2)}, u32[]{:S(2)}) collective-permute-start(bf16[4,320,256]{2,1,0:T(8,128)(2,1)S(1)} %first.1.first_ref), channel_id=1, source_target_pairs={{2,6},{6,2},{3,7},{7,3},{18,22},{22,18},{19,23},{23,19}} | collective-permute-start | bytes 1966088 | tf_op jit(solution)/shard_map/ppermute | solution.py:434
  27.0 6.9 %collective-permute-start.5 = (bf16[4,320,256]{2,1,0:T(8,128)(2,1)S(1)}, bf16[4,320,256]{2,1,0:T(8,128)(2,1)S(1)}, u32[]{:S(2)}, u32[]{:S(2)}) collective-permute-start(bf16[4,320,256]{2,1,0:T(8,128)(2,1)S(1)} %collective-permute-done.4.middle_ref), channel_id=1, source_target_pairs={{13,2},{1,14},{29,18},{17,30}} | collective-permute-start | bytes 1966088 | tf_op jit(solution)/shard_map/ppermute | solution.py:468
  28.7 9.9 %collective-permute-start.8 = (bf16[2,320,256]{2,1,0:T(8,128)(2,1)S(1)}, bf16[2,320,256]{2,1,0:T(8,128)(2,1)S(1)}, u32[]{:S(2)}, u32[]{:S(2)}) collective-permute-start(bf16[2,320,256]{2,1,0:T(8,128)(2,1)S(1)} %get-tuple-element.57), channel_id=1, source_target_pairs={{4,3},{8,7},{12,11},{0,15},{20,19},{24,23},{28,27},{16,31}} | collective-permute-start | bytes 983048 | tf_op jit(solution)/shard_map/ppermute | solution.py:482
  34.0 11.2 %collective-permute-start.7 = (bf16[2,320,256]{2,1,0:T(8,128)(2,1)S(1)}, bf16[2,320,256]{2,1,0:T(8,128)(2,1)S(1)}, u32[]{:S(2)}, u32[]{:S(2)}) collective-permute-start(bf16[2,320,256]{2,1,0:T(8,128)(2,1)S(1)} %get-tuple-element.56), channel_id=1, source_target_pairs={{3,4},{7,8},{11,12},{15,0},{19,20},{23,24},{27,28},{31,16}} | collective-permute-start | bytes 983048 | tf_op jit(solution)/shard_map/ppermute | solution.py:504
  35.4 9.7 %collective-permute-start.9 = (bf16[2,320,256]{2,1,0:T(8,128)(2,1)S(1)}, bf16[2,320,256]{2,1,0:T(8,128)(2,1)S(1)}, u32[]{:S(2)}, u32[]{:S(2)}) collective-permute-start(bf16[2,320,256]{2,1,0:T(8,128)(2,1)S(1)} %get-tuple-element.51.refs_1_), channel_id=1, source_target_pairs={{0,1},{1,0},{2,3},{3,2},{4,5},{5,4},{6,7},{7,6},{8,9},{9,8},{10,11... | collective-permute-start | bytes 983048 | tf_op jit(solution)/shard_map/ppermute | solution.py:505

commit v11 on v10

--- a/solution.py
+++ b/solution.py
@@ -72,14 +72,14 @@
 
 
 def fetch_kernel(
-    latent_hbm, weight_hbm, inside_ref, across_ref, latent_ref, weight_ref, sems, *, bands
+    latent_hbm, weight_hbm, inside_ref, across_ref, weight_ref, field_ref, latent, sems, *, bands
 ):
-    last = latent_hbm.shape[1] - 1
+    clips, rows, channels, width = latent.shape
     odd = lax.rem(place(bands)[0], 2)
     pieces = [
-        (latent_hbm.at[:, last * odd], across_ref),
-        (latent_hbm.at[:, last * (1 - odd)], inside_ref),
-        (latent_hbm, latent_ref),
+        (latent_hbm, latent),
+        (latent_hbm.at[:, (rows - 1) * odd], across_ref),
+        (latent_hbm.at[:, (rows - 1) * (1 - odd)], inside_ref),
         (weight_hbm, weight_ref),
     ]
     gets = [
@@ -88,17 +88,17 @@
     ]
     for get in gets:
         get.start()
-    for get in gets:
-        get.wait()
-
-
-def prepare_kernel(latent_ref, weight_ref, turned_ref, field_ref):
-    clips, rows, channels, width = latent_ref.shape
     pick = sort_pick(width, clips)
+    gets[0].wait()
     for row in range(rows):
-        value = dot(jnp.concatenate([latent_ref[clip, row] for clip in range(clips)], axis=1), pick)
+        value = dot(jnp.concatenate([latent[clip, row] for clip in range(clips)], axis=1), pick)
         lanes = value.shape[1] // 2
         store_taps(field_ref, row * 3 * channels, value[:, :lanes], value[:, lanes:], width // 2)
+    for get in gets[1:]:
+        get.wait()
+
+
+def prepare_kernel(weight_ref, turned_ref):
     turned_ref[...] = weight_ref[...].T
 
 
@@ -396,29 +396,29 @@
     whole = pl.BlockSpec(memory_space=pltpu.VMEM)
     turned = jnp.swapaxes(latents, 2, 3)
 
-    inside_rim, across_rim, latent, in_rows = call(
+    inside_rim, across_rim, in_rows, field = call(
         functools.partial(fetch_kernel, bands=bands),
         "fetch",
         [
             ((clips, channels, width), BF16),
             ((clips, channels, width), BF16),
-            (turned.shape, BF16),
             ((3 * depth, channels), BF16),
+            ((rows * depth, wide), BF16),
         ],
-        1,
-        [pltpu.SemaphoreType.DMA((4,))],
+        8,
+        [pltpu.VMEM(turned.shape, BF16), pltpu.SemaphoreType.DMA((4,))],
         inputs=[anywhere, anywhere],
     )(in_hbm(turned), in_hbm(in_weight.reshape(3 * depth, channels)))
     inside_row = lax.ppermute(inside_rim, "frames", inside)
     across_row = lax.ppermute(across_rim, "frames", across)
-    in_turned, field = call(
+    (in_turned,) = call(
         prepare_kernel,
         "prepare",
-        [((channels, 3 * depth), BF16), ((rows * depth, wide), BF16)],
+        [((channels, 3 * depth), BF16)],
         8,
         flops=2 * rows * wide * channels * wide,
-        inputs=[whole] * 2,
-    )(*in_vmem(latent, in_rows))
+        inputs=[whole],
+    )(*in_vmem(in_rows))
     (first,) = call(
         functools.partial(first_kernel, bands=bands),
         "first",

time: 50 us -> 49.8 us (level)
  the two profiles are of different devices: /device:TPU:18 before, /device:TPU:0 now
where the time goes in v11:
time: 49.8 us; the launch traced here: 49.6 us
  Pallas kernels  20.6 us (41%)
  starting transfers between devices  20.2 us (41%)
  waiting for transfers between devices  8.58 us (17%)
    ppermute x1, starting transfers between devices, body(): across_row = lax.ppermute(across_rim, 'frames', across)  7.56 us
    pallas_call x1, Pallas kernels, body(): call(functools.partial(weights_kernel, bands=bands), 'weights', [((channe...  6.91 us
    pallas_call x1, Pallas kernels, body(): call(functools.partial(last_kernel, bands=bands), 'last', [(turned.shape,...  4.64 us
    ppermute x1, waiting for transfers between devices, body(): upper_across = lax.ppermute(upper_rows, 'frames', of_half(across, True))  4.34 us
    ppermute x1, starting transfers between devices, body(): lower_outer = lax.ppermute(first, 'frames', of_half(outer_frames, False))  4.15 us
    pallas_call x1, Pallas kernels, body(): call(lambda *refs: own_kernel(*refs, half=width // 2), 'own_rows', [((row...  3.03 us
    pallas_call x1, Pallas kernels, body(): call(functools.partial(first_kernel, bands=bands), 'first', [((rows, chan...  2.45 us
    ppermute x1, waiting for transfers between devices, body(): across_row = lax.ppermute(across_rim, 'frames', across)  2.44 us
  transfers between devices with their start and end apart: 10, of which 3 were waited for; matrix products, arithmetic and copies ran while one was open for 0% of the time, Pallas kernels for 23%

profile of v11, /device:TPU:0, one launch (start us, length us, event | category | flops | bytes accessed | tf_op | source)
XLA Modules:
  0.0 49.6 jit_solution(10113577491325234996)
XLA Ops:
  0.0 2.0 %fetch.1 = (bf16[2,320,128]{2,1,0:T(8,128)(2,1)S(1)}, bf16[2,320,128]{2,1,0:T(8,128)(2,1)S(1)}, bf16[2880,320]{1,0:T(8,128)(2,1)S(1)}, bf16[3840,256]{1,0:T(8,128)(2,1)S(1)}) custom-call(bf16[2,4,320,128]{3,2,1,0:T(8,128)(2,1)} %bitcast.10, bf16[2880,320]{1,0:T(8,128)(2,1)} %bitcast.8), custom_call_target="tpu_custom_call" | custom-call | bytes 1048576 | tf_op jit(solution)/shard_map/fetch/pallas_call | solution.py:399
  2.0 0.5 %collective-permute-start = (bf16[2,320,128]{2,1,0:T(8,128)(2,1)S(1)}, bf16[2,320,128]{2,1,0:T(8,128)(2,1)S(1)}, u32[]{:S(2)}, u32[]{:S(2)}) collective-permute-start(bf16[2,320,128]{2,1,0:T(8,128)(2,1)S(1)} %get-tuple-element.30), channel_id=1, source_target_pairs={{0,1},{1,0},{2,3},{3,2},{4,5},{5,4},{6,7},{7,6},{8,9},{9,8},{10,11... | collective-permute-start | bytes 491528 | tf_op jit(solution)/shard_map/ppermute | solution.py:412
  2.5 7.6 %collective-permute-start.1 = (bf16[2,320,128]{2,1,0:T(8,128)(2,1)S(1)}, bf16[2,320,128]{2,1,0:T(8,128)(2,1)S(1)}, u32[]{:S(2)}, u32[]{:S(2)}) collective-permute-start(bf16[2,320,128]{2,1,0:T(8,128)(2,1)S(1)} %get-tuple-element.31), channel_id=1, source_target_pairs={{3,4},{4,3},{7,8},{8,7},{11,12},{12,11},{15,0},{0,15},{19,20},{20,... | collective-permute-start | bytes 491528 | tf_op jit(solution)/shard_map/ppermute | solution.py:413
  10.1 0.6 %prepare.1.turned_ref = bf16[320,2880]{1,0:T(8,128)(2,1)S(1)} custom-call(bf16[2880,320]{1,0:T(8,128)(2,1)S(1)} %get-tuple-element.32.weight_ref), custom_call_target="tpu_custom_call" | custom-call | flops 167772160 | bytes 1048576 | tf_op jit(solution)/shard_map/prepare/pallas_call | solution.py:414
  10.7 0.0 collective-permute-done.inside_ref
  10.7 2.4 %collective-permute-done.1.across_ref = bf16[2,320,128]{2,1,0:T(8,128)(2,1)S(1)} collective-permute-done((bf16[2,320,128]{2,1,0:T(8,128)(2,1)S(1)}, bf16[2,320,128]{2,1,0:T(8,128)(2,1)S(1)}, u32[]{:S(2)}, u32[]{:S(2)}) %collective-permute-start.1) | collective-permute-done | bytes 163872 | tf_op jit(solution)/shard_map/ppermute | solution.py:413
  13.2 2.5 %first.1.first_ref = bf16[4,320,256]{2,1,0:T(8,128)(2,1)S(1)} custom-call(bf16[2,320,128]{2,1,0:T(8,128)(2,1)S(1)} %collective-permute-done.inside_ref, bf16[2,320,128]{2,1,0:T(8,128)(2,1)S(1)} %collective-permute-done.1.across_ref, bf16[320,2880]{1,0:T(8,128)(2,1)S(1)} %prepare.1.turned_ref, bf16[3840,256]{1,0:T(8,128)(2,1)S(1)} %get-tuple-element.33.field_ref), custom_call_target="tpu_custom_call" | custom-call | flops 1887436800 | bytes 1048576 | tf_op jit(solution)/shard_map/first/pallas_call | solution.py:422
  15.6 0.7 %collective-permute-start.4 = (bf16[4,320,256]{2,1,0:T(8,128)(2,1)S(1)}, bf16[4,320,256]{2,1,0:T(8,128)(2,1)S(1)}, u32[]{:S(2)}, u32[]{:S(2)}) collective-permute-start(bf16[4,320,256]{2,1,0:T(8,128)(2,1)S(1)} %first.1.first_ref), channel_id=1, source_target_pairs={{4,8},{8,4},{5,9},{9,5},{14,13},{2,1},{20,24},{24,20},{21,25},{25,... | collective-permute-start | bytes 1966088 | tf_op jit(solution)/shard_map/ppermute | solution.py:433
  16.3 4.1 %collective-permute-start.6 = (bf16[4,320,256]{2,1,0:T(8,128)(2,1)S(1)}, bf16[4,320,256]{2,1,0:T(8,128)(2,1)S(1)}, u32[]{:S(2)}, u32[]{:S(2)}) collective-permute-start(bf16[4,320,256]{2,1,0:T(8,128)(2,1)S(1)} %first.1.first_ref), channel_id=1, source_target_pairs={{0,4},{4,0},{1,5},{5,1},{8,12},{12,8},{9,13},{13,9},{16,20},{20,16... | collective-permute-start | bytes 1966088 | tf_op jit(solution)/shard_map/ppermute | solution.py:432
  20.5 0.7 %collective-permute-start.2 = (bf16[4,320,256]{2,1,0:T(8,128)(2,1)S(1)}, bf16[4,320,256]{2,1,0:T(8,128)(2,1)S(1)}, u32[]{:S(2)}, u32[]{:S(2)}) collective-permute-start(bf16[4,320,256]{2,1,0:T(8,128)(2,1)S(1)} %first.1.first_ref), channel_id=1, source_target_pairs={{6,10},{10,6},{7,11},{11,7},{15,3},{3,15},{22,26},{26,22},{23,27},... | collective-permute-start | bytes 1966088 | tf_op jit(solution)/shard_map/ppermute | solution.py:435
  21.2 0.7 %collective-permute-start.3 = (bf16[4,320,256]{2,1,0:T(8,128)(2,1)S(1)}, bf16[4,320,256]{2,1,0:T(8,128)(2,1)S(1)}, u32[]{:S(2)}, u32[]{:S(2)}) collective-permute-start(bf16[4,320,256]{2,1,0:T(8,128)(2,1)S(1)} %first.1.first_ref), channel_id=1, source_target_pairs={{2,6},{6,2},{3,7},{7,3},{18,22},{22,18},{19,23},{23,19}} | collective-permute-start | bytes 1966088 | tf_op jit(solution)/shard_map/ppermute | solution.py:434
  21.9 6.9 %weights.1 = (bf16[320,960]{1,0:T(8,128)(2,1)S(1)}, bf16[320,640]{1,0:T(8,128)(2,1)S(1)}, bf16[320,320]{1,0:T(8,128)(2,1)S(1)}, bf16[320,320]{1,0:T(8,128)(2,1)S...) custom-call(bf16[960,320]{1,0:T(8,128)(2,1)} %bitcast.9, ...), custom_call_target="tpu_custom_call" | custom-call | flops 2000000000 | bytes 1048576 | tf_op jit(solution)/shard_map/weights/pallas_call | solution.py:444
  28.8 0.0 collective-permute-done.4.middle_ref
  28.8 0.7 %collective-permute-start.5 = (bf16[4,320,256]{2,1,0:T(8,128)(2,1)S(1)}, bf16[4,320,256]{2,1,0:T(8,128)(2,1)S(1)}, u32[]{:S(2)}, u32[]{:S(2)}) collective-permute-start(bf16[4,320,256]{2,1,0:T(8,128)(2,1)S(1)} %collective-permute-done.4.middle_ref), channel_id=1, source_target_pairs={{13,2},{1,14},{29,18},{17,30}} | collective-permute-start | bytes 1966088 | tf_op jit(solution)/shard_map/ppermute | solution.py:468
  29.5 1.8 %collective-permute-done.6.outer_ref = bf16[4,320,256]{2,1,0:T(8,128)(2,1)S(1)} collective-permute-done((bf16[4,320,256]{2,1,0:T(8,128)(2,1)S(1)}, bf16[4,320,256]{2,1,0:T(8,128)(2,1)S(1)}, u32[]{:S(2)}, u32[]{:S(2)}) %collective-permute-start.6) | collective-permute-done | bytes 655392 | tf_op jit(solution)/shard_map/ppermute | solution.py:432
  31.3 0.9 %skip_lower.1 = (bf16[4,320,256]{2,1,0:T(8,128)(2,1)S(1)}, bf16[2,320,256]{2,1,0:T(8,128)(2,1)S(1)}, bf16[2,320,256]{2,1,0:T(8,128)(2,1)S(1)}) custom-call(bf16[4,320,256]{2,1,0:T(8,128)(2,1)S(1)} %first.1.first_ref, bf16[4,320,256]{2,1,0:T(8,128)(2,1)S(1)} %collective-permute-done.6.outer_ref, bf16[4,320,256]{2,1,0:T(8,128)(2,1)S(1)} %collective-permute-done.4.middle_ref, ...), custom_call_target="tpu_custom_call" | custom-call | flops 629145600 | bytes 1048576 | tf_op jit(solution)/shard_map/skip_lower/pallas_call | solution.py:474
  32.3 1.5 %collective-permute-start.8 = (bf16[2,320,256]{2,1,0:T(8,128)(2,1)S(1)}, bf16[2,320,256]{2,1,0:T(8,128)(2,1)S(1)}, u32[]{:S(2)}, u32[]{:S(2)}) collective-permute-start(bf16[2,320,256]{2,1,0:T(8,128)(2,1)S(1)} %get-tuple-element.53), channel_id=1, source_target_pairs={{4,3},{8,7},{12,11},{0,15},{20,19},{24,23},{28,27},{16,31}} | collective-permute-start | bytes 983048 | tf_op jit(solution)/shard_map/ppermute | solution.py:482
  33.7 0.0 collective-permute-done.2.outer_ref
  33.8 0.0 collective-permute-done.3.middle_ref
  33.8 0.0 collective-permute-done.5.relayed_ref
  33.8 1.5 %collective-permute-start.7 = (bf16[2,320,256]{2,1,0:T(8,128)(2,1)S(1)}, bf16[2,320,256]{2,1,0:T(8,128)(2,1)S(1)}, u32[]{:S(2)}, u32[]{:S(2)}) collective-permute-start(bf16[2,320,256]{2,1,0:T(8,128)(2,1)S(1)} %get-tuple-element.52), channel_id=1, source_target_pairs={{3,4},{7,8},{11,12},{15,0},{19,20},{23,24},{27,28},{31,16}} | collective-permute-start | bytes 983048 | tf_op jit(solution)/shard_map/ppermute | solution.py:504
  35.3 2.2 %collective-permute-start.9 = (bf16[2,320,256]{2,1,0:T(8,128)(2,1)S(1)}, bf16[2,320,256]{2,1,0:T(8,128)(2,1)S(1)}, u32[]{:S(2)}, u32[]{:S(2)}) collective-permute-start(bf16[2,320,256]{2,1,0:T(8,128)(2,1)S(1)} %get-tuple-element.47.refs_1_), channel_id=1, source_target_pairs={{0,1},{1,0},{2,3},{3,2},{4,5},{5,4},{6,7},{7,6},{8,9},{9,8},{10,11... | collective-permute-start | bytes 983048 | tf_op jit(solution)/shard_map/ppermute | solution.py:505
  37.5 3.0 %own_rows.1 = (f32[4,320,256]{2,1,0:T(8,128)S(1)}, f32[640,512]{1,0:T(8,128)S(1)}) custom-call(bf16[4,320,256]{2,1,0:T(8,128)(2,1)S(1)} %get-tuple-element.46.refs_0_, bf16[2,320,256]{2,1,0:T(8,128)(2,1)S(1)} %get-tuple-element.47.refs_1_, bf16[640,2880]{1,0:T(8,128)(2,1)S(1)} %get-tuple-element.48.refs_2_.mid_ref, ...), custom_call_target="tpu_custom_call" | custom-call | flops 2516582400 | bytes 1048576 | tf_op jit(solution)/shard_map/own_rows/pallas_call | solution.py:507
  40.6 0.0 collective-permute-done.8.lower_ref
  40.6 4.3 %collective-permute-done.7.upper_ref = bf16[2,320,256]{2,1,0:T(8,128)(2,1)S(1)} collective-permute-done((bf16[2,320,256]{2,1,0:T(8,128)(2,1)S(1)}, bf16[2,320,256]{2,1,0:T(8,128)(2,1)S(1)}, u32[]{:S(2)}, u32[]{:S(2)}) %collective-permute-start.7) | collective-permute-done | bytes 327712 | tf_op jit(solution)/shard_map/ppermute | solution.py:504
  44.9 0.0 collective-permute-done.9.inside_ref
  44.9 4.6 %last.1 = bf16[2,4,320,128]{3,2,1,0:T(8,128)(2,1)} custom-call(f32[4,320,256]{2,1,0:T(8,128)S(1)} %get-tuple-element.50.mixed_ref, f32[640,512]{1,0:T(8,128)S(1)} %get-tuple-element.51.middle_ref, bf16[2,320,256]{2,1,0:T(8,128)(2,1)S(1)} %collective-permute-done.7.upper_ref, bf16[2,320,256]{2,1,0:T(8,128)(2,1)S(1)} %collective-permute-done.8.lower_ref, ...), custom_call_target="tpu_custom_call" | custom-call | flops 2936012800 | bytes 1048576 | tf_op jit(solution)/shard_map/last/pallas_call | solution.py:517
  (2 shorter events, 0.0 us)
Async XLA Ops:
  2.0 8.7 %collective-permute-start = (bf16[2,320,128]{2,1,0:T(8,128)(2,1)S(1)}, bf16[2,320,128]{2,1,0:T(8,128)(2,1)S(1)}, u32[]{:S(2)}, u32[]{:S(2)}) collective-permute-start(bf16[2,320,128]{2,1,0:T(8,128)(2,1)S(1)} %get-tuple-element.30), channel_id=1, source_target_pairs={{0,1},{1,0},{2,3},{3,2},{4,5},{5,4},{6,7},{7,6},{8,9},{9,8},{10,11... | collective-permute-start | bytes 491528 | tf_op jit(solution)/shard_map/ppermute | solution.py:412
  2.5 10.7 %collective-permute-start.1 = (bf16[2,320,128]{2,1,0:T(8,128)(2,1)S(1)}, bf16[2,320,128]{2,1,0:T(8,128)(2,1)S(1)}, u32[]{:S(2)}, u32[]{:S(2)}) collective-permute-start(bf16[2,320,128]{2,1,0:T(8,128)(2,1)S(1)} %get-tuple-element.31), channel_id=1, source_target_pairs={{3,4},{4,3},{7,8},{8,7},{11,12},{12,11},{15,0},{0,15},{19,20},{20,... | collective-permute-start | bytes 491528 | tf_op jit(solution)/shard_map/ppermute | solution.py:413
  15.6 13.2 %collective-permute-start.4 = (bf16[4,320,256]{2,1,0:T(8,128)(2,1)S(1)}, bf16[4,320,256]{2,1,0:T(8,128)(2,1)S(1)}, u32[]{:S(2)}, u32[]{:S(2)}) collective-permute-start(bf16[4,320,256]{2,1,0:T(8,128)(2,1)S(1)} %first.1.first_ref), channel_id=1, source_target_pairs={{4,8},{8,4},{5,9},{9,5},{14,13},{2,1},{20,24},{24,20},{21,25},{25,... | collective-permute-start | bytes 1966088 | tf_op jit(solution)/shard_map/ppermute | solution.py:433
  16.3 15.0 %collective-permute-start.6 = (bf16[4,320,256]{2,1,0:T(8,128)(2,1)S(1)}, bf16[4,320,256]{2,1,0:T(8,128)(2,1)S(1)}, u32[]{:S(2)}, u32[]{:S(2)}) collective-permute-start(bf16[4,320,256]{2,1,0:T(8,128)(2,1)S(1)} %first.1.first_ref), channel_id=1, source_target_pairs={{0,4},{4,0},{1,5},{5,1},{8,12},{12,8},{9,13},{13,9},{16,20},{20,16... | collective-permute-start | bytes 1966088 | tf_op jit(solution)/shard_map/ppermute | solution.py:432
  20.5 13.2 %collective-permute-start.2 = (bf16[4,320,256]{2,1,0:T(8,128)(2,1)S(1)}, bf16[4,320,256]{2,1,0:T(8,128)(2,1)S(1)}, u32[]{:S(2)}, u32[]{:S(2)}) collective-permute-start(bf16[4,320,256]{2,1,0:T(8,128)(2,1)S(1)} %first.1.first_ref), channel_id=1, source_target_pairs={{6,10},{10,6},{7,11},{11,7},{15,3},{3,15},{22,26},{26,22},{23,27},... | collective-permute-start | bytes 1966088 | tf_op jit(solution)/shard_map/ppermute | solution.py:435
  21.2 12.6 %collective-permute-start.3 = (bf16[4,320,256]{2,1,0:T(8,128)(2,1)S(1)}, bf16[4,320,256]{2,1,0:T(8,128)(2,1)S(1)}, u32[]{:S(2)}, u32[]{:S(2)}) collective-permute-start(bf16[4,320,256]{2,1,0:T(8,128)(2,1)S(1)} %first.1.first_ref), channel_id=1, source_target_pairs={{2,6},{6,2},{3,7},{7,3},{18,22},{22,18},{19,23},{23,19}} | collective-permute-start | bytes 1966088 | tf_op jit(solution)/shard_map/ppermute | solution.py:434
  28.8 4.9 %collective-permute-start.5 = (bf16[4,320,256]{2,1,0:T(8,128)(2,1)S(1)}, bf16[4,320,256]{2,1,0:T(8,128)(2,1)S(1)}, u32[]{:S(2)}, u32[]{:S(2)}) collective-permute-start(bf16[4,320,256]{2,1,0:T(8,128)(2,1)S(1)} %collective-permute-done.4.middle_ref), channel_id=1, source_target_pairs={{13,2},{1,14},{29,18},{17,30}} | collective-permute-start | bytes 1966088 | tf_op jit(solution)/shard_map/ppermute | solution.py:468
  32.3 8.3 %collective-permute-start.8 = (bf16[2,320,256]{2,1,0:T(8,128)(2,1)S(1)}, bf16[2,320,256]{2,1,0:T(8,128)(2,1)S(1)}, u32[]{:S(2)}, u32[]{:S(2)}) collective-permute-start(bf16[2,320,256]{2,1,0:T(8,128)(2,1)S(1)} %get-tuple-element.53), channel_id=1, source_target_pairs={{4,3},{8,7},{12,11},{0,15},{20,19},{24,23},{28,27},{16,31}} | collective-permute-start | bytes 983048 | tf_op jit(solution)/shard_map/ppermute | solution.py:482
  33.8 11.1 %collective-permute-start.7 = (bf16[2,320,256]{2,1,0:T(8,128)(2,1)S(1)}, bf16[2,320,256]{2,1,0:T(8,128)(2,1)S(1)}, u32[]{:S(2)}, u32[]{:S(2)}) collective-permute-start(bf16[2,320,256]{2,1,0:T(8,128)(2,1)S(1)} %get-tuple-element.52), channel_id=1, source_target_pairs={{3,4},{7,8},{11,12},{15,0},{19,20},{23,24},{27,28},{31,16}} | collective-permute-start | bytes 983048 | tf_op jit(solution)/shard_map/ppermute | solution.py:504
  35.3 9.6 %collective-permute-start.9 = (bf16[2,320,256]{2,1,0:T(8,128)(2,1)S(1)}, bf16[2,320,256]{2,1,0:T(8,128)(2,1)S(1)}, u32[]{:S(2)}, u32[]{:S(2)}) collective-permute-start(bf16[2,320,256]{2,1,0:T(8,128)(2,1)S(1)} %get-tuple-element.47.refs_1_), channel_id=1, source_target_pairs={{0,1},{1,0},{2,3},{3,2},{4,5},{5,4},{6,7},{7,6},{8,9},{9,8},{10,11... | collective-permute-start | bytes 983048 | tf_op jit(solution)/shard_map/ppermute | solution.py:505
